TPU v7x, 32 devices: a whole 2x2x4 slice. The times are simulated.
32 devices in a mesh: path: 8 (over z, x), mp: 4 (over y, core).
Axes of the slice: x: 2, y: 2, z: 4, core: 2. Of those that a mesh axis runs over, the one named last changes fastest.
Arguments:
- tokens: bfloat16 [3072, 2048], P('path', 'mp'), may hold values from -6 to 6
- cotangent: bfloat16 [3072, 2048], P('path', 'mp'), may hold values from -6 to 6
- path_weights: bfloat16 [8, 3, 4096, 2048], P('path', None, 'mp'), may hold values from -6 to 6
- outer_weights: float32 [8, 3, 2, 4, 128, 2048], P('path', None, None, 'mp'), may hold values from -6 to 6
- momentum: bfloat16 [8, 3, 2, 4, 128, 2048], P('path', None, None, 'mp'), may hold values from -6 to 6
- assignment: int32 [3, 8], replicated, may hold values from 0 to 1, as said below
- owners: int32 [3, 2, 8], replicated, may hold values from 0 to 7, each once within a row
Outputs:
- outputs: bfloat16 [3072, 2048], P('path', 'mp')
- refreshed: bfloat16 [8, 3, 2, 4, 128, 2048], P('path', None, None, 'mp')
Inputs may be any that keep to these rules, and one draw needn't show every extreme that they name: `assignment`: every one of the 2 modules of a level is used by at least one path; how many paths share a module varies from module to module. For each level and module, the owners of its 8 pieces are the 8 path indices, each once.
All inputs are finite; a program needn't handle non-finite values.
Results may differ from a plain program's by a relative error of at most 0.0068.
Values may be sent and summed in bfloat16 or wider, within the bound.
No kernel may reach another device: no remote copies, remote signals or barrier semaphores. Data moves between devices by JAX's collectives and lax.ppermute only.
A program may use at most 128 MiB of HBM per device.

v0:
```python
import jax
import jax.numpy as jnp
from jax import lax
from jax.sharding import PartitionSpec as P

D = 2048
FF = 4096


mu_outer = 0.9
eta_outer = 0.7
lr_inner = 2.0


def contract(left, right, left_dim, right_dim):
    return lax.dot_general(
        left, right, (((left_dim,), (right_dim,)), ((), ())), preferred_element_type=jnp.float32
    )


def shards(tokens, cotangent, path_weights, outer_weights, momentum, assignment, owners):
    inputs, upstream = (
        lax.all_gather(tokens, "mp", axis=1, tiled=True),
        lax.all_gather(cotangent, "mp", axis=1, tiled=True),
    )
    weights = path_weights[0]
    levels = weights.shape[0]
    width = weights.shape[2]
    paths = lax.axis_size("path")
    modules = outer_weights.shape[2]
    block = outer_weights.shape[4]
    scale_d = D ** (-0.5)
    scale_f = FF ** (-0.5)
    level_ids = jnp.arange(levels, dtype=jnp.int32)
    mine = lax.dynamic_index_in_dim(assignment, lax.axis_index("path"), 1, keepdims=False)
    owner_rows = owners[level_ids, mine]
    path_ids = jnp.arange(paths, dtype=jnp.int32)
    inverse = jnp.sum(
        path_ids[None, :, None]
        * (owner_rows[:, :, None] == path_ids[None, None, :]).astype(jnp.int32),
        axis=1,
    )
    table = (assignment[:, None, :] == jnp.arange(modules, dtype=jnp.int32)[None, :, None]).astype(
        jnp.float32
    )
    shares = jnp.sum(table, axis=2)
    stored = outer_weights[0, :, :, 0]
    velocity_old = momentum[0, :, :, 0].astype(jnp.float32)
    gate = contract(inputs, weights[0], 1, 1) * scale_d
    upper = contract(inputs, weights[1], 1, 1) * scale_d
    sig = jax.nn.sigmoid(gate)
    act = gate * sig
    hidden = (act * upper).astype(jnp.bfloat16)
    grad_hidden = contract(upstream, weights[2], 1, 1) * scale_f
    pre_gate = (grad_hidden * upper * sig * (1.0 + gate * (1.0 - sig))).astype(jnp.bfloat16)
    pre_up = (grad_hidden * act).astype(jnp.bfloat16)
    fresh_parts = [None, None, None]
    new_parts = [None, None, None]
    for level in (2, 0, 1):
        if level == 2:
            grad = contract(hidden, upstream, 0, 0) * scale_f
        elif level == 0:
            grad = contract(pre_gate, inputs, 0, 0) * scale_d
        else:
            grad = contract(pre_up, inputs, 0, 0) * scale_d
        finals = (weights[level].astype(jnp.float32) - lr_inner * grad)[None]
        outgoing_count = finals.shape[0]
        blocks = finals.reshape(outgoing_count, paths, block, width)
        received = lax.all_to_all(
            blocks[jnp.arange(outgoing_count)[:, None], inverse[level : level + outgoing_count]],
            "path",
            split_axis=1,
            concat_axis=1,
            tiled=True,
        )
        owner_count = received.shape[0]
        sums = jnp.einsum(
            "lmp,lpbd->lmbd",
            table[level : level + owner_count],
            received,
            precision=lax.Precision.HIGHEST,
        )
        mean = sums / shares[level : level + owner_count, :, None, None]
        delta = stored[level : level + owner_count] - mean
        velocity = mu_outer * velocity_old[level : level + owner_count] + delta
        owner_fresh = (
            stored[level : level + owner_count] - eta_outer * (delta + mu_outer * velocity)
        ).astype(jnp.bfloat16)
        leaving = owner_fresh[
            jnp.arange(owner_count)[:, None], assignment[level : level + owner_count]
        ]
        returned = lax.all_to_all(leaving, "path", split_axis=1, concat_axis=1, tiled=True)
        fresh_parts[level] = owner_fresh
        count = returned.shape[0]
        placed = returned[jnp.arange(count)[:, None], owner_rows[level : level + count]]
        new_parts[level] = placed.reshape(count, paths * block, width)[0]
    fresh = jnp.concatenate(fresh_parts, axis=0)
    new_weights = jnp.stack(new_parts)
    gate_new = contract(inputs, new_weights[0], 1, 1) * scale_d
    upper_new = contract(inputs, new_weights[1], 1, 1) * scale_d
    hidden_new = (gate_new * jax.nn.sigmoid(gate_new) * upper_new).astype(jnp.bfloat16)
    partial_out = contract(hidden_new, new_weights[2], 1, 0) * scale_f
    outputs = lax.psum_scatter(partial_out, "mp", scatter_dimension=1, tiled=True).astype(
        jnp.bfloat16
    )
    refreshed = fresh.reshape(1, levels, modules, 1, block, width)
    return (outputs, refreshed)


def solution(mesh):
    return jax.shard_map(
        shards,
        mesh=mesh,
        in_specs=(
            P("path", "mp"),
            P("path", "mp"),
            P("path", None, "mp", None),
            P("path", None, None, "mp", None, None),
            P("path", None, None, "mp", None, None),
            P(),
            P(),
        ),
        out_specs=(P("path", "mp"), P("path", None, None, "mp", None, None)),
        check_vma=False,
    )
```

profile of v0, /device:TPU:0, one launch (start us, length us, event | category | flops | bytes accessed | tf_op | source)
XLA Modules:
  0.0 995.7 jit_solution(7992425063736991647)
XLA Ops:
  10.3 21.7 %all-gather.5.cloned.1.call-done = bf16[384,2048]{1,0:T(8,128)(2,1)} async-done(((bf16[384,512]{1,0:T(8,128)(2,1)}), bf16[384,2048]{1,0:T(8,128)(2,1)}) %all-gather.5.cloned.1.call-update) | async-done | bytes 1572880 | tf_op jit(solution)/shard_map/all_gather | solution.py:23
  32.0 5.7 fusion.38
  37.7 15.6 %all-gather.3.cloned.1.call-done = bf16[384,2048]{1,0:T(8,128)(2,1)} async-done(((bf16[384,512]{1,0:T(8,128)(2,1)}), bf16[384,2048]{1,0:T(8,128)(2,1)}) %all-gather.3.cloned.1.call-update) | async-done | bytes 1572880 | tf_op jit(solution)/shard_map/all_gather | solution.py:24
  57.9 8.5 multiply_subtract_fusion.1
  66.4 7.7 gather_fusion.4
  74.1 5.5 all-to-all-start.2
  83.9 8.7 multiply_subtract_fusion.2
  92.6 7.7 gather_fusion.1
  100.3 162.9 %all-to-all-done.2 = f32[1,8,128,2048]{3,2,0,1:T(8,128)} async-done(((f32[1,8,128,2048]{3,2,0,1:T(8,128)}), f32[1,8,128,2048]{3,2,0,1:T(8,128)}, u32[]{:S(2)}, u32[]{:S(2)}) %all-to-all-start.2) | async-done | bytes 8388640 | tf_op jit(solution)/shard_map/all_to_all | solution.py:69
  263.2 5.6 all-to-all-start
  268.8 8.9 multiply_subtract_fusion
  277.7 7.7 gather_fusion.7
  285.4 166.0 %all-to-all-done = f32[1,8,128,2048]{3,2,0,1:T(8,128)} async-done(((f32[1,8,128,2048]{3,2,0,1:T(8,128)}), f32[1,8,128,2048]{3,2,0,1:T(8,128)}, u32[]{:S(2)}, u32[]{:S(2)}) %all-to-all-start) | async-done | bytes 8388640 | tf_op jit(solution)/shard_map/all_to_all | solution.py:69
  456.7 6.0 fusion.74
  466.0 18.1 %fusion.32 = bf16[1,2,128,2048]{3,1,2,0:T(2,128)(2,1)S(1)} fusion(f32[1,3,2,1,128,2048]{5,2,4,3,1,0:T(2,128)S(1)} %copy_convert_fusion, f32[1,1,2,1,128,2048]{5,4,3,2,1,0:T(8,128)} %get-tuple-element.13, f32[1,8,128,2048]{3,2,0,1:T(8,128)} %all-to-all-done, f32[2]{0:T(128)S(1)} %get-tuple-element.23, pred[3,2,8]{2,1,0:T(4,128)(4,1)S(1)} %get-tuple-element.11), kind=kOutput, calls=%fused_computation.57 | convolution fusion | flops 55050240 | bytes 13632512 | tf_op jit(solution)/shard_map/lmp,lpbd->lmbd/dot_general | solution.py:77
  487.3 151.2 %all-to-all-done.4 = f32[1,8,128,2048]{3,2,0,1:T(8,128)} async-done(((f32[1,8,128,2048]{3,2,0,1:T(8,128)}), f32[1,8,128,2048]{3,2,0,1:T(8,128)}, u32[]{:S(2)}, u32[]{:S(2)}) %all-to-all-start.4) | async-done | bytes 8388640 | tf_op jit(solution)/shard_map/all_to_all | solution.py:69
  643.3 16.0 %fusion.31 = bf16[1,2,128,2048]{3,1,2,0:T(2,128)(2,1)S(1)} fusion(f32[1,3,2,1,128,2048]{5,2,4,3,1,0:T(2,128)} %copy-done.2, f32[1,1,2,1,128,2048]{5,4,3,2,1,0:T(8,128)} %get-tuple-element.12, f32[1,8,128,2048]{3,2,0,1:T(8,128)} %all-to-all-done.2, f32[2]{0:T(128)S(1)} %get-tuple-element.21, pred[3,2,8]{2,1,0:T(4,128)(4,1)S(1)} %get-tuple-element.11), kind=kOutput, calls=%fused_computation.55 | convolution fusion | flops 55050240 | bytes 13632512 | tf_op jit(solution)/shard_map/lmp,lpbd->lmbd/dot_general | solution.py:77
  662.5 73.5 %all-to-all-done.1 = bf16[1,8,128,2048]{3,2,0,1:T(8,128)(2,1)} async-done(((bf16[1,8,128,2048]{3,2,0,1:T(8,128)(2,1)}), bf16[1,8,128,2048]{3,2,0,1:T(8,128)(2,1)}, u32[]{:S(2)}, u32[]{:S(2)}) %all-to-all-start.1) | async-done | bytes 4194336 | tf_op jit(solution)/shard_map/all_to_all | solution.py:92
  740.8 16.0 %fusion.30 = bf16[1,2,128,2048]{3,1,2,0:T(2,128)(2,1)S(1)} fusion(f32[1,3,2,1,128,2048]{5,2,4,3,1,0:T(2,128)} %copy-done.2, f32[1,1,2,1,128,2048]{5,4,3,2,1,0:T(8,128)} %get-tuple-element.14, f32[1,8,128,2048]{3,2,0,1:T(8,128)} %all-to-all-done.4, f32[2]{0:T(128)S(1)} %get-tuple-element.22, pred[3,2,8]{2,1,0:T(4,128)(4,1)S(1)} %get-tuple-element.11), kind=kOutput, calls=%fused_computation.53 | convolution fusion | flops 55050240 | bytes 13632512 | tf_op jit(solution)/shard_map/lmp,lpbd->lmbd/dot_general | solution.py:77
  761.0 72.3 %all-to-all-done.3 = bf16[1,8,128,2048]{3,2,0,1:T(8,128)(2,1)} async-done(((bf16[1,8,128,2048]{3,2,0,1:T(8,128)(2,1)}), bf16[1,8,128,2048]{3,2,0,1:T(8,128)(2,1)}, u32[]{:S(2)}, u32[]{:S(2)}) %all-to-all-start.3) | async-done | bytes 4194336 | tf_op jit(solution)/shard_map/all_to_all | solution.py:92
  848.4 82.0 %all-to-all-done.5 = bf16[1,8,128,2048]{3,2,0,1:T(8,128)(2,1)} async-done(((bf16[1,8,128,2048]{3,2,0,1:T(8,128)(2,1)}), bf16[1,8,128,2048]{3,2,0,1:T(8,128)(2,1)}, u32[]{:S(2)}, u32[]{:S(2)}) %all-to-all-start.5) | async-done | bytes 4194336 | tf_op jit(solution)/shard_map/all_to_all | solution.py:92
  935.3 5.6 fusion.75
  941.0 9.7 convolution_multiply_fusion
  960.3 26.6 %reduce-scatter.2.cloned.1.call-done = f32[384,512]{1,0:T(8,128)} async-done(((f32[384,2048]{1,0:T(8,128)}), f32[384,512]{1,0:T(8,128)}) %reduce-scatter.2.cloned.1.call-update) | async-done | bytes 786448 | tf_op jit(solution)/shard_map/reduce_scatter | solution.py:103
  (78 shorter events, 72.1 us)
Async XLA Ops:
  7.2 2.4 copy-start
  7.2 24.8 %all-gather.5.cloned.1.call-start = ((), (), s32[]{:S(2)}) async-start(), calls=%async_computation.8 | async-start | bytes 1966080 | tf_op jit(solution)/shard_map/all_gather | solution.py:23
  7.9 45.3 %all-gather.3.cloned.1.call-start = ((), (), s32[]{:S(2)}) async-start(), calls=%async_computation.7 | async-start | bytes 1966080 | tf_op jit(solution)/shard_map/all_gather | solution.py:24
  37.7 20.2 %copy-start.7 = (bf16[384,2048]{1,0:T(8,128)(2,1)S(1)}, bf16[384,2048]{1,0:T(8,128)(2,1)}, u32[]{:S(2)}) copy-start(bf16[384,2048]{1,0:T(8,128)(2,1)} %all-gather.5.cloned.1.call-done) | copy-start | bytes 4718596
  53.2 4.6 copy-start.9
  57.9 8.5 copy-start.12
  74.1 189.1 %all-to-all-start.2 = ((f32[1,8,128,2048]{3,2,0,1:T(8,128)}), f32[1,8,128,2048]{3,2,0,1:T(8,128)}, u32[]{:S(2)}, u32[]{:S(2)}) async-start(f32[1,8,128,2048]{3,2,0,1:T(8,128)} %bitcast.240), calls=%async_computation.2 | async-start | bytes 16777216 | tf_op jit(solution)/shard_map/all_to_all | solution.py:69
  79.7 4.2 copy-start.10
  79.7 4.2 copy-start.13
  83.9 8.8 copy-start.11
  263.2 5.6 copy-start.8
  263.2 188.2 %all-to-all-start = ((f32[1,8,128,2048]{3,2,0,1:T(8,128)}), f32[1,8,128,2048]{3,2,0,1:T(8,128)}, u32[]{:S(2)}, u32[]{:S(2)}) async-start(f32[1,8,128,2048]{3,2,0,1:T(8,128)} %bitcast.239), calls=%async_computation | async-start | bytes 16777216 | tf_op jit(solution)/shard_map/all_to_all | solution.py:69
  451.4 5.2 copy-start.6
  451.4 187.1 %all-to-all-start.4 = ((f32[1,8,128,2048]{3,2,0,1:T(8,128)}), f32[1,8,128,2048]{3,2,0,1:T(8,128)}, u32[]{:S(2)}, u32[]{:S(2)}) async-start(f32[1,8,128,2048]{3,2,0,1:T(8,128)} %bitcast.238), calls=%async_computation.4 | async-start | bytes 16777216 | tf_op jit(solution)/shard_map/all_to_all | solution.py:69
  456.7 6.0 copy-start.5
  466.0 18.1 %copy-start.2 = (f32[1,3,2,1,128,2048]{5,2,4,3,1,0:T(2,128)}, f32[1,3,2,1,128,2048]{5,2,4,3,1,0:T(2,128)S(1)}, u32[]{:S(2)}) copy-start(f32[1,3,2,1,128,2048]{5,2,4,3,1,0:T(2,128)S(1)} %copy_convert_fusion) | copy-start | bytes 18874372
  638.5 97.5 %all-to-all-start.1 = ((bf16[1,8,128,2048]{3,2,0,1:T(8,128)(2,1)}), bf16[1,8,128,2048]{3,2,0,1:T(8,128)(2,1)}, u32[]{:S(2)}, u32[]{:S(2)}) async-start(bf16[1,8,128,2048]{3,2,0,1:T(8,128)(2,1)} %bitcast.243), calls=%async_computation.1 | async-start | bytes 8388608 | tf_op jit(solution)/shard_map/all_to_all | solution.py:92
  736.0 97.3 %all-to-all-start.3 = ((bf16[1,8,128,2048]{3,2,0,1:T(8,128)(2,1)}), bf16[1,8,128,2048]{3,2,0,1:T(8,128)(2,1)}, u32[]{:S(2)}, u32[]{:S(2)}) async-start(bf16[1,8,128,2048]{3,2,0,1:T(8,128)(2,1)} %bitcast.242), calls=%async_computation.3 | async-start | bytes 8388608 | tf_op jit(solution)/shard_map/all_to_all | solution.py:92
  756.8 1.1 copy-start.3
  833.3 97.1 %all-to-all-start.5 = ((bf16[1,8,128,2048]{3,2,0,1:T(8,128)(2,1)}), bf16[1,8,128,2048]{3,2,0,1:T(8,128)(2,1)}, u32[]{:S(2)}, u32[]{:S(2)}) async-start(bf16[1,8,128,2048]{3,2,0,1:T(8,128)(2,1)} %bitcast.241), calls=%async_computation.5 | async-start | bytes 8388608 | tf_op jit(solution)/shard_map/all_to_all | solution.py:92
  837.9 149.0 %reduce-scatter.2.cloned.1.call-start = ((), (), s32[]{:S(2)}) async-start(), calls=%async_computation.9 | async-start | bytes 3932160 | tf_op jit(solution)/shard_map/reduce_scatter | solution.py:103
  950.7 1.2 copy-start.4
  957.3 31.6 %copy-start.1 = (s32[3,2,8]{2,1,0:T(2,128)S(1)}, s32[3,2,8]{2,1,0:T(2,128)}, u32[]{:S(2)}) copy-start(s32[3,2,8]{2,1,0:T(2,128)} %param.13) | copy-start | bytes 580
Sparse Core Ops, SparseCore 0:
  9.6 22.3 all-gather.4
  33.5 19.6 all-gather.2
  950.8 36.0 reduce-scatter.1
where the time goes:
time: 1010 us; the launch traced here: 996 us
  waiting for transfers between devices  773 us (77%)
  matrix products  106 us (10%)
  local copies, waits for them, and re-layouts  59.6 us (6%)
  starting transfers between devices  30.8 us (3%)
  between operations  14.4 us (1%)
  other arithmetic  11.8 us (1%)
    all_to_all x3, waiting for transfers between devices, shards(): lax.all_to_all(blocks[jnp.arange(outgoing_count)[:, None], inverse[level:...  480 us
    all_to_all x3, waiting for transfers between devices, shards(): lax.all_to_all(leaving, 'path', split_axis=1, concat_axis=1, tiled=True)  228 us
    dot_general x8, matrix products, contract(): lax.dot_general(left, right, (((left_dim,), (right_dim,)), ((), ())), pre...  55.9 us
    dot_general x3, matrix products, shards(): jnp.einsum('lmp,lpbd->lmbd', table[level:level + owner_count], received,...  50.1 us
    reduce_scatter x1, waiting for transfers between devices, shards(): lax.psum_scatter(partial_out, 'mp', scatter_dimension=1, tiled=True)  26.6 us
    gather x3, local copies, waits for them, and re-layouts, shards(): blocks[jnp.arange(outgoing_count)[:, None], inverse[level:level + outgoin...  23.1 us
    all_gather x1, waiting for transfers between devices, shards(): lax.all_gather(tokens, 'mp', axis=1, tiled=True)  21.7 us
  transfers between devices with their start and end apart: 9, of which 9 were waited for; matrix products, arithmetic and copies ran while one was open for 13% of the time, Pallas kernels for 0%

commit v1 on v0

v1 whole, which is shorter than its diff:
```python
import functools

import jax
import jax.numpy as jnp
from jax import lax
from jax.experimental import pallas as pl
from jax.experimental.pallas import tpu as pltpu
from jax.sharding import PartitionSpec as P

mu_outer = 0.9
eta_outer = 0.7
lr_inner = 2.0

STREAMS = 2
FOLD = 2


def contract(left, right, left_dim, right_dim):
    return lax.dot_general(
        left, right, (((left_dim,), (right_dim,)), ((), ())), preferred_element_type=jnp.float32
    )


def params():
    return pltpu.CompilerParams(vmem_limit_bytes=56 * 2**20)


def front_kernel(scale_d, scale_f, x_ref, c_ref, gate_ref, up_ref, down_ref, hidden_ref, pre_gate_ref, pre_up_ref):
    gate = contract(gate_ref[0, 0], x_ref[...], 1, 1) * scale_d
    upper = contract(up_ref[0, 0], x_ref[...], 1, 1) * scale_d
    grad = contract(down_ref[0, 0], c_ref[...], 1, 1) * scale_f
    sig = jax.nn.sigmoid(gate)
    act = gate * sig
    hidden_ref[...] = (act * upper).astype(jnp.bfloat16)
    pre_gate_ref[...] = (grad * upper * sig * (1.0 + gate * (1.0 - sig))).astype(jnp.bfloat16)
    pre_up_ref[...] = (grad * act).astype(jnp.bfloat16)


def front(inputs, upstream, weights, scale_d, scale_f):
    rows, width = inputs.shape
    units = weights.shape[2]
    tile = min(256, units)
    whole = pl.BlockSpec((rows, width), lambda i: (0, 0))
    return pl.pallas_call(
        functools.partial(front_kernel, scale_d, scale_f),
        grid=(units // tile,),
        in_specs=[whole, whole]
        + [pl.BlockSpec((1, 1, tile, width), lambda i, level=level: (0, level, i, 0)) for level in range(3)],
        out_specs=[pl.BlockSpec((tile, rows), lambda i: (i, 0))] * 3,
        out_shape=[jax.ShapeDtypeStruct((units, rows), jnp.bfloat16)] * 3,
        compiler_params=params(),
        cost_estimate=pl.CostEstimate(
            flops=6 * rows * width * units,
            bytes_accessed=6 * units * width + 4 * rows * width + 6 * units * rows,
            transcendentals=units * rows,
        ),
    )(inputs, upstream, weights, weights, weights)


def finals_kernel(scale, block, pieces, table_ref, left_ref, right_ref, weight_ref, own_ref, send_ref):
    grad = contract(left_ref[...], right_ref[...], 1, 0) * (lr_inner * scale)
    for q in range(pieces):
        rows = slice(q * block, (q + 1) * block)
        final = weight_ref[0, 0, rows, :].astype(jnp.float32) - grad[rows]
        spot = table_ref[1, q]

        @pl.when(table_ref[0, q] == 0)
        def _():
            own_ref[spot] = final

        @pl.when(table_ref[0, q] != 0)
        def _():
            send_ref[spot] = final.astype(jnp.bfloat16)


def finals(table, left, right, weights, level, columns, scale, line, block):
    start, tiles, tile = columns
    units, rows = left.shape
    spec = pl.BlockSpec((line, block, tile), lambda t, table: (0, 0, t))
    width = tiles * tile
    shape = (line, block, width)
    return pl.pallas_call(
        functools.partial(finals_kernel, scale, block, units // block),
        grid_spec=pltpu.PrefetchScalarGridSpec(
            num_scalar_prefetch=1,
            grid=(tiles,),
            in_specs=[
                pl.BlockSpec((units, rows), lambda t, table: (0, 0)),
                pl.BlockSpec((rows, tile), lambda t, table: (0, start(t))),
                pl.BlockSpec((1, 1, units, tile), lambda t, table: (0, level, 0, start(t))),
            ],
            out_specs=[spec, spec],
        ),
        out_shape=[jax.ShapeDtypeStruct(shape, jnp.float32), jax.ShapeDtypeStruct(shape, jnp.bfloat16)],
        compiler_params=params(),
        cost_estimate=pl.CostEstimate(
            flops=2 * rows * width * units, bytes_accessed=5 * units * width + 2 * units * rows, transcendentals=0
        ),
    )(table, left, right, weights)


def product(x_ref, parts):
    total = None
    at = 0
    for part in parts:
        width = part.shape[2]
        value = contract(part[...].reshape(-1, width), x_ref[:, at : at + width], 1, 1)
        total = value if total is None else total + value
        at += width
    return total


def gate_kernel(scale, block, line, table_ref, x_ref, *refs):
    out_ref = refs[-1]
    count = (len(refs) - 1) // 2
    for side, parts in enumerate((refs[:count], refs[count:-1])):
        value = product(x_ref, parts) * scale
        for r in range(line):
            out_ref[table_ref[0, side * line + r]] = value[r * block : (r + 1) * block]


def hidden_kernel(scale, block, line, table_ref, x_ref, gate_ref, *refs):
    out_ref = refs[-1]
    count = (len(refs) - 1) // 2
    for side, parts in enumerate((refs[:count], refs[count:-1])):
        value = product(x_ref, parts) * scale
        for r in range(line):
            gate = gate_ref[table_ref[0, side * line + r]]
            upper = value[r * block : (r + 1) * block]
            hidden = gate * jax.nn.sigmoid(gate) * upper
            out_ref[table_ref[1, side * line + r]] = hidden.astype(jnp.bfloat16)


def forward(kernel, table, inputs, extra, parts, dtype, scale, line, block):
    rows = inputs.shape[0]
    pieces = 2 * line
    vmem = pl.BlockSpec(memory_space=pltpu.VMEM)
    return pl.pallas_call(
        functools.partial(kernel, scale, block, line),
        in_specs=[pl.BlockSpec(memory_space=pltpu.SMEM)] + [vmem] * (1 + len(extra) + len(parts)),
        out_specs=vmem,
        out_shape=jax.ShapeDtypeStruct((pieces, block, rows), dtype),
        compiler_params=params(),
        cost_estimate=pl.CostEstimate(
            flops=2 * rows * inputs.shape[1] * pieces * block,
            bytes_accessed=2 * inputs.shape[1] * pieces * block,
            transcendentals=0,
        ),
    )(table, inputs, *extra, *parts)


def down_kernel(scale, left_ref, near_ref, far_ref, out_ref):
    half = left_ref.shape[1] // 2
    width = near_ref.shape[2]
    total = contract(left_ref[:, :half], near_ref[...].reshape(-1, width), 1, 0)
    total = total + contract(left_ref[:, half:], far_ref[...].reshape(-1, width), 1, 0)
    out_ref[...] = total * scale


def down(left, near, far, scale):
    rows, units = left.shape
    line, block, width = near.shape
    tile = width
    spec = pl.BlockSpec((line, block, tile), lambda t: (0, 0, t))
    return pl.pallas_call(
        functools.partial(down_kernel, scale),
        grid=(width // tile,),
        in_specs=[pl.BlockSpec((rows, units), lambda t: (0, 0)), spec, spec],
        out_specs=pl.BlockSpec((rows, tile), lambda t: (0, t)),
        out_shape=jax.ShapeDtypeStruct((rows, width), jnp.float32),
        compiler_params=params(),
        cost_estimate=pl.CostEstimate(
            flops=2 * rows * width * units, bytes_accessed=2 * units * width + 4 * rows * width, transcendentals=0
        ),
    )(left, near, far)


def pairs_of(size, bit):
    return [(i, i ^ bit) for i in range(size)]


def gather_mp(value, size, index):
    parts = [value]
    bit = size // 2
    while bit:
        sent = jnp.concatenate(parts, axis=1)
        got = lax.ppermute(sent, "mp", pairs_of(size, bit))
        high = (index & bit) != 0
        width = value.shape[1]
        merged = []
        for i, part in enumerate(parts):
            other = got[:, i * width : (i + 1) * width]
            merged += [jnp.where(high, other, part), jnp.where(high, part, other)]
        parts = merged
        bit //= 2
    return jnp.concatenate(parts, axis=1)


def scatter_mp(value, size, index):
    width = value.shape[1] // size
    parts = [value[:, i * width : (i + 1) * width] for i in range(size)]
    bit = 1
    while bit < size:
        high = (index & bit) != 0
        keep = [jnp.where(high, parts[i + 1], parts[i]) for i in range(0, len(parts), 2)]
        sent = [jnp.where(high, parts[i], parts[i + 1]) for i in range(0, len(parts), 2)]
        got = lax.ppermute(jnp.concatenate(sent, axis=1), "mp", pairs_of(size, bit))
        parts = [part + got[:, i * width : (i + 1) * width] for i, part in enumerate(keep)]
        bit *= 2
    return parts[0]


def shards(tokens, cotangent, path_weights, outer_weights, momentum, assignment, owners):
    paths = lax.axis_size("path")
    ranks = lax.axis_size("mp")
    line = paths // FOLD
    me = lax.axis_index("path")
    rank = lax.axis_index("mp")
    z, side = me // FOLD, me % FOLD
    levels, units, width = path_weights.shape[1:]
    modules, block = outer_weights.shape[2], outer_weights.shape[4]
    scale_d = width ** (-0.5)
    scale_f = (units * ranks) ** (-0.5)

    module_ids = jnp.arange(modules, dtype=jnp.int32)
    path_ids = jnp.arange(paths, dtype=jnp.int32)
    mine = lax.dynamic_index_in_dim(assignment, me, 1, keepdims=False)
    theirs = lax.dynamic_index_in_dim(assignment, me ^ 1, 1, keepdims=False)
    is_mine = mine[:, None] == module_ids[None, :]
    is_theirs = theirs[:, None] == module_ids[None, :]
    shares = jnp.sum((assignment[:, None, :] == module_ids[None, :, None]).astype(jnp.float32), axis=2)
    owner_rows = jnp.sum(jnp.where(is_mine[:, :, None], owners, 0), axis=1)
    apart = (owner_rows % FOLD) ^ side
    leaves = jnp.stack([apart, owner_rows // FOLD], axis=1)
    slot = apart * line + (z - owner_rows // FOLD + line) % line
    piece_at = jnp.sum(
        jnp.where(slot[:, None, :] == path_ids[None, :, None], path_ids[None, None, :], 0), axis=2
    )
    down_at = jnp.sum(
        jnp.where(piece_at[1][:, None] == path_ids[None, :], slot[2][None, :], 0), axis=1
    )
    gate_table = piece_at[0][None]
    hidden_table = jnp.stack([piece_at[1], down_at])

    right = [(i, i + FOLD) for i in range(paths - FOLD)]
    left = [(i + FOLD, i) for i in range(paths - FOLD)]
    across = pairs_of(paths, 1)

    def permute(value, pairs):
        return lax.ppermute(value, "path", pairs)

    half = width // STREAMS
    narrow = width // (ranks * STREAMS)

    def ranges(level, s):
        if level == 2:
            return [(j * narrow * STREAMS + s * narrow, narrow) for j in range(ranks)]
        return [(s * half, half)]

    def columns(level, s):
        if level == 2:
            return (lambda t: t * STREAMS + s), ranks, narrow
        tile = min(512, half)
        return (lambda t: s * (half // tile) + t), half // tile, tile

    def cut(array, level, s):
        parts = [array[..., at : at + size] for at, size in ranges(level, s)]
        return parts[0] if len(parts) == 1 else jnp.concatenate(parts, axis=-1)

    inputs = gather_mp(tokens, ranks, rank)
    upstream = gather_mp(cotangent, ranks, rank)
    hidden, pre_gate, pre_up = front(inputs, upstream, path_weights, scale_d, scale_f)
    sources = ((pre_gate, inputs, scale_d), (pre_up, inputs, scale_d), (hidden, upstream, scale_f))

    zeros = jnp.zeros((modules, block, half), jnp.bfloat16)
    flow = [[zeros, zeros] for _ in range(STREAMS)]
    waiting = [None] * STREAMS
    near = [[None] * STREAMS for _ in range(levels)]
    far = [[None] * STREAMS for _ in range(levels)]
    fresh_all = [[None] * STREAMS for _ in range(levels)]

    def term(own, got, level, at, live):
        kept = lax.dynamic_index_in_dim(own, at, 0, keepdims=True)
        come = lax.dynamic_index_in_dim(got, at, 0, keepdims=True).astype(jnp.float32)
        a = (is_mine[level] & live)[:, None, None]
        b = (is_theirs[level] & live)[:, None, None]
        return jnp.where(a, kept, 0.0) + jnp.where(b, come, 0.0)

    def deliver(level, s, seen):
        fresh, rights, lefts = seen
        ring = [fresh] + [
            jnp.where(z >= r, rights[r - 1], lefts[line - 1 - r]) for r in range(1, line)
        ]
        pick = lambda m: jnp.stack([lax.dynamic_index_in_dim(a, m, 0, keepdims=False) for a in ring])
        near[level][s] = pick(mine[level])
        far[level][s] = permute(pick(theirs[level]), across)

    def round_(level, s):
        if level < levels:
            source = sources[level]
            own, send = finals(
                leaves[level], source[0], source[1], path_weights, level, columns(level, s), source[2], line, block
            )
            got = permute(send, across)
        for step in range(1, line):
            moved = []
            for way, pairs in enumerate((right, left)):
                value = flow[s][way]
                if level < levels:
                    at = line - step + z if way == 0 else z - line + step
                    live = z < step if way == 0 else z >= line - step
                    value = value.astype(jnp.float32) + term(own, got, level, jnp.clip(at, 0, line - 1), live)
                    value = value.astype(jnp.bfloat16)
                elif step == line - 1:
                    break
                moved.append(permute(value, pairs))
            if moved:
                flow[s] = moved
            if waiting[s] is not None:
                if step < line - 1:
                    waiting[s][1].append(moved[0])
                    waiting[s][2].append(moved[1])
                if step == max(line - 2, 1):
                    deliver(level - 1, s, waiting[s])
        if level < levels:
            sums = term(own, got, level, z, True) + flow[s][0].astype(jnp.float32) + flow[s][1].astype(jnp.float32)
            stored = cut(outer_weights[0, level, :, 0], level, s)
            old = cut(momentum[0, level, :, 0], level, s).astype(jnp.float32)
            delta = stored - sums / shares[level][:, None, None]
            velocity = mu_outer * old + delta
            fresh = (stored - eta_outer * (delta + mu_outer * velocity)).astype(jnp.bfloat16)
            fresh_all[level][s] = fresh
            flow[s] = [permute(fresh, right), permute(fresh, left)]
            waiting[s] = (fresh, [flow[s][0]], [flow[s][1]])

    gate_new = hidden_new = None
    outs = []
    for level in range(levels + 1):
        for s in range(STREAMS):
            round_(level, s)
            if level == 3:
                total = down(hidden_new, near[2][s], far[2][s], scale_f)
                outs.append(scatter_mp(total, ranks, rank))
        if level == 1:
            gate_new = forward(
                gate_kernel, gate_table, inputs, (), near[0] + far[0], jnp.float32, scale_d, line, block
            )
        if level == 2:
            value = forward(
                hidden_kernel, hidden_table, inputs, (gate_new,), near[1] + far[1], jnp.bfloat16, scale_d, line, block
            )
            hidden_new = value.reshape(units, -1).T

    outputs = jnp.concatenate(outs, axis=1).astype(jnp.bfloat16)
    rows = []
    for level in range(levels):
        parts = {}
        for s in range(STREAMS):
            at = 0
            for start, size in ranges(level, s):
                parts[start] = fresh_all[level][s][..., at : at + size]
                at += size
        rows.append(jnp.concatenate([parts[k] for k in sorted(parts)], axis=-1))
    refreshed = jnp.stack(rows).reshape(1, levels, modules, 1, block, width)
    return outputs, refreshed


def solution(mesh):
    return jax.shard_map(
        shards,
        mesh=mesh,
        in_specs=(
            P("path", "mp"),
            P("path", "mp"),
            P("path", None, "mp", None),
            P("path", None, None, "mp", None, None),
            P("path", None, None, "mp", None, None),
            P(),
            P(),
        ),
        out_specs=(P("path", "mp"), P("path", None, None, "mp", None, None)),
        check_vma=False,
    )
```

time: 1010 us -> 580 us (0.57)
  waiting for transfers between devices: 773 us -> 199 us
  starting transfers between devices: 30.8 us -> 179 us
  matrix products: 106 us -> 0 us
  Pallas kernels: 0 us -> 67.5 us
  other arithmetic: 11.8 us -> 64.8 us
  local copies, waits for them, and re-layouts: 59.6 us -> 44.3 us
    all_to_all x6 -> x0, waiting for transfers between devices: 708 us -> none  [the longest x3 480 us: shards(): lax.all_to_all(blocks[jnp.arange(outgoing_count)[:, None], inverse[level:...]
    ppermute x0 -> x76, waiting for transfers between devices: none -> 199 us  [the longest x68 184 us: permute(): return lax.ppermute(value, 'path', pairs)]
    ppermute x0 -> x76, starting transfers between devices: none -> 179 us  [the longest x68 174 us: permute(): return lax.ppermute(value, 'path', pairs)]
    dot_general x11 -> x0, matrix products: 106 us -> none  [the longest x8 55.9 us: contract(): lax.dot_general(left, right, (((left_dim,), (right_dim,)), ((), ())), pre...]
    pallas_call x0 -> x11, Pallas kernels: none -> 67.5 us  [the longest x6 35.5 us: finals(): pl.pallas_call(functools.partial(finals_kernel, scale, block, units // bl...]
    gather x10 -> x0, local copies, waits for them, and re-layouts: 47.2 us -> none  [the longest x3 23.1 us: shards(): blocks[jnp.arange(outgoing_count)[:, None], inverse[level:level + outgoin...]
    all_gather x2 -> x0, waiting for transfers between devices: 37.3 us -> none  [the longest x1 21.7 us: shards(): lax.all_gather(tokens, 'mp', axis=1, tiled=True)]
    all_to_all x6 -> x0, starting transfers between devices: 30.4 us -> none  [the longest x3 16.2 us: shards(): lax.all_to_all(blocks[jnp.arange(outgoing_count)[:, None], inverse[level:...]
  transfers between devices with their start and end apart: 9 -> 76, of which waited for: 9 -> 40; matrix products, arithmetic and copies ran while one was open for 13% -> 16% of each run, Pallas kernels for 0% -> 9%
where the time goes in v1:
time: 580 us; the launch traced here: 569 us
  waiting for transfers between devices  199 us (34%)
  starting transfers between devices  179 us (31%)
  Pallas kernels  67.5 us (12%)
  other arithmetic  64.8 us (11%)
  local copies, waits for them, and re-layouts  44.3 us (8%)
  between operations  14.3 us (2%)
    ppermute x68, waiting for transfers between devices, permute(): return lax.ppermute(value, 'path', pairs)  184 us
    ppermute x68, starting transfers between devices, permute(): return lax.ppermute(value, 'path', pairs)  174 us
    pallas_call x6, Pallas kernels, finals(): pl.pallas_call(functools.partial(finals_kernel, scale, block, units // bl...  35.5 us
    convert_element_type x18, other arithmetic, round_(): value = value.astype(jnp.bfloat16)  15.7 us
    ppermute x4, waiting for transfers between devices, scatter_mp(): got = lax.ppermute(jnp.concatenate(sent, axis=1), 'mp', pairs_of(size, bit))  14.4 us
    pallas_call x2, Pallas kernels, forward(): pl.pallas_call(functools.partial(kernel, scale, block, line), in_specs=[p...  12.6 us
    unnamed x259, local copies, waits for them, and re-layouts  11.7 us
    pallas_call x1, Pallas kernels, front(): pl.pallas_call(functools.partial(front_kernel, scale_d, scale_f), grid=(u...  11.6 us
  transfers between devices with their start and end apart: 76, of which 40 were waited for; matrix products, arithmetic and copies ran while one was open for 16% of the time, Pallas kernels for 9%

profile of v1, /device:TPU:0, one launch (start us, length us, event | category | flops | bytes accessed | tf_op | source)
XLA Modules:
  0.0 569.3 jit_solution(17603241236695878978)
XLA Ops:
  8.2 5.8 %slice_bitcast_fusion = (f32[2,128,2048]{2,1,0:T(8,128)}, f32[2,128,2048]{2,1,0:T(8,128)S(1)}, f32[2,128,2048]{2,1,0:T(8,128)}) fusion(f32[1,3,2,1,128,2048]{5,4,2,3,1,0:T(8,128)} %bitcast.363), kind=kLoop, calls=%fused_computation.1 | loop fusion | bytes 12582912 | tf_op jit(solution)/shard_map/squeeze | solution.py:327
  47.4 11.6 %shard_map.86 = (bf16[1024,384]{1,0:T(8,128)(2,1)}, bf16[1024,384]{1,0:T(8,128)(2,1)}, bf16[1024,384]{1,0:T(8,128)(2,1)}) custom-call(bf16[384,2048]{1,0:T(8,128)(2,1)} %pad_maximum_fusion.x_ref.right_ref, bf16[384,2048]{1,0:T(8,128)(2,1)} %pad_maximum_fusion.1.c_ref.right_ref, bf16[1,3,1024,2048]{3,2,1,0:T(8,128)(2,1)} %weight_ref.11, ...), custom_call_target="tpu_custom_call" | custom-call | flops 4831838208 | bytes 18087936 | tf_op jit(solution)/shard_map/pallas_call | solution.py:44
  78.4 5.6 shard_map.88
  84.0 6.6 %shard_map.93 = (f32[4,128,1024]{2,1,0:T(8,128)}, bf16[4,128,1024]{2,1,0:T(8,128)(2,1)}) custom-call(s32[2,8]{1,0:T(2,128)} %bitcast.366, bf16[1024,384]{1,0:T(8,128)(2,1)} %get-tuple-element.27.left_ref, bf16[384,2048]{1,0:T(8,128)(2,1)} %pad_maximum_fusion.1.c_ref.right_ref, bf16[1,3,1024,2048]{3,2,1,0:T(8,128)(2,1)} %weight_ref.11), custom_call_target="tpu_custom_call" | custom-call | flops 805306368 | bytes 6029312 | tf_op jit(solution)/shard_map/pallas_call | solution.py:82
  96.6 16.0 %collective-permute-done.4 = bf16[4,128,1024]{2,1,0:T(8,128)(2,1)S(1)} collective-permute-done((bf16[4,128,1024]{2,1,0:T(8,128)(2,1)}, bf16[4,128,1024]{2,1,0:T(8,128)(2,1)S(1)}, u32[]{:S(2)}, u32[]{:S(2)}) %collective-permute-start.4) | collective-permute-done | bytes 1048608 | tf_op jit(solution)/shard_map/ppermute | solution.py:250
  118.2 6.5 %shard_map.92 = (f32[4,128,1024]{2,1,0:T(8,128)}, bf16[4,128,1024]{2,1,0:T(8,128)(2,1)}) custom-call(s32[2,8]{1,0:T(2,128)} %bitcast.367, bf16[1024,384]{1,0:T(8,128)(2,1)} %get-tuple-element.27.left_ref, bf16[384,2048]{1,0:T(8,128)(2,1)} %pad_maximum_fusion.1.c_ref.right_ref, bf16[1,3,1024,2048]{3,2,1,0:T(8,128)(2,1)} %weight_ref.11), custom_call_target="tpu_custom_call" | custom-call | flops 805306368 | bytes 6029312 | tf_op jit(solution)/shard_map/pallas_call | solution.py:82
  147.4 7.4 %collective-permute-done.5 = bf16[2,128,1024]{2,1,0:T(8,128)(2,1)S(1)} collective-permute-done((bf16[2,128,1024]{2,1,0:T(8,128)(2,1)S(1)}, bf16[2,128,1024]{2,1,0:T(8,128)(2,1)S(1)}, u32[]{:S(2)}, u32[]{:S(2)}) %collective-permute-start.5) | collective-permute-done | bytes 524320 | tf_op jit(solution)/shard_map/ppermute | solution.py:250
  172.2 7.8 %collective-permute-done.6 = bf16[2,128,1024]{2,1,0:T(8,128)(2,1)S(1)} collective-permute-done((bf16[2,128,1024]{2,1,0:T(8,128)(2,1)S(1)}, bf16[2,128,1024]{2,1,0:T(8,128)(2,1)S(1)}, u32[]{:S(2)}, u32[]{:S(2)}) %collective-permute-start.6) | collective-permute-done | bytes 524320 | tf_op jit(solution)/shard_map/ppermute | solution.py:250
  197.5 6.9 %collective-permute-done.7 = bf16[2,128,1024]{2,1,0:T(8,128)(2,1)S(1)} collective-permute-done((bf16[2,128,1024]{2,1,0:T(8,128)(2,1)S(1)}, bf16[2,128,1024]{2,1,0:T(8,128)(2,1)S(1)}, u32[]{:S(2)}, u32[]{:S(2)}) %collective-permute-start.7) | collective-permute-done | bytes 524320 | tf_op jit(solution)/shard_map/ppermute | solution.py:250
  220.1 15.8 %collective-permute-done.38 = bf16[4,128,1024]{2,1,0:T(8,128)(2,1)S(1)} collective-permute-done((bf16[4,128,1024]{2,1,0:T(8,128)(2,1)S(1)}, bf16[4,128,1024]{2,1,0:T(8,128)(2,1)S(1)}, u32[]{:S(2)}, u32[]{:S(2)}) %collective-permute-start.38) | collective-permute-done | bytes 1048608 | tf_op jit(solution)/shard_map/ppermute | solution.py:250
  253.8 6.5 %collective-permute-done.26 = bf16[2,128,1024]{2,1,0:T(8,128)(2,1)S(1)} collective-permute-done((bf16[2,128,1024]{2,1,0:T(8,128)(2,1)S(1)}, bf16[2,128,1024]{2,1,0:T(8,128)(2,1)S(1)}, u32[]{:S(2)}, u32[]{:S(2)}) %collective-permute-start.26) | collective-permute-done | bytes 524320 | tf_op jit(solution)/shard_map/ppermute | solution.py:250
  270.3 6.0 %collective-permute-done.14 = bf16[2,128,1024]{2,1,0:T(8,128)(2,1)S(1)} collective-permute-done((bf16[2,128,1024]{2,1,0:T(8,128)(2,1)S(1)}, bf16[2,128,1024]{2,1,0:T(8,128)(2,1)S(1)}, u32[]{:S(2)}, u32[]{:S(2)}) %collective-permute-start.14) | collective-permute-done | bytes 524320 | tf_op jit(solution)/shard_map/ppermute | solution.py:250
  276.3 7.4 %collective-permute-done.28 = bf16[2,128,1024]{2,1,0:T(8,128)(2,1)S(1)} collective-permute-done((bf16[2,128,1024]{2,1,0:T(8,128)(2,1)S(1)}, bf16[2,128,1024]{2,1,0:T(8,128)(2,1)S(1)}, u32[]{:S(2)}, u32[]{:S(2)}) %collective-permute-start.28) | collective-permute-done | bytes 524320 | tf_op jit(solution)/shard_map/ppermute | solution.py:250
  291.7 7.0 %collective-permute-done.15 = bf16[2,128,1024]{2,1,0:T(8,128)(2,1)S(1)} collective-permute-done((bf16[2,128,1024]{2,1,0:T(8,128)(2,1)S(1)}, bf16[2,128,1024]{2,1,0:T(8,128)(2,1)S(1)}, u32[]{:S(2)}, u32[]{:S(2)}) %collective-permute-start.15) | collective-permute-done | bytes 524320 | tf_op jit(solution)/shard_map/ppermute | solution.py:250
  300.0 7.0 %collective-permute-done.29 = bf16[2,128,1024]{2,1,0:T(8,128)(2,1)S(1)} collective-permute-done((bf16[2,128,1024]{2,1,0:T(8,128)(2,1)S(1)}, bf16[2,128,1024]{2,1,0:T(8,128)(2,1)S(1)}, u32[]{:S(2)}, u32[]{:S(2)}) %collective-permute-start.29) | collective-permute-done | bytes 524320 | tf_op jit(solution)/shard_map/ppermute | solution.py:250
  321.2 5.6 collective-permute-done.35
  376.8 6.2 %shard_map.91.gate_ref = f32[8,128,384]{2,1,0:T(8,128)} custom-call(s32[1,8]{1,0:T(1,128)} %get-tuple-element.240.table_ref, bf16[384,2048]{1,0:T(8,128)(2,1)} %pad_maximum_fusion.x_ref.right_ref, bf16[4,128,1024]{2,1,0:T(8,128)(2,1)} %pad_maximum_fusion.2.refs_0_, bf16[4,128,1024]{2,1,0:T(8,128)(2,1)} %pad_maximum_fusion.3.refs_1_, ...), custom_call_target="tpu_custom_call" | custom-call | flops 1610612736 | bytes 4194304 | tf_op jit(solution)/shard_map/pallas_call | solution.py:138
  386.2 5.6 collective-permute-start.42
  391.8 7.8 %collective-permute-done.48 = bf16[2,128,1024]{2,1,0:T(8,128)(2,1)} collective-permute-done((bf16[2,128,1024]{2,1,0:T(8,128)(2,1)}, bf16[2,128,1024]{2,1,0:T(8,128)(2,1)}, u32[]{:S(2)}, u32[]{:S(2)}) %collective-permute-start.48) | collective-permute-done | bytes 524320 | tf_op jit(solution)/shard_map/ppermute | solution.py:250
  411.6 7.0 %collective-permute-done.40 = bf16[2,128,1024]{2,1,0:T(8,128)(2,1)S(1)} collective-permute-done((bf16[2,128,1024]{2,1,0:T(8,128)(2,1)S(1)}, bf16[2,128,1024]{2,1,0:T(8,128)(2,1)S(1)}, u32[]{:S(2)}, u32[]{:S(2)}) %collective-permute-start.40) | collective-permute-done | bytes 524320 | tf_op jit(solution)/shard_map/ppermute | solution.py:250
  420.1 9.2 %collective-permute-done.49 = bf16[2,128,1024]{2,1,0:T(8,128)(2,1)S(1)} collective-permute-done((bf16[2,128,1024]{2,1,0:T(8,128)(2,1)S(1)}, bf16[2,128,1024]{2,1,0:T(8,128)(2,1)S(1)}, u32[]{:S(2)}, u32[]{:S(2)}) %collective-permute-start.49) | collective-permute-done | bytes 524320 | tf_op jit(solution)/shard_map/ppermute | solution.py:250
  518.0 6.4 %shard_map.94 = bf16[8,128,384]{2,1,0:T(8,128)(2,1)} custom-call(s32[2,8]{1,0:T(2,128)} %pad_add_fusion.3.table_ref, bf16[384,2048]{1,0:T(8,128)(2,1)} %pad_maximum_fusion.x_ref.right_ref, f32[8,128,384]{2,1,0:T(8,128)} %shard_map.91.gate_ref, bf16[4,128,1024]{2,1,0:T(8,128)(2,1)} %pad_maximum_fusion.6.refs_0_, ...), custom_call_target="tpu_custom_call" | custom-call | flops 1610612736 | bytes 4194304 | tf_op jit(solution)/shard_map/pallas_call | solution.py:138
  553.5 6.4 %collective-permute-done.75 = f32[384,256]{1,0:T(8,128)S(1)} collective-permute-done((f32[384,256]{1,0:T(8,128)S(1)}, f32[384,256]{1,0:T(8,128)S(1)}, u32[]{:S(2)}, u32[]{:S(2)}) %collective-permute-start.75) | collective-permute-done | bytes 393248 | tf_op jit(solution)/shard_map/ppermute | solution.py:207
  560.0 7.9 %collective-permute-done.64 = f32[384,256]{1,0:T(8,128)S(1)} collective-permute-done((f32[384,256]{1,0:T(8,128)S(1)}, f32[384,256]{1,0:T(8,128)S(1)}, u32[]{:S(2)}, u32[]{:S(2)}) %collective-permute-start.64) | collective-permute-done | bytes 393248 | tf_op jit(solution)/shard_map/ppermute | solution.py:207
  (531 shorter events, 368.8 us)
Async XLA Ops:
  64.6 30.2 %collective-permute-start.18 = (bf16[4,128,1024]{2,1,0:T(8,128)(2,1)}, bf16[4,128,1024]{2,1,0:T(8,128)(2,1)S(1)}, u32[]{:S(2)}, u32[]{:S(2)}) collective-permute-start(bf16[4,128,1024]{2,1,0:T(8,128)(2,1)} %get-tuple-element.24), channel_id=1, source_target_pairs={{0,4},{4,0},{8,12},{12,8},{16,20},{20,16},{24,28},{28,24},{1,5},{5... | collective-permute-start | bytes 3145736 | tf_op jit(solution)/shard_map/ppermute | solution.py:250
  72.7 39.9 %collective-permute-start.4 = (bf16[4,128,1024]{2,1,0:T(8,128)(2,1)}, bf16[4,128,1024]{2,1,0:T(8,128)(2,1)S(1)}, u32[]{:S(2)}, u32[]{:S(2)}) collective-permute-start(bf16[4,128,1024]{2,1,0:T(8,128)(2,1)} %get-tuple-element.19), channel_id=1, source_target_pairs={{0,4},{4,0},{8,12},{12,8},{16,20},{20,16},{24,28},{28,24},{1,5},{5... | collective-permute-start | bytes 3145736 | tf_op jit(solution)/shard_map/ppermute | solution.py:250
  116.8 25.3 %collective-permute-start.8 = (bf16[2,128,1024]{2,1,0:T(8,128)(2,1)}, bf16[2,128,1024]{2,1,0:T(8,128)(2,1)}, u32[]{:S(2)}, u32[]{:S(2)}) collective-permute-start(bf16[2,128,1024]{2,1,0:T(8,128)(2,1)} %get-tuple-element.278), channel_id=1, source_target_pairs={{8,0},{12,4},{16,8},{20,12},{24,16},{28,20},{9,1},{13,5},{17,9},{2... | collective-permute-start | bytes 1572872 | tf_op jit(solution)/shard_map/ppermute | solution.py:250
  124.6 61.8 %collective-permute-start.27 = (bf16[4,128,1024]{2,1,0:T(8,128)(2,1)}, bf16[4,128,1024]{2,1,0:T(8,128)(2,1)S(1)}, u32[]{:S(2)}, u32[]{:S(2)}) collective-permute-start(bf16[4,128,1024]{2,1,0:T(8,128)(2,1)} %get-tuple-element.26), channel_id=1, source_target_pairs={{0,4},{4,0},{8,12},{12,8},{16,20},{20,16},{24,28},{28,24},{1,5},{5... | collective-permute-start | bytes 3145736 | tf_op jit(solution)/shard_map/ppermute | solution.py:250
  126.4 66.1 %collective-permute-start.13 = (bf16[4,128,1024]{2,1,0:T(8,128)(2,1)}, bf16[4,128,1024]{2,1,0:T(8,128)(2,1)S(1)}, u32[]{:S(2)}, u32[]{:S(2)}) collective-permute-start(bf16[4,128,1024]{2,1,0:T(8,128)(2,1)} %get-tuple-element.22), channel_id=1, source_target_pairs={{0,4},{4,0},{8,12},{12,8},{16,20},{20,16},{24,28},{28,24},{1,5},{5... | collective-permute-start | bytes 3145736 | tf_op jit(solution)/shard_map/ppermute | solution.py:250
  146.1 23.3 %collective-permute-start.9 = (bf16[2,128,1024]{2,1,0:T(8,128)(2,1)S(1)}, bf16[2,128,1024]{2,1,0:T(8,128)(2,1)S(1)}, u32[]{:S(2)}, u32[]{:S(2)}) collective-permute-start(bf16[2,128,1024]{2,1,0:T(8,128)(2,1)S(1)} %get-tuple-element.276), channel_id=1, source_target_pairs={{8,0},{12,4},{16,8},{20,12},{24,16},{28,20},{9,1},{13,5},{17,9},{2... | collective-permute-start | bytes 1572872 | tf_op jit(solution)/shard_map/ppermute | solution.py:250
  169.9 24.3 %collective-permute-start.24 = (bf16[2,128,1024]{2,1,0:T(8,128)(2,1)S(1)}, bf16[2,128,1024]{2,1,0:T(8,128)(2,1)S(1)}, u32[]{:S(2)}, u32[]{:S(2)}) collective-permute-start(bf16[2,128,1024]{2,1,0:T(8,128)(2,1)S(1)} %get-tuple-element.273), channel_id=1, source_target_pairs={{8,0},{12,4},{16,8},{20,12},{24,16},{28,20},{9,1},{13,5},{17,9},{2... | collective-permute-start | bytes 1572872 | tf_op jit(solution)/shard_map/ppermute | solution.py:250
  192.4 26.2 %collective-permute-start.47 = (bf16[4,128,1024]{2,1,0:T(8,128)(2,1)S(1)}, bf16[4,128,1024]{2,1,0:T(8,128)(2,1)S(1)}, u32[]{:S(2)}, u32[]{:S(2)}) collective-permute-start(bf16[4,128,1024]{2,1,0:T(8,128)(2,1)S(1)} %copy-done.124), channel_id=1, source_target_pairs={{0,4},{4,0},{8,12},{12,8},{16,20},{20,16},{24,28},{28,24},{1,5},{5... | collective-permute-start | bytes 3145736 | tf_op jit(solution)/shard_map/ppermute | solution.py:250
  194.4 41.5 %collective-permute-start.38 = (bf16[4,128,1024]{2,1,0:T(8,128)(2,1)S(1)}, bf16[4,128,1024]{2,1,0:T(8,128)(2,1)S(1)}, u32[]{:S(2)}, u32[]{:S(2)}) collective-permute-start(bf16[4,128,1024]{2,1,0:T(8,128)(2,1)S(1)} %copy-done.125), channel_id=1, source_target_pairs={{0,4},{4,0},{8,12},{12,8},{16,20},{20,16},{24,28},{28,24},{1,5},{5... | collective-permute-start | bytes 3145736 | tf_op jit(solution)/shard_map/ppermute | solution.py:250
  205.7 34.6 %collective-permute-start.25 = (bf16[2,128,1024]{2,1,0:T(8,128)(2,1)S(1)}, bf16[2,128,1024]{2,1,0:T(8,128)(2,1)S(1)}, u32[]{:S(2)}, u32[]{:S(2)}) collective-permute-start(bf16[2,128,1024]{2,1,0:T(8,128)(2,1)S(1)} %get-tuple-element.51), channel_id=1, source_target_pairs={{0,8},{4,12},{8,16},{12,20},{16,24},{20,28},{1,9},{5,13},{9,17},{1... | collective-permute-start | bytes 1572872 | tf_op jit(solution)/shard_map/ppermute | solution.py:250
  210.1 30.1 %collective-permute-start.11 = (bf16[2,128,1024]{2,1,0:T(8,128)(2,1)S(1)}, bf16[2,128,1024]{2,1,0:T(8,128)(2,1)S(1)}, u32[]{:S(2)}, u32[]{:S(2)}) collective-permute-start(bf16[2,128,1024]{2,1,0:T(8,128)(2,1)S(1)} %get-tuple-element.52), channel_id=1, source_target_pairs={{0,8},{4,12},{8,16},{12,20},{16,24},{20,28},{1,9},{5,13},{9,17},{1... | collective-permute-start | bytes 1572872 | tf_op jit(solution)/shard_map/ppermute | solution.py:250
  240.8 23.7 %collective-permute-start.30 = (bf16[2,128,1024]{2,1,0:T(8,128)(2,1)S(1)}, bf16[2,128,1024]{2,1,0:T(8,128)(2,1)S(1)}, u32[]{:S(2)}, u32[]{:S(2)}) collective-permute-start(bf16[2,128,1024]{2,1,0:T(8,128)(2,1)S(1)} %get-tuple-element.265), channel_id=1, source_target_pairs={{0,8},{4,12},{8,16},{12,20},{16,24},{20,28},{1,9},{5,13},{9,17},{1... | collective-permute-start | bytes 1572872 | tf_op jit(solution)/shard_map/ppermute | solution.py:250
  265.1 26.6 %collective-permute-start.17 = (bf16[2,128,1024]{2,1,0:T(8,128)(2,1)S(1)}, bf16[2,128,1024]{2,1,0:T(8,128)(2,1)S(1)}, u32[]{:S(2)}, u32[]{:S(2)}) collective-permute-start(bf16[2,128,1024]{2,1,0:T(8,128)(2,1)S(1)} %get-tuple-element.264), channel_id=1, source_target_pairs={{0,8},{4,12},{8,16},{12,20},{16,24},{20,28},{1,9},{5,13},{9,17},{1... | collective-permute-start | bytes 1572872 | tf_op jit(solution)/shard_map/ppermute | solution.py:250
  285.5 23.5 %collective-permute-start.31 = (bf16[2,128,1024]{2,1,0:T(8,128)(2,1)S(1)}, bf16[2,128,1024]{2,1,0:T(8,128)(2,1)S(1)}, u32[]{:S(2)}, u32[]{:S(2)}) collective-permute-start(bf16[2,128,1024]{2,1,0:T(8,128)(2,1)S(1)} %get-tuple-element.263), channel_id=1, source_target_pairs={{0,8},{4,12},{8,16},{12,20},{16,24},{20,28},{1,9},{5,13},{9,17},{1... | collective-permute-start | bytes 1572872 | tf_op jit(solution)/shard_map/ppermute | solution.py:250
  299.0 74.7 %collective-permute-start.32 = (bf16[4,128,1024]{2,1,0:T(8,128)(2,1)S(1)}, bf16[4,128,1024]{2,1,0:T(8,128)(2,1)S(1)}, u32[]{:S(2)}, u32[]{:S(2)}) collective-permute-start(bf16[4,128,1024]{2,1,0:T(8,128)(2,1)S(1)} %pad_maximum_fusion.4), channel_id=1, source_target_pairs={{0,4},{4,0},{8,12},{12,8},{16,20},{20,16},{24,28},{28,24},{1,5},{5... | collective-permute-start | bytes 3145736 | tf_op jit(solution)/shard_map/ppermute | solution.py:250
  336.6 39.3 %collective-permute-start.33 = (bf16[4,128,1024]{2,1,0:T(8,128)(2,1)S(1)}, bf16[4,128,1024]{2,1,0:T(8,128)(2,1)S(1)}, u32[]{:S(2)}, u32[]{:S(2)}) collective-permute-start(bf16[4,128,1024]{2,1,0:T(8,128)(2,1)S(1)} %pad_maximum_fusion.5), channel_id=1, source_target_pairs={{0,4},{4,0},{8,12},{12,8},{16,20},{20,16},{24,28},{28,24},{1,5},{5... | collective-permute-start | bytes 3145736 | tf_op jit(solution)/shard_map/ppermute | solution.py:250
  346.7 24.2 %collective-permute-start.46 = (bf16[2,128,1024]{2,1,0:T(8,128)(2,1)S(1)}, bf16[2,128,1024]{2,1,0:T(8,128)(2,1)S(1)}, u32[]{:S(2)}, u32[]{:S(2)}) collective-permute-start(bf16[2,128,1024]{2,1,0:T(8,128)(2,1)S(1)} %get-tuple-element.49), channel_id=1, source_target_pairs={{8,0},{12,4},{16,8},{20,12},{24,16},{28,20},{9,1},{13,5},{17,9},{2... | collective-permute-start | bytes 1572872 | tf_op jit(solution)/shard_map/ppermute | solution.py:250
  355.1 27.9 %collective-permute-start.50 = (bf16[2,128,1024]{2,1,0:T(8,128)(2,1)}, bf16[2,128,1024]{2,1,0:T(8,128)(2,1)S(1)}, u32[]{:S(2)}, u32[]{:S(2)}) collective-permute-start(bf16[2,128,1024]{2,1,0:T(8,128)(2,1)} %get-tuple-element.253), channel_id=1, source_target_pairs={{0,8},{4,12},{8,16},{12,20},{16,24},{20,28},{1,9},{5,13},{9,17},{1... | collective-permute-start | bytes 1572872 | tf_op jit(solution)/shard_map/ppermute | solution.py:250
  360.4 22.6 %collective-permute-start.41 = (bf16[2,128,1024]{2,1,0:T(8,128)(2,1)}, bf16[2,128,1024]{2,1,0:T(8,128)(2,1)S(1)}, u32[]{:S(2)}, u32[]{:S(2)}) collective-permute-start(bf16[2,128,1024]{2,1,0:T(8,128)(2,1)} %get-tuple-element.254), channel_id=1, source_target_pairs={{0,8},{4,12},{8,16},{12,20},{16,24},{20,28},{1,9},{5,13},{9,17},{1... | collective-permute-start | bytes 1572872 | tf_op jit(solution)/shard_map/ppermute | solution.py:250
  373.7 25.9 %collective-permute-start.48 = (bf16[2,128,1024]{2,1,0:T(8,128)(2,1)}, bf16[2,128,1024]{2,1,0:T(8,128)(2,1)}, u32[]{:S(2)}, u32[]{:S(2)}) collective-permute-start(bf16[2,128,1024]{2,1,0:T(8,128)(2,1)} %get-tuple-element.249), channel_id=1, source_target_pairs={{8,0},{12,4},{16,8},{20,12},{24,16},{28,20},{9,1},{13,5},{17,9},{2... | collective-permute-start | bytes 1572872 | tf_op jit(solution)/shard_map/ppermute | solution.py:250
  386.2 25.3 %collective-permute-start.42 = (bf16[2,128,1024]{2,1,0:T(8,128)(2,1)S(1)}, bf16[2,128,1024]{2,1,0:T(8,128)(2,1)S(1)}, u32[]{:S(2)}, u32[]{:S(2)}) collective-permute-start(bf16[2,128,1024]{2,1,0:T(8,128)(2,1)S(1)} %get-tuple-element.252), channel_id=1, source_target_pairs={{0,8},{4,12},{8,16},{12,20},{16,24},{20,28},{1,9},{5,13},{9,17},{1... | collective-permute-start | bytes 1572872 | tf_op jit(solution)/shard_map/ppermute | solution.py:250
  418.9 98.2 %collective-permute-start.52 = (bf16[4,128,1024]{2,1,0:T(8,128)(2,1)S(1)}, bf16[4,128,1024]{2,1,0:T(8,128)(2,1)}, u32[]{:S(2)}, u32[]{:S(2)}) collective-permute-start(bf16[4,128,1024]{2,1,0:T(8,128)(2,1)S(1)} %pad_maximum_fusion.8), channel_id=1, source_target_pairs={{0,4},{4,0},{8,12},{12,8},{16,20},{20,16},{24,28},{28,24},{1,5},{5... | collective-permute-start | bytes 3145736 | tf_op jit(solution)/shard_map/ppermute | solution.py:250
  488.0 29.1 %collective-permute-start.53 = (bf16[4,128,1024]{2,1,0:T(8,128)(2,1)S(1)}, bf16[4,128,1024]{2,1,0:T(8,128)(2,1)S(1)}, u32[]{:S(2)}, u32[]{:S(2)}) collective-permute-start(bf16[4,128,1024]{2,1,0:T(8,128)(2,1)S(1)} %pad_maximum_fusion.9), channel_id=1, source_target_pairs={{0,4},{4,0},{8,12},{12,8},{16,20},{20,16},{24,28},{28,24},{1,5},{5... | collective-permute-start | bytes 3145736 | tf_op jit(solution)/shard_map/ppermute | solution.py:250
  515.9 24.1 %collective-permute-start.62 = (bf16[4,128,1024]{2,1,0:T(8,128)(2,1)}, bf16[4,128,1024]{2,1,0:T(8,128)(2,1)}, u32[]{:S(2)}, u32[]{:S(2)}) collective-permute-start(bf16[4,128,1024]{2,1,0:T(8,128)(2,1)} %pad_maximum_fusion.12), channel_id=1, source_target_pairs={{0,4},{4,0},{8,12},{12,8},{16,20},{20,16},{24,28},{28,24},{1,5},{5... | collective-permute-start | bytes 3145736 | tf_op jit(solution)/shard_map/ppermute | solution.py:250
  (178 other events, 1811.6 us)

commit v2 on v1

v2 whole, which is shorter than its diff:
```python
import functools

import jax
import jax.numpy as jnp
from jax import lax
from jax.experimental import pallas as pl
from jax.experimental.pallas import tpu as pltpu
from jax.sharding import PartitionSpec as P

mu_outer = 0.9
eta_outer = 0.7
lr_inner = 2.0

STREAMS = 2
FOLD = 2


def contract(left, right, left_dim, right_dim):
    return lax.dot_general(
        left, right, (((left_dim,), (right_dim,)), ((), ())), preferred_element_type=jnp.float32
    )


def params(mib):
    return pltpu.CompilerParams(vmem_limit_bytes=mib * 2**20)


def spread(position, left, right_ref, chunks):
    size = left.shape[1] // chunks
    total = None
    for j in range(chunks):
        value = contract(left[:, j * size : (j + 1) * size], right_ref[position(j)], 1, 1)
        total = value if total is None else total + value
    return total


def open_kernel(scale, chunks, order_ref, x_ref, gate_w_ref, up_w_ref, gate_ref, up_ref, hidden_ref):
    position = lambda j: order_ref[j]
    gate = spread(position, gate_w_ref[0, 0], x_ref, chunks) * scale
    upper = spread(position, up_w_ref[0, 0], x_ref, chunks) * scale
    gate_ref[...] = gate
    up_ref[...] = upper
    hidden_ref[...] = (gate * jax.nn.sigmoid(gate) * upper).astype(jnp.bfloat16)


def close_kernel(scale, chunks, order_ref, c_ref, weight_ref, gate_ref, up_ref, pre_gate_ref, pre_up_ref):
    grad = spread(lambda j: order_ref[j], weight_ref[0, 0], c_ref, chunks) * scale
    gate, upper = gate_ref[...], up_ref[...]
    sig = jax.nn.sigmoid(gate)
    act = gate * sig
    pre_gate_ref[...] = (grad * upper * sig * (1.0 + gate * (1.0 - sig))).astype(jnp.bfloat16)
    pre_up_ref[...] = (grad * act).astype(jnp.bfloat16)


def front(kernel, scale, order, right, weights, picked, extra, dtypes):
    chunks, rows, size = right.shape
    units, width = weights.shape[2:]
    tile = min(256, units)
    thin = pl.BlockSpec((tile, rows), lambda i, order: (i, 0))
    return pl.pallas_call(
        functools.partial(kernel, scale, chunks),
        grid_spec=pltpu.PrefetchScalarGridSpec(
            num_scalar_prefetch=1,
            grid=(units // tile,),
            in_specs=[pl.BlockSpec((chunks, rows, size), lambda i, order: (0, 0, 0))]
            + [
                pl.BlockSpec((1, 1, tile, width), lambda i, order, level=level: (0, level, i, 0))
                for level in picked
            ]
            + [thin] * len(extra),
            out_specs=[thin] * len(dtypes),
        ),
        out_shape=[jax.ShapeDtypeStruct((units, rows), dtype) for dtype in dtypes],
        compiler_params=params(32),
        cost_estimate=pl.CostEstimate(
            flops=2 * len(picked) * rows * width * units,
            bytes_accessed=2 * len(picked) * units * width,
            transcendentals=units * rows,
        ),
    )(order, right, *[weights] * len(picked), *extra)


def finals_kernel(scale, block, pieces, table_ref, left_ref, right_ref, weight_ref, *refs):
    own_ref, send_ref = refs[-2:]
    grad = contract(left_ref[...], right_ref[0], 1, 0) * (lr_inner * scale)
    for q in range(pieces):
        rows = slice(q * block, (q + 1) * block)
        final = weight_ref[0, 0, rows, :].astype(jnp.float32) - grad[rows]
        spot = table_ref[1, q]

        @pl.when(table_ref[0, q] == 0)
        def _():
            own_ref[spot] = final

        @pl.when(table_ref[0, q] != 0)
        def _():
            send_ref[spot] = final.astype(jnp.bfloat16)


def finals(table, order, left, right, weights, level, columns, scale, line, block, after):
    start, tiles, tile = columns
    units, rows = left.shape
    per = right.shape[2] // tile
    spec = pl.BlockSpec((line, block, tile), lambda t, table, order: (0, 0, t))
    width = tiles * tile
    shape = (line, block, width)

    def kernel(table_ref, order_ref, *refs):
        finals_kernel(scale, block, units // block, table_ref, *refs)

    return pl.pallas_call(
        kernel,
        grid_spec=pltpu.PrefetchScalarGridSpec(
            num_scalar_prefetch=2,
            grid=(tiles,),
            in_specs=[
                pl.BlockSpec((units, rows), lambda t, table, order: (0, 0)),
                pl.BlockSpec(
                    (1, rows, tile), lambda t, table, order: (order[start(t) // per], 0, start(t) % per)
                ),
                pl.BlockSpec((1, 1, units, tile), lambda t, table, order: (0, level, 0, start(t))),
            ]
            + [pl.BlockSpec(memory_space=pl.ANY)] * len(after),
            out_specs=[spec, spec],
        ),
        out_shape=[jax.ShapeDtypeStruct(shape, jnp.float32), jax.ShapeDtypeStruct(shape, jnp.bfloat16)],
        compiler_params=params(24),
        cost_estimate=pl.CostEstimate(
            flops=2 * rows * width * units, bytes_accessed=5 * units * width + 2 * units * rows, transcendentals=0
        ),
    )(table, order, left, right, weights, *after)


def places(line, step):
    ups = lambda at: jnp.clip(line - step + at[2], 0, line - 1)
    downs = lambda at: jnp.clip(at[2] - line + step, 0, line - 1)
    return ups, downs


def running_kernel(line, step, at_ref, *refs):
    own_refs, got_refs, flow_refs, out_refs = refs[:2], refs[2:4], refs[4:-2], refs[-2:]
    modules = out_refs[0].shape[0]
    z = at_ref[2]
    lives = (z < step, z >= line - step)
    for way in range(2):
        for m in range(modules):
            total = jnp.where(lives[way] & (at_ref[0] == m), own_refs[way][0], 0.0)
            total = total + jnp.where(
                lives[way] & (at_ref[1] == m), got_refs[way][0].astype(jnp.float32), 0.0
            )
            if flow_refs:
                total = total + flow_refs[way][m].astype(jnp.float32)
            out_refs[way][m] = total.astype(jnp.bfloat16)


def running(at, own, got, flow, modules, step):
    line, block, width = own.shape
    tile = min(512, width)
    ups, downs = places(line, step)
    one = [
        pl.BlockSpec((1, block, tile), lambda t, at, spot=spot: (spot(at), 0, t)) for spot in (ups, downs)
    ]
    wide = pl.BlockSpec((modules, block, tile), lambda t, at: (0, 0, t))
    return pl.pallas_call(
        functools.partial(running_kernel, line, step),
        grid_spec=pltpu.PrefetchScalarGridSpec(
            num_scalar_prefetch=1,
            grid=(width // tile,),
            in_specs=one + one + [wide] * len(flow),
            out_specs=[wide, wide],
        ),
        out_shape=[jax.ShapeDtypeStruct((modules, block, width), jnp.bfloat16)] * 2,
        compiler_params=params(12),
        cost_estimate=pl.CostEstimate(
            flops=12 * modules * block * width, bytes_accessed=20 * block * width, transcendentals=0
        ),
    )(at, own, own, got, got, *flow)


def update_kernel(count, at_ref, share_ref, own_ref, got_ref, up_ref, low_ref, stored_ref, old_ref, *refs):
    fresh_ref, whole_ref = refs[-2:]
    for m in range(count):
        total = jnp.where(at_ref[0] == m, own_ref[0], 0.0)
        total = total + jnp.where(at_ref[1] == m, got_ref[0].astype(jnp.float32), 0.0)
        total = total + up_ref[m].astype(jnp.float32) + low_ref[m].astype(jnp.float32)
        stored = stored_ref[0, 0, m, 0]
        delta = stored - total / share_ref[m]
        velocity = mu_outer * old_ref[0, 0, m, 0].astype(jnp.float32) + delta
        fresh = (stored - eta_outer * (delta + mu_outer * velocity)).astype(jnp.bfloat16)
        fresh_ref[m] = fresh
        whole_ref[0, 0, m, 0] = fresh


def update(at, share, own, got, flow, outer_weights, momentum, whole, level, columns, after):
    start, tiles, tile = columns
    modules, block = outer_weights.shape[2], outer_weights.shape[4]
    one = pl.BlockSpec((1, block, tile), lambda t, at: (at[2], 0, t))
    wide = pl.BlockSpec((modules, block, tile), lambda t, at: (0, 0, t))
    state = pl.BlockSpec((1, 1, modules, 1, block, tile), lambda t, at: (0, level, 0, 0, 0, start(t)))
    extra = ([] if whole is None else [whole]) + after
    return pl.pallas_call(
        functools.partial(update_kernel, modules),
        grid_spec=pltpu.PrefetchScalarGridSpec(
            num_scalar_prefetch=1,
            grid=(tiles,),
            in_specs=[pl.BlockSpec(memory_space=pltpu.SMEM), one, one, wide, wide, state, state]
            + [pl.BlockSpec(memory_space=pl.ANY)] * len(extra),
            out_specs=[wide, state],
        ),
        out_shape=[
            jax.ShapeDtypeStruct((modules, block, tiles * tile), jnp.bfloat16),
            jax.ShapeDtypeStruct(outer_weights.shape, jnp.bfloat16),
        ],
        input_output_aliases={} if whole is None else {8: 1},
        compiler_params=params(16),
        cost_estimate=pl.CostEstimate(
            flops=12 * modules * block * tiles * tile,
            bytes_accessed=16 * modules * block * tiles * tile,
            transcendentals=0,
        ),
    )(at, share, own, got, *flow, outer_weights, momentum, *extra)


def deliver_kernel(line, at_ref, fresh_ref, *refs):
    ups, lows = refs[: line - 1], refs[line - 1 : 2 * line - 2]
    near_ref, far_ref, sems = refs[-3:]
    z = at_ref[2]
    for side, out_ref in enumerate((near_ref, far_ref)):
        module = at_ref[side]

        def copy(source, r, side=side, out_ref=out_ref, module=module):
            return pltpu.make_async_copy(source.at[module], out_ref.at[r], sems.at[side, r])

        copy(fresh_ref, 0).start()
        for r in range(1, line):

            @pl.when(z >= r)
            def _():
                copy(ups[r - 1], r).start()

            @pl.when(z < r)
            def _():
                copy(lows[line - 1 - r], r).start()

    for side, out_ref in enumerate((near_ref, far_ref)):
        for r in range(line):
            pltpu.make_async_copy(fresh_ref.at[0], out_ref.at[r], sems.at[side, r]).wait()


def deliver(at, fresh, ups, lows, after):
    line = len(ups) + 1
    shape = jax.ShapeDtypeStruct((line,) + fresh.shape[1:], fresh.dtype)
    anywhere = pl.BlockSpec(memory_space=pl.ANY)
    return pl.pallas_call(
        functools.partial(deliver_kernel, line),
        in_specs=[pl.BlockSpec(memory_space=pltpu.SMEM)] + [anywhere] * (2 * line - 1 + len(after)),
        out_specs=[pl.BlockSpec(memory_space=pltpu.VMEM)] * 2,
        out_shape=[shape, shape],
        scratch_shapes=[pltpu.SemaphoreType.DMA((2, line))],
        compiler_params=params(12),
        cost_estimate=pl.CostEstimate(
            flops=0, bytes_accessed=4 * shape.size * 2, transcendentals=0
        ),
    )(at, fresh, *ups, *lows, *after)


def product(order_ref, x_ref, parts):
    total = None
    size = x_ref.shape[2]
    at = 0
    for part in parts:
        for i in range(part.shape[2] // size):
            left = part[:, :, i * size : (i + 1) * size].reshape(-1, size)
            value = contract(left, x_ref[order_ref[at]], 1, 1)
            total = value if total is None else total + value
            at += 1
    return total


def gate_kernel(scale, block, line, order_ref, table_ref, x_ref, *refs):
    out_ref = refs[-1]
    count = (len(refs) - 1) // 2
    for side, parts in enumerate((refs[:count], refs[count:-1])):
        value = product(order_ref, x_ref, parts) * scale
        for r in range(line):
            out_ref[table_ref[0, side * line + r]] = value[r * block : (r + 1) * block]


def hidden_kernel(scale, block, line, order_ref, table_ref, x_ref, gate_ref, *refs):
    out_ref = refs[-1]
    count = (len(refs) - 1) // 2
    for side, parts in enumerate((refs[:count], refs[count:-1])):
        value = product(order_ref, x_ref, parts) * scale
        for r in range(line):
            gate = gate_ref[table_ref[0, side * line + r]]
            upper = value[r * block : (r + 1) * block]
            hidden = gate * jax.nn.sigmoid(gate) * upper
            out_ref[table_ref[1, side * line + r]] = hidden.astype(jnp.bfloat16)


def forward(kernel, order, table, inputs, extra, parts, dtype, scale, line, block):
    chunks, rows, size = inputs.shape
    pieces = 2 * line
    smem = pl.BlockSpec(memory_space=pltpu.SMEM)
    vmem = pl.BlockSpec(memory_space=pltpu.VMEM)
    return pl.pallas_call(
        functools.partial(kernel, scale, block, line),
        in_specs=[smem, smem] + [vmem] * (1 + len(extra) + len(parts)),
        out_specs=vmem,
        out_shape=jax.ShapeDtypeStruct((pieces, block, rows), dtype),
        compiler_params=params(32),
        cost_estimate=pl.CostEstimate(
            flops=2 * rows * chunks * size * pieces * block,
            bytes_accessed=2 * chunks * size * pieces * block,
            transcendentals=0,
        ),
    )(order, table, inputs, *extra, *parts)


def down_kernel(scale, left_ref, near_ref, far_ref, out_ref):
    line, block, width = near_ref.shape
    rows = left_ref.shape[2]
    near_left = left_ref[:line].reshape(line * block, rows)
    far_left = left_ref[line:].reshape(line * block, rows)
    total = contract(near_left, near_ref[...].reshape(-1, width), 0, 0)
    total = total + contract(far_left, far_ref[...].reshape(-1, width), 0, 0)
    out_ref[...] = total * scale


def down(left, near, far, scale):
    pieces, block, rows = left.shape
    width = near.shape[2]
    vmem = pl.BlockSpec(memory_space=pltpu.VMEM)
    return pl.pallas_call(
        functools.partial(down_kernel, scale),
        in_specs=[vmem] * 3,
        out_specs=vmem,
        out_shape=jax.ShapeDtypeStruct((rows, width), jnp.float32),
        compiler_params=params(24),
        cost_estimate=pl.CostEstimate(
            flops=2 * rows * width * pieces * block,
            bytes_accessed=2 * pieces * block * width + 4 * rows * width,
            transcendentals=0,
        ),
    )(left, near, far)


def pairs_of(size, bit):
    return [(i, i ^ bit) for i in range(size)]


def gather_mp(values, size):
    held = [value[None] for value in values]
    offsets = [0]
    bit = size // 2
    while bit:
        held = [jnp.concatenate([part, lax.ppermute(part, "mp", pairs_of(size, bit))], axis=0) for part in held]
        offsets = offsets + [offset ^ bit for offset in offsets]
        bit //= 2
    return held, offsets


def scatter_mp(value, size, index):
    width = value.shape[1] // size
    parts = [value[:, i * width : (i + 1) * width] for i in range(size)]
    bit = 1
    while bit < size:
        high = (index & bit) != 0
        keep = [jnp.where(high, parts[i + 1], parts[i]) for i in range(0, len(parts), 2)]
        sent = [jnp.where(high, parts[i], parts[i + 1]) for i in range(0, len(parts), 2)]
        got = lax.ppermute(jnp.concatenate(sent, axis=1), "mp", pairs_of(size, bit))
        parts = [part + got[:, i * width : (i + 1) * width] for i, part in enumerate(keep)]
        bit *= 2
    return parts[0]


def shards(tokens, cotangent, path_weights, outer_weights, momentum, assignment, owners):
    paths = lax.axis_size("path")
    ranks = lax.axis_size("mp")
    line = paths // FOLD
    me = lax.axis_index("path")
    rank = lax.axis_index("mp")
    z, side = me // FOLD, me % FOLD
    levels, units, width = path_weights.shape[1:]
    modules, block = outer_weights.shape[2], outer_weights.shape[4]
    scale_d = width ** (-0.5)
    scale_f = (units * ranks) ** (-0.5)

    (inputs, upstream), offsets = gather_mp([tokens, cotangent], ranks)
    spots = jnp.asarray([offsets.index(i) for i in range(ranks)], jnp.int32)
    rank_ids = jnp.arange(ranks, dtype=jnp.int32)
    order = jnp.sum(jnp.where((rank_ids ^ rank)[:, None] == rank_ids[None, :], spots[None, :], 0), axis=1)

    module_ids = jnp.arange(modules, dtype=jnp.int32)
    path_ids = jnp.arange(paths, dtype=jnp.int32)
    mine = lax.dynamic_index_in_dim(assignment, me, 1, keepdims=False)
    theirs = lax.dynamic_index_in_dim(assignment, me ^ 1, 1, keepdims=False)
    at_all = jnp.stack([mine, theirs, jnp.full_like(mine, z)], axis=1)
    is_mine = mine[:, None] == module_ids[None, :]
    shares = jnp.sum((assignment[:, None, :] == module_ids[None, :, None]).astype(jnp.float32), axis=2)
    owner_rows = jnp.sum(jnp.where(is_mine[:, :, None], owners, 0), axis=1)
    apart = (owner_rows % FOLD) ^ side
    leaves = jnp.stack([apart, owner_rows // FOLD], axis=1)
    slot = apart * line + (z - owner_rows // FOLD + line) % line
    piece_at = jnp.sum(
        jnp.where(slot[:, None, :] == path_ids[None, :, None], path_ids[None, None, :], 0), axis=2
    )
    down_at = jnp.sum(
        jnp.where(piece_at[1][:, None] == path_ids[None, :], slot[2][None, :], 0), axis=1
    )
    gate_table = piece_at[0][None]
    hidden_table = jnp.stack([piece_at[1], down_at])

    across = pairs_of(paths, 1)

    def permute(value, pairs):
        return lax.ppermute(value, "path", pairs)

    def along(values, first, last):
        up = [(i, i + FOLD) for i in range(paths - FOLD) if first <= i // FOLD <= last]
        low = [(paths - 1 - i, paths - 1 - j) for i, j in up]
        return [permute(values[0], up), permute(values[1], low)]

    half = width // STREAMS
    chunk = width // ranks
    narrow = chunk // STREAMS

    def columns(level, s):
        if level == 2:
            return (lambda t: t * STREAMS + s), ranks, narrow
        tile = min(chunk, half)
        return (lambda t: s * (half // tile) + t), half // tile, tile

    gate, upper, hidden = front(
        open_kernel, scale_d, order, inputs, path_weights, (0, 1), (), (jnp.float32, jnp.float32, jnp.bfloat16)
    )
    pre_gate, pre_up = front(
        close_kernel, scale_f, order, upstream, path_weights, (2,), (gate, upper), (jnp.bfloat16, jnp.bfloat16)
    )
    sources = ((pre_gate, inputs, scale_d), (pre_up, inputs, scale_d), (hidden, upstream, scale_f))

    flow = [[] for _ in range(STREAMS)]
    first = [[] for _ in range(STREAMS)]
    waiting = [None] * STREAMS
    near = [[None] * STREAMS for _ in range(levels)]
    far = [[None] * STREAMS for _ in range(levels)]
    whole = None
    hidden_new = gate_new = None

    def give(level, s):
        near[level][s], leaving = deliver(at_all[level], *waiting[s], [hidden_new] if level == 2 else [])
        far[level][s] = permute(leaving, across)

    outs = []
    for level in range(levels + 1):
        own, got = [None] * STREAMS, [None] * STREAMS
        if level < levels:
            left, right, scale = sources[level]
            for s in range(STREAMS):
                own[s], send = finals(
                    leaves[level], order, left, right, path_weights, level, columns(level, s), scale, line, block, first[s]
                )
                got[s] = permute(send, across)
        for step in range(1, line):
            for s in range(STREAMS):
                if level < levels:
                    value = running(at_all[level], own[s], got[s], flow[s], modules, step)
                    flow[s] = along(value, 0, step - 1 if level == 0 else line)
                elif step < line - 1:
                    flow[s] = along(flow[s], step, line)
                if step == 1:
                    first[s] = flow[s][:1]
                if waiting[s] is not None:
                    if step < line - 1:
                        waiting[s][1].append(flow[s][0])
                        waiting[s][2].append(flow[s][1])
                    if step == max(line - 2, 1):
                        give(level - 1, s)
        if level < levels:
            for s in range(STREAMS):
                after = [near[level - 1][s]] if level else []
                if level == 2:
                    after.append(gate_new)
                fresh, whole = update(
                    at_all[level], shares[level], own[s], got[s], flow[s], outer_weights, momentum, whole, level,
                    columns(level, s), after,
                )
                flow[s] = along((fresh, fresh), 0, line)
                waiting[s] = (fresh, [flow[s][0]], [flow[s][1]])
        if level == 1:
            gate_new = forward(
                gate_kernel, order, gate_table, inputs, (), near[0] + far[0], jnp.float32, scale_d, line, block
            )
        if level == 2:
            hidden_new = forward(
                hidden_kernel, order, hidden_table, inputs, (gate_new,), near[1] + far[1], jnp.bfloat16, scale_d,
                line, block,
            )
        if level == 3:
            for s in range(STREAMS):
                outs.append(scatter_mp(down(hidden_new, near[2][s], far[2][s], scale_f), ranks, rank))

    outputs = jnp.concatenate(outs, axis=1).astype(jnp.bfloat16)
    return outputs, whole


def solution(mesh):
    return jax.shard_map(
        shards,
        mesh=mesh,
        in_specs=(
            P("path", "mp"),
            P("path", "mp"),
            P("path", None, "mp", None),
            P("path", None, None, "mp", None, None),
            P("path", None, None, "mp", None, None),
            P(),
            P(),
        ),
        out_specs=(P("path", "mp"), P("path", None, None, "mp", None, None)),
        check_vma=False,
    )
```

time: 580 us -> 469 us (0.81); the launches traced: 569 us -> 467 us
  other arithmetic: 64.8 us -> 8.2 us
  Pallas kernels: 67.5 us -> 93.9 us
  starting transfers between devices: 179 us -> 154 us
  local copies, waits for them, and re-layouts: 44.3 us -> 20.4 us
  between operations: 14.3 us -> 2.17 us
  waiting for transfers between devices: 199 us -> 188 us
    ppermute x68, waiting for transfers between devices: 184 us -> 157 us  [permute(): return lax.ppermute(value, 'path', pairs)]
    pallas_call x11 -> x42, Pallas kernels: 67.5 us -> 93.9 us  [the longest x18 28.5 us: running(): pl.pallas_call(functools.partial(running_kernel, line, step), grid_spec=p...]
    ppermute x68, starting transfers between devices: 174 us -> 148 us  [permute(): return lax.ppermute(value, 'path', pairs)]
    convert_element_type x22 -> x0, other arithmetic: 19.6 us -> none  [the longest x18 15.7 us: round_(): value = value.astype(jnp.bfloat16)]
    ppermute x4, waiting for transfers between devices: 0.01 us -> 15.4 us  [gather_mp(): lax.ppermute(part, 'mp', pairs_of(size, bit))]
    another operation x16 -> x3, other arithmetic: 11.8 us -> 0.26 us  [the longest x12 10.5 us: deliver(): jnp.stack([lax.dynamic_index_in_dim(a, m, 0, keepdims=False) for a in ring])]
    dynamic_slice x25 -> x1, local copies, waits for them, and re-layouts: 9.09 us -> 0.94 us  [shards(): mine = lax.dynamic_index_in_dim(assignment, me, 1, keepdims=False)]
    squeeze x4 -> x2, local copies, waits for them, and re-layouts: 8.04 us -> 0.01 us  [the longest x1 0.01 us: shards(): value = running(at_all[level], own[s], got[s], flow[s], modules, step)]
  transfers between devices with their start and end apart: 76 -> 76, of which waited for: 40 -> 37; matrix products, arithmetic and copies ran while one was open for 16% -> 1% of each run, Pallas kernels for 9% -> 18%
where the time goes in v2:
time: 469 us; the launch traced here: 467 us
  waiting for transfers between devices  188 us (40%)
  starting transfers between devices  154 us (33%)
  Pallas kernels  93.9 us (20%)
  local copies, waits for them, and re-layouts  20.4 us (4%)
  other arithmetic  8.2 us (2%)
    ppermute x68, waiting for transfers between devices, permute(): return lax.ppermute(value, 'path', pairs)  157 us
    ppermute x68, starting transfers between devices, permute(): return lax.ppermute(value, 'path', pairs)  148 us
    pallas_call x18, Pallas kernels, running(): pl.pallas_call(functools.partial(running_kernel, line, step), grid_spec=p...  28.5 us
    pallas_call x6, Pallas kernels, finals(): pl.pallas_call(kernel, grid_spec=pltpu.PrefetchScalarGridSpec(num_scalar_...  22.4 us
    unnamed x140, local copies, waits for them, and re-layouts  19.3 us
    pallas_call x6, Pallas kernels, update(): pl.pallas_call(functools.partial(update_kernel, modules), grid_spec=pltpu...  17.7 us
    ppermute x4, waiting for transfers between devices, scatter_mp(): got = lax.ppermute(jnp.concatenate(sent, axis=1), 'mp', pairs_of(size, bit))  16.1 us
    ppermute x4, waiting for transfers between devices, gather_mp(): lax.ppermute(part, 'mp', pairs_of(size, bit))  15.4 us
  transfers between devices with their start and end apart: 76, of which 37 were waited for; matrix products, arithmetic and copies ran while one was open for 1% of the time, Pallas kernels for 18%

profile of v2, /device:TPU:0, one launch (start us, length us, event | category | flops | bytes accessed | tf_op | source)
XLA Modules:
  0.0 467.1 jit_solution(11733203149301431141)
XLA Ops:
  4.8 9.1 %collective-permute-done = bf16[1,384,512]{2,1,0:T(8,128)(2,1)S(1)} collective-permute-done((bf16[1,384,512]{2,1,0:T(8,128)(2,1)}, bf16[1,384,512]{2,1,0:T(8,128)(2,1)S(1)}, u32[]{:S(2)}, u32[]{:S(2)}) %collective-permute-start) | collective-permute-done | bytes 393248 | tf_op jit(solution)/shard_map/ppermute | solution.py:357
  15.1 6.3 %collective-permute-done.2 = bf16[1,384,512]{2,1,0:T(8,128)(2,1)S(1)} collective-permute-done((bf16[1,384,512]{2,1,0:T(8,128)(2,1)}, bf16[1,384,512]{2,1,0:T(8,128)(2,1)S(1)}, u32[]{:S(2)}, u32[]{:S(2)}) %collective-permute-start.2) | collective-permute-done | bytes 393248 | tf_op jit(solution)/shard_map/ppermute | solution.py:357
  26.9 5.6 %shard_map.95 = (f32[1024,384]{1,0:T(8,128)S(1)}, f32[1024,384]{1,0:T(8,128)S(1)}, bf16[1024,384]{1,0:T(8,128)(2,1)S(1)}) custom-call(s32[4]{0:T(128)S(1)} %select_reduce_fusion.3.order_ref, bf16[4,384,512]{2,1,0:T(8,128)(2,1)S(1)} %pad_maximum_fusion.x_ref.refs_1_, bf16[1,3,1024,2048]{3,2,1,0:T(8,128)(2,1)S(1)} %copy-done, ...), custom_call_target="tpu_custom_call" | custom-call | flops 3221225472 | bytes 8388608 | tf_op jit(solution)/shard_map/pallas_call | solution.py:60
  53.9 19.0 %collective-permute-done.4.refs_2_.refs_3_.got_ref = bf16[4,128,1024]{2,1,0:T(8,128)(2,1)} collective-permute-done((bf16[4,128,1024]{2,1,0:T(8,128)(2,1)}, bf16[4,128,1024]{2,1,0:T(8,128)(2,1)}, u32[]{:S(2)}, u32[]{:S(2)}) %collective-permute-start.4) | collective-permute-done | bytes 1048608 | tf_op jit(solution)/shard_map/ppermute | solution.py:417
  81.0 13.4 %collective-permute-done.18.refs_2_.refs_3_.got_ref = bf16[4,128,1024]{2,1,0:T(8,128)(2,1)S(1)} collective-permute-done((bf16[4,128,1024]{2,1,0:T(8,128)(2,1)}, bf16[4,128,1024]{2,1,0:T(8,128)(2,1)S(1)}, u32[]{:S(2)}, u32[]{:S(2)}) %collective-permute-start.18) | collective-permute-done | bytes 1048608 | tf_op jit(solution)/shard_map/ppermute | solution.py:417
  104.9 7.1 %collective-permute-done.19.refs_4_.refs_3_ = bf16[2,128,1024]{2,1,0:T(8,128)(2,1)S(1)} collective-permute-done((bf16[2,128,1024]{2,1,0:T(8,128)(2,1)S(1)}, bf16[2,128,1024]{2,1,0:T(8,128)(2,1)S(1)}, u32[]{:S(2)}, u32[]{:S(2)}) %collective-permute-start.19) | collective-permute-done | bytes 524320 | tf_op jit(solution)/shard_map/ppermute | solution.py:417
  118.7 4.6 collective-permute-done.7.refs_4_
  138.0 4.9 %collective-permute-start.23 = (bf16[2,128,1024]{2,1,0:T(8,128)(2,1)S(1)}, bf16[2,128,1024]{2,1,0:T(8,128)(2,1)S(1)}, u32[]{:S(2)}, u32[]{:S(2)}) collective-permute-start(bf16[2,128,1024]{2,1,0:T(8,128)(2,1)S(1)} %get-tuple-element.105), channel_id=1, source_target_pairs={{0,8},{4,12},{8,16},{12,20},{16,24},{20,28},{1,9},{5,13},{9,17},{1... | collective-permute-start | bytes 1572872 | tf_op jit(solution)/shard_map/ppermute | solution.py:417
  179.3 4.7 %collective-permute-done.27.refs_5_.refs_3_ = bf16[2,128,1024]{2,1,0:T(8,128)(2,1)S(1)} collective-permute-done((bf16[2,128,1024]{2,1,0:T(8,128)(2,1)S(1)}, bf16[2,128,1024]{2,1,0:T(8,128)(2,1)S(1)}, u32[]{:S(2)}, u32[]{:S(2)}) %collective-permute-start.27) | collective-permute-done | bytes 524320 | tf_op jit(solution)/shard_map/ppermute | solution.py:417
  219.8 4.6 collective-permute-start.34
  233.6 5.6 %collective-permute-start.43 = (bf16[2,128,1024]{2,1,0:T(8,128)(2,1)}, bf16[2,128,1024]{2,1,0:T(8,128)(2,1)}, u32[]{:S(2)}, u32[]{:S(2)}) collective-permute-start(bf16[2,128,1024]{2,1,0:T(8,128)(2,1)} %get-tuple-element.130), channel_id=1, source_target_pairs={{0,8},{4,12},{8,16},{12,20},{16,24},{20,28},{1,9},{5,13},{9,17},{1... | collective-permute-start | bytes 1572872 | tf_op jit(solution)/shard_map/ppermute | solution.py:417
  252.9 5.2 %collective-permute-start.36 = (bf16[2,128,1024]{2,1,0:T(8,128)(2,1)S(1)}, bf16[2,128,1024]{2,1,0:T(8,128)(2,1)S(1)}, u32[]{:S(2)}, u32[]{:S(2)}) collective-permute-start(bf16[2,128,1024]{2,1,0:T(8,128)(2,1)S(1)} %get-tuple-element.121.fresh_ref), channel_id=1, source_target_pairs={{0,8},{4,12},{8,16},{12,20},{16,24},{20,28},{1,9},{5,13},{9,17},{1... | collective-permute-start | bytes 1572872 | tf_op jit(solution)/shard_map/ppermute | solution.py:417
  258.9 4.9 %collective-permute-done.44.low_ref = bf16[2,128,1024]{2,1,0:T(8,128)(2,1)S(1)} collective-permute-done((bf16[2,128,1024]{2,1,0:T(8,128)(2,1)S(1)}, bf16[2,128,1024]{2,1,0:T(8,128)(2,1)S(1)}, u32[]{:S(2)}, u32[]{:S(2)}) %collective-permute-start.44) | collective-permute-done | bytes 524320 | tf_op jit(solution)/shard_map/ppermute | solution.py:417
  279.2 7.1 %collective-permute-done.47.refs_5_.refs_3_ = bf16[2,128,1024]{2,1,0:T(8,128)(2,1)S(1)} collective-permute-done((bf16[2,128,1024]{2,1,0:T(8,128)(2,1)S(1)}, bf16[2,128,1024]{2,1,0:T(8,128)(2,1)S(1)}, u32[]{:S(2)}, u32[]{:S(2)}) %collective-permute-start.47) | collective-permute-done | bytes 524320 | tf_op jit(solution)/shard_map/ppermute | solution.py:417
  310.1 5.0 %collective-permute-start.50 = (bf16[2,128,1024]{2,1,0:T(8,128)(2,1)S(1)}, bf16[2,128,1024]{2,1,0:T(8,128)(2,1)S(1)}, u32[]{:S(2)}, u32[]{:S(2)}) collective-permute-start(bf16[2,128,1024]{2,1,0:T(8,128)(2,1)S(1)} %get-tuple-element.138), channel_id=1, source_target_pairs={{0,8},{4,12},{8,16},{12,20},{16,24},{20,28},{1,9},{5,13},{9,17},{1... | collective-permute-start | bytes 1572872 | tf_op jit(solution)/shard_map/ppermute | solution.py:417
  321.3 5.0 %collective-permute-start.54 = (bf16[2,128,1024]{2,1,0:T(8,128)(2,1)S(1)}, bf16[2,128,1024]{2,1,0:T(8,128)(2,1)S(1)}, u32[]{:S(2)}, u32[]{:S(2)}) collective-permute-start(bf16[2,128,1024]{2,1,0:T(8,128)(2,1)S(1)} %get-tuple-element.143), channel_id=1, source_target_pairs={{0,8},{4,12},{8,16},{12,20},{16,24},{20,28},{1,9},{5,13},{9,17},{1... | collective-permute-start | bytes 1572872 | tf_op jit(solution)/shard_map/ppermute | solution.py:417
  334.8 4.7 %collective-permute-start.65 = (bf16[2,128,1024]{2,1,0:T(8,128)(2,1)S(1)}, bf16[2,128,1024]{2,1,0:T(8,128)(2,1)S(1)}, u32[]{:S(2)}, u32[]{:S(2)}) collective-permute-start(bf16[2,128,1024]{2,1,0:T(8,128)(2,1)S(1)} %get-tuple-element.149), channel_id=1, source_target_pairs={{0,8},{4,12},{8,16},{12,20},{16,24},{20,28},{1,9},{5,13},{9,17},{1... | collective-permute-start | bytes 1572872 | tf_op jit(solution)/shard_map/ppermute | solution.py:417
  339.6 8.0 %collective-permute-done.33.refs_3_ = bf16[4,128,1024]{2,1,0:T(8,128)(2,1)S(1)} collective-permute-done((bf16[4,128,1024]{2,1,0:T(8,128)(2,1)S(1)}, bf16[4,128,1024]{2,1,0:T(8,128)(2,1)S(1)}, u32[]{:S(2)}, u32[]{:S(2)}) %collective-permute-start.33) | collective-permute-done | bytes 1048608 | tf_op jit(solution)/shard_map/ppermute | solution.py:417
  356.7 7.6 %collective-permute-done.66.low_ref = bf16[2,128,1024]{2,1,0:T(8,128)(2,1)S(1)} collective-permute-done((bf16[2,128,1024]{2,1,0:T(8,128)(2,1)S(1)}, bf16[2,128,1024]{2,1,0:T(8,128)(2,1)S(1)}, u32[]{:S(2)}, u32[]{:S(2)}) %collective-permute-start.66) | collective-permute-done | bytes 524320 | tf_op jit(solution)/shard_map/ppermute | solution.py:417
  386.2 9.2 %collective-permute-done.59.refs_3_ = bf16[2,128,1024]{2,1,0:T(8,128)(2,1)S(1)} collective-permute-done((bf16[2,128,1024]{2,1,0:T(8,128)(2,1)S(1)}, bf16[2,128,1024]{2,1,0:T(8,128)(2,1)S(1)}, u32[]{:S(2)}, u32[]{:S(2)}) %collective-permute-start.59) | collective-permute-done | bytes 524320 | tf_op jit(solution)/shard_map/ppermute | solution.py:417
  422.2 7.8 %collective-permute-done.73.far_ref = bf16[4,128,1024]{2,1,0:T(8,128)(2,1)S(1)} collective-permute-done((bf16[4,128,1024]{2,1,0:T(8,128)(2,1)}, bf16[4,128,1024]{2,1,0:T(8,128)(2,1)S(1)}, u32[]{:S(2)}, u32[]{:S(2)}) %collective-permute-start.73) | collective-permute-done | bytes 1048608 | tf_op jit(solution)/shard_map/ppermute | solution.py:417
  433.6 7.8 %collective-permute-done.62.far_ref = bf16[4,128,1024]{2,1,0:T(8,128)(2,1)} collective-permute-done((bf16[4,128,1024]{2,1,0:T(8,128)(2,1)}, bf16[4,128,1024]{2,1,0:T(8,128)(2,1)}, u32[]{:S(2)}, u32[]{:S(2)}) %collective-permute-start.62) | collective-permute-done | bytes 1048608 | tf_op jit(solution)/shard_map/ppermute | solution.py:417
  450.1 8.1 %collective-permute-done.75 = f32[384,256]{1,0:T(8,128)S(1)} collective-permute-done((f32[384,256]{1,0:T(8,128)S(1)}, f32[384,256]{1,0:T(8,128)S(1)}, u32[]{:S(2)}, u32[]{:S(2)}) %collective-permute-start.75) | collective-permute-done | bytes 393248 | tf_op jit(solution)/shard_map/ppermute | solution.py:371
  458.2 8.0 %collective-permute-done.64 = f32[384,256]{1,0:T(8,128)S(1)} collective-permute-done((f32[384,256]{1,0:T(8,128)S(1)}, f32[384,256]{1,0:T(8,128)S(1)}, u32[]{:S(2)}, u32[]{:S(2)}) %collective-permute-start.64) | collective-permute-done | bytes 393248 | tf_op jit(solution)/shard_map/ppermute | solution.py:371
  (343 shorter events, 291.4 us)
Async XLA Ops:
  46.6 26.3 %collective-permute-start.4 = (bf16[4,128,1024]{2,1,0:T(8,128)(2,1)}, bf16[4,128,1024]{2,1,0:T(8,128)(2,1)}, u32[]{:S(2)}, u32[]{:S(2)}) collective-permute-start(bf16[4,128,1024]{2,1,0:T(8,128)(2,1)} %get-tuple-element.83), channel_id=1, source_target_pairs={{0,4},{4,0},{8,12},{12,8},{16,20},{20,16},{24,28},{28,24},{1,5},{5... | collective-permute-start | bytes 3145736 | tf_op jit(solution)/shard_map/ppermute | solution.py:417
  53.4 41.1 %collective-permute-start.18 = (bf16[4,128,1024]{2,1,0:T(8,128)(2,1)}, bf16[4,128,1024]{2,1,0:T(8,128)(2,1)S(1)}, u32[]{:S(2)}, u32[]{:S(2)}) collective-permute-start(bf16[4,128,1024]{2,1,0:T(8,128)(2,1)} %get-tuple-element.100), channel_id=1, source_target_pairs={{0,4},{4,0},{8,12},{12,8},{16,20},{20,16},{24,28},{28,24},{1,5},{5... | collective-permute-start | bytes 3145736 | tf_op jit(solution)/shard_map/ppermute | solution.py:417
  76.6 24.0 %collective-permute-start.5 = (bf16[2,128,1024]{2,1,0:T(8,128)(2,1)S(1)}, bf16[2,128,1024]{2,1,0:T(8,128)(2,1)S(1)}, u32[]{:S(2)}, u32[]{:S(2)}) collective-permute-start(bf16[2,128,1024]{2,1,0:T(8,128)(2,1)S(1)} %get-tuple-element.84), channel_id=1, source_target_pairs={{0,8},{4,12},{1,9},{5,13},{2,10},{6,14},{3,11},{7,15}} | collective-permute-start | bytes 1572872 | tf_op jit(solution)/shard_map/ppermute | solution.py:417
  102.7 20.6 %collective-permute-start.7 = (bf16[2,128,1024]{2,1,0:T(8,128)(2,1)S(1)}, bf16[2,128,1024]{2,1,0:T(8,128)(2,1)S(1)}, u32[]{:S(2)}, u32[]{:S(2)}) collective-permute-start(bf16[2,128,1024]{2,1,0:T(8,128)(2,1)S(1)} %get-tuple-element.86), channel_id=1, source_target_pairs={{0,8},{4,12},{8,16},{12,20},{1,9},{5,13},{9,17},{13,21},{2,10},{6,... | collective-permute-start | bytes 1572872 | tf_op jit(solution)/shard_map/ppermute | solution.py:417
  113.4 22.5 %collective-permute-start.21 = (bf16[2,128,1024]{2,1,0:T(8,128)(2,1)S(1)}, bf16[2,128,1024]{2,1,0:T(8,128)(2,1)S(1)}, u32[]{:S(2)}, u32[]{:S(2)}) collective-permute-start(bf16[2,128,1024]{2,1,0:T(8,128)(2,1)S(1)} %get-tuple-element.103), channel_id=1, source_target_pairs={{0,8},{4,12},{8,16},{12,20},{1,9},{5,13},{9,17},{13,21},{2,10},{6,... | collective-permute-start | bytes 1572872 | tf_op jit(solution)/shard_map/ppermute | solution.py:417
  125.4 22.2 %collective-permute-start.9 = (bf16[2,128,1024]{2,1,0:T(8,128)(2,1)S(1)}, bf16[2,128,1024]{2,1,0:T(8,128)(2,1)S(1)}, u32[]{:S(2)}, u32[]{:S(2)}) collective-permute-start(bf16[2,128,1024]{2,1,0:T(8,128)(2,1)S(1)} %get-tuple-element.88), channel_id=1, source_target_pairs={{0,8},{4,12},{8,16},{12,20},{16,24},{20,28},{1,9},{5,13},{9,17},{1... | collective-permute-start | bytes 1572872 | tf_op jit(solution)/shard_map/ppermute | solution.py:417
  132.9 32.6 %collective-permute-start.12 = (bf16[4,128,1024]{2,1,0:T(8,128)(2,1)S(1)}, bf16[4,128,1024]{2,1,0:T(8,128)(2,1)S(1)}, u32[]{:S(2)}, u32[]{:S(2)}) collective-permute-start(bf16[4,128,1024]{2,1,0:T(8,128)(2,1)S(1)} %get-tuple-element.93), channel_id=1, source_target_pairs={{0,4},{4,0},{8,12},{12,8},{16,20},{20,16},{24,28},{28,24},{1,5},{5... | collective-permute-start | bytes 3145736 | tf_op jit(solution)/shard_map/ppermute | solution.py:417
  147.7 31.6 %collective-permute-start.26 = (bf16[4,128,1024]{2,1,0:T(8,128)(2,1)S(1)}, bf16[4,128,1024]{2,1,0:T(8,128)(2,1)S(1)}, u32[]{:S(2)}, u32[]{:S(2)}) collective-permute-start(bf16[4,128,1024]{2,1,0:T(8,128)(2,1)S(1)} %get-tuple-element.110), channel_id=1, source_target_pairs={{0,4},{4,0},{8,12},{12,8},{16,20},{20,16},{24,28},{28,24},{1,5},{5... | collective-permute-start | bytes 3145736 | tf_op jit(solution)/shard_map/ppermute | solution.py:417
  207.8 23.7 %collective-permute-start.30 = (bf16[2,128,1024]{2,1,0:T(8,128)(2,1)S(1)}, bf16[2,128,1024]{2,1,0:T(8,128)(2,1)S(1)}, u32[]{:S(2)}, u32[]{:S(2)}) collective-permute-start(bf16[2,128,1024]{2,1,0:T(8,128)(2,1)S(1)} %get-tuple-element.113), channel_id=1, source_target_pairs={{0,8},{4,12},{8,16},{12,20},{16,24},{20,28},{1,9},{5,13},{9,17},{1... | collective-permute-start | bytes 1572872 | tf_op jit(solution)/shard_map/ppermute | solution.py:417
  219.8 27.1 %collective-permute-start.34 = (bf16[2,128,1024]{2,1,0:T(8,128)(2,1)}, bf16[2,128,1024]{2,1,0:T(8,128)(2,1)}, u32[]{:S(2)}, u32[]{:S(2)}) collective-permute-start(bf16[2,128,1024]{2,1,0:T(8,128)(2,1)} %get-tuple-element.118), channel_id=1, source_target_pairs={{0,8},{4,12},{8,16},{12,20},{16,24},{20,28},{1,9},{5,13},{9,17},{1... | collective-permute-start | bytes 1572872 | tf_op jit(solution)/shard_map/ppermute | solution.py:417
  230.0 38.0 %collective-permute-start.37 = (bf16[4,128,1024]{2,1,0:T(8,128)(2,1)}, bf16[4,128,1024]{2,1,0:T(8,128)(2,1)S(1)}, u32[]{:S(2)}, u32[]{:S(2)}) collective-permute-start(bf16[4,128,1024]{2,1,0:T(8,128)(2,1)} %get-tuple-element.124), channel_id=1, source_target_pairs={{0,4},{4,0},{8,12},{12,8},{16,20},{20,16},{24,28},{28,24},{1,5},{5... | collective-permute-start | bytes 3145736 | tf_op jit(solution)/shard_map/ppermute | solution.py:417
  243.6 35.6 %collective-permute-start.46 = (bf16[4,128,1024]{2,1,0:T(8,128)(2,1)}, bf16[4,128,1024]{2,1,0:T(8,128)(2,1)S(1)}, u32[]{:S(2)}, u32[]{:S(2)}) collective-permute-start(bf16[4,128,1024]{2,1,0:T(8,128)(2,1)} %get-tuple-element.135), channel_id=1, source_target_pairs={{0,4},{4,0},{8,12},{12,8},{16,20},{20,16},{24,28},{28,24},{1,5},{5... | collective-permute-start | bytes 3145736 | tf_op jit(solution)/shard_map/ppermute | solution.py:417
  251.4 23.6 %collective-permute-start.38 = (bf16[2,128,1024]{2,1,0:T(8,128)(2,1)S(1)}, bf16[2,128,1024]{2,1,0:T(8,128)(2,1)S(1)}, u32[]{:S(2)}, u32[]{:S(2)}) collective-permute-start(bf16[2,128,1024]{2,1,0:T(8,128)(2,1)S(1)} %get-tuple-element.121.fresh_ref), channel_id=1, source_target_pairs={{28,20},{24,16},{20,12},{16,8},{12,4},{8,0},{29,21},{25,17},{21,13... | collective-permute-start | bytes 1572872 | tf_op jit(solution)/shard_map/ppermute | solution.py:417
  252.9 22.2 %collective-permute-start.36 = (bf16[2,128,1024]{2,1,0:T(8,128)(2,1)S(1)}, bf16[2,128,1024]{2,1,0:T(8,128)(2,1)S(1)}, u32[]{:S(2)}, u32[]{:S(2)}) collective-permute-start(bf16[2,128,1024]{2,1,0:T(8,128)(2,1)S(1)} %get-tuple-element.121.fresh_ref), channel_id=1, source_target_pairs={{0,8},{4,12},{8,16},{12,20},{16,24},{20,28},{1,9},{5,13},{9,17},{1... | collective-permute-start | bytes 1572872 | tf_op jit(solution)/shard_map/ppermute | solution.py:417
  297.6 21.1 %collective-permute-start.41 = (bf16[2,128,1024]{2,1,0:T(8,128)(2,1)S(1)}, bf16[2,128,1024]{2,1,0:T(8,128)(2,1)S(1)}, u32[]{:S(2)}, u32[]{:S(2)}) collective-permute-start(bf16[2,128,1024]{2,1,0:T(8,128)(2,1)S(1)} %get-tuple-element.127), channel_id=1, source_target_pairs={{0,8},{4,12},{8,16},{12,20},{16,24},{20,28},{1,9},{5,13},{9,17},{1... | collective-permute-start | bytes 1572872 | tf_op jit(solution)/shard_map/ppermute | solution.py:417
  302.0 32.8 %collective-permute-start.32 = (bf16[4,128,1024]{2,1,0:T(8,128)(2,1)S(1)}, bf16[4,128,1024]{2,1,0:T(8,128)(2,1)S(1)}, u32[]{:S(2)}, u32[]{:S(2)}) collective-permute-start(bf16[4,128,1024]{2,1,0:T(8,128)(2,1)S(1)} %get-tuple-element.116), channel_id=1, source_target_pairs={{0,4},{4,0},{8,12},{12,8},{16,20},{20,16},{24,28},{28,24},{1,5},{5... | collective-permute-start | bytes 3145736 | tf_op jit(solution)/shard_map/ppermute | solution.py:417
  302.7 44.8 %collective-permute-start.33 = (bf16[4,128,1024]{2,1,0:T(8,128)(2,1)S(1)}, bf16[4,128,1024]{2,1,0:T(8,128)(2,1)S(1)}, u32[]{:S(2)}, u32[]{:S(2)}) collective-permute-start(bf16[4,128,1024]{2,1,0:T(8,128)(2,1)S(1)} %get-tuple-element.117), channel_id=1, source_target_pairs={{0,4},{4,0},{8,12},{12,8},{16,20},{20,16},{24,28},{28,24},{1,5},{5... | collective-permute-start | bytes 3145736 | tf_op jit(solution)/shard_map/ppermute | solution.py:417
  321.3 31.4 %collective-permute-start.54 = (bf16[2,128,1024]{2,1,0:T(8,128)(2,1)S(1)}, bf16[2,128,1024]{2,1,0:T(8,128)(2,1)S(1)}, u32[]{:S(2)}, u32[]{:S(2)}) collective-permute-start(bf16[2,128,1024]{2,1,0:T(8,128)(2,1)S(1)} %get-tuple-element.143), channel_id=1, source_target_pairs={{0,8},{4,12},{8,16},{12,20},{16,24},{20,28},{1,9},{5,13},{9,17},{1... | collective-permute-start | bytes 1572872 | tf_op jit(solution)/shard_map/ppermute | solution.py:417
  329.9 22.9 %collective-permute-start.55 = (bf16[2,128,1024]{2,1,0:T(8,128)(2,1)S(1)}, bf16[2,128,1024]{2,1,0:T(8,128)(2,1)S(1)}, u32[]{:S(2)}, u32[]{:S(2)}) collective-permute-start(bf16[2,128,1024]{2,1,0:T(8,128)(2,1)S(1)} %get-tuple-element.144), channel_id=1, source_target_pairs={{28,20},{24,16},{20,12},{16,8},{12,4},{8,0},{29,21},{25,17},{21,13... | collective-permute-start | bytes 1572872 | tf_op jit(solution)/shard_map/ppermute | solution.py:417
  333.5 45.8 %collective-permute-start.52 = (bf16[4,128,1024]{2,1,0:T(8,128)(2,1)S(1)}, bf16[4,128,1024]{2,1,0:T(8,128)(2,1)S(1)}, u32[]{:S(2)}, u32[]{:S(2)}) collective-permute-start(bf16[4,128,1024]{2,1,0:T(8,128)(2,1)S(1)} %get-tuple-element.141), channel_id=1, source_target_pairs={{0,4},{4,0},{8,12},{12,8},{16,20},{20,16},{24,28},{28,24},{1,5},{5... | collective-permute-start | bytes 3145736 | tf_op jit(solution)/shard_map/ppermute | solution.py:417
  334.8 21.9 %collective-permute-start.65 = (bf16[2,128,1024]{2,1,0:T(8,128)(2,1)S(1)}, bf16[2,128,1024]{2,1,0:T(8,128)(2,1)S(1)}, u32[]{:S(2)}, u32[]{:S(2)}) collective-permute-start(bf16[2,128,1024]{2,1,0:T(8,128)(2,1)S(1)} %get-tuple-element.149), channel_id=1, source_target_pairs={{0,8},{4,12},{8,16},{12,20},{16,24},{20,28},{1,9},{5,13},{9,17},{1... | collective-permute-start | bytes 1572872 | tf_op jit(solution)/shard_map/ppermute | solution.py:417
  373.4 22.1 %collective-permute-start.59 = (bf16[2,128,1024]{2,1,0:T(8,128)(2,1)S(1)}, bf16[2,128,1024]{2,1,0:T(8,128)(2,1)S(1)}, u32[]{:S(2)}, u32[]{:S(2)}) collective-permute-start(bf16[2,128,1024]{2,1,0:T(8,128)(2,1)S(1)} %get-tuple-element.146.fresh_ref), channel_id=1, source_target_pairs={{28,20},{24,16},{20,12},{16,8},{12,4},{8,0},{29,21},{25,17},{21,13... | collective-permute-start | bytes 1572872 | tf_op jit(solution)/shard_map/ppermute | solution.py:417
  374.7 22.1 %collective-permute-start.56 = (bf16[2,128,1024]{2,1,0:T(8,128)(2,1)S(1)}, bf16[2,128,1024]{2,1,0:T(8,128)(2,1)S(1)}, u32[]{:S(2)}, u32[]{:S(2)}) collective-permute-start(bf16[2,128,1024]{2,1,0:T(8,128)(2,1)S(1)} %get-tuple-element.146.fresh_ref), channel_id=1, source_target_pairs={{0,8},{4,12},{8,16},{12,20},{16,24},{20,28},{1,9},{5,13},{9,17},{1... | collective-permute-start | bytes 1572872 | tf_op jit(solution)/shard_map/ppermute | solution.py:417
  379.2 30.3 %collective-permute-start.53 = (bf16[4,128,1024]{2,1,0:T(8,128)(2,1)S(1)}, bf16[4,128,1024]{2,1,0:T(8,128)(2,1)S(1)}, u32[]{:S(2)}, u32[]{:S(2)}) collective-permute-start(bf16[4,128,1024]{2,1,0:T(8,128)(2,1)S(1)} %get-tuple-element.142), channel_id=1, source_target_pairs={{0,4},{4,0},{8,12},{12,8},{16,20},{20,16},{24,28},{28,24},{1,5},{5... | collective-permute-start | bytes 3145736 | tf_op jit(solution)/shard_map/ppermute | solution.py:417
  (122 other events, 1815.8 us)

commit v3 on v2

--- a/solution.py
+++ b/solution.py
@@ -12,6 +12,7 @@
 lr_inner = 2.0
 
 STREAMS = 2
+BRIEF = pl.CostEstimate(flops=1, bytes_accessed=1, transcendentals=0)
 FOLD = 2
 
 
@@ -71,42 +72,53 @@
             out_specs=[thin] * len(dtypes),
         ),
         out_shape=[jax.ShapeDtypeStruct((units, rows), dtype) for dtype in dtypes],
-        compiler_params=params(32),
-        cost_estimate=pl.CostEstimate(
-            flops=2 * len(picked) * rows * width * units,
-            bytes_accessed=2 * len(picked) * units * width,
-            transcendentals=units * rows,
-        ),
+        compiler_params=params(16),
+        cost_estimate=BRIEF,
     )(order, right, *[weights] * len(picked), *extra)
 
 
-def finals_kernel(scale, block, pieces, table_ref, left_ref, right_ref, weight_ref, *refs):
-    own_ref, send_ref = refs[-2:]
+def finals_kernel(scale, block, pieces, split, table_ref, left_ref, right_ref, weight_ref, *refs):
+    own_ref, send_refs = refs[0], refs[1:]
+    line = own_ref.shape[0]
     grad = contract(left_ref[...], right_ref[0], 1, 0) * (lr_inner * scale)
     for q in range(pieces):
         rows = slice(q * block, (q + 1) * block)
         final = weight_ref[0, 0, rows, :].astype(jnp.float32) - grad[rows]
         spot = table_ref[1, q]
-
-        @pl.when(table_ref[0, q] == 0)
+        leaves = table_ref[0, q] != 0
+        outer = (spot == 0) | (spot == line - 1)
+
+        @pl.when(jnp.logical_not(leaves))
         def _():
             own_ref[spot] = final
 
-        @pl.when(table_ref[0, q] != 0)
-        def _():
-            send_ref[spot] = final.astype(jnp.bfloat16)
-
-
-def finals(table, order, left, right, weights, level, columns, scale, line, block, after):
+        if split:
+
+            @pl.when(leaves & outer)
+            def _():
+                send_refs[0][jnp.where(spot == 0, 0, 1)] = final.astype(jnp.bfloat16)
+
+            @pl.when(leaves & jnp.logical_not(outer))
+            def _():
+                send_refs[1][jnp.clip(spot - 1, 0, line - 3)] = final.astype(jnp.bfloat16)
+
+        else:
+
+            @pl.when(leaves)
+            def _():
+                send_refs[0][spot] = final.astype(jnp.bfloat16)
+
+
+def finals(table, order, left, right, weights, level, columns, scale, line, block, split, after):
     start, tiles, tile = columns
     units, rows = left.shape
     per = right.shape[2] // tile
-    spec = pl.BlockSpec((line, block, tile), lambda t, table, order: (0, 0, t))
     width = tiles * tile
-    shape = (line, block, width)
-
-    def kernel(table_ref, order_ref, *refs):
-        finals_kernel(scale, block, units // block, table_ref, *refs)
+    counts = [line] + ([2, line - 2] if split else [line])
+
+    def kernel(table_ref, order_ref, left_ref, right_ref, weight_ref, *refs):
+        outs = refs[len(after) :]
+        finals_kernel(scale, block, units // block, split, table_ref, left_ref, right_ref, weight_ref, *outs)
 
     return pl.pallas_call(
         kernel,
@@ -121,13 +133,14 @@
                 pl.BlockSpec((1, 1, units, tile), lambda t, table, order: (0, level, 0, start(t))),
             ]
             + [pl.BlockSpec(memory_space=pl.ANY)] * len(after),
-            out_specs=[spec, spec],
+            out_specs=[pl.BlockSpec((n, block, tile), lambda t, table, order: (0, 0, t)) for n in counts],
         ),
-        out_shape=[jax.ShapeDtypeStruct(shape, jnp.float32), jax.ShapeDtypeStruct(shape, jnp.bfloat16)],
-        compiler_params=params(24),
-        cost_estimate=pl.CostEstimate(
-            flops=2 * rows * width * units, bytes_accessed=5 * units * width + 2 * units * rows, transcendentals=0
-        ),
+        out_shape=[
+            jax.ShapeDtypeStruct((n, block, width), jnp.bfloat16 if i else jnp.float32)
+            for i, n in enumerate(counts)
+        ],
+        compiler_params=params(16),
+        cost_estimate=BRIEF,
     )(table, order, left, right, weights, *after)
 
 
@@ -137,8 +150,8 @@
     return ups, downs
 
 
-def running_kernel(line, step, at_ref, *refs):
-    own_refs, got_refs, flow_refs, out_refs = refs[:2], refs[2:4], refs[4:-2], refs[-2:]
+def running_kernel(line, step, flows, at_ref, *refs):
+    own_refs, got_refs, flow_refs, out_refs = refs[:2], refs[2:4], refs[4 : 4 + flows], refs[-2:]
     modules = out_refs[0].shape[0]
     z = at_ref[2]
     lives = (z < step, z >= line - step)
@@ -153,28 +166,28 @@
             out_refs[way][m] = total.astype(jnp.bfloat16)
 
 
-def running(at, own, got, flow, modules, step):
+def running(at, own, got, flow, modules, step, outer, after):
     line, block, width = own.shape
     tile = min(512, width)
-    ups, downs = places(line, step)
-    one = [
-        pl.BlockSpec((1, block, tile), lambda t, at, spot=spot: (spot(at), 0, t)) for spot in (ups, downs)
-    ]
+    both = places(line, step)
+    one = lambda spot: pl.BlockSpec((1, block, tile), lambda t, at: (spot(at), 0, t))
+    ends = (lambda at: 1, lambda at: 0)
     wide = pl.BlockSpec((modules, block, tile), lambda t, at: (0, 0, t))
     return pl.pallas_call(
-        functools.partial(running_kernel, line, step),
+        functools.partial(running_kernel, line, step, len(flow)),
         grid_spec=pltpu.PrefetchScalarGridSpec(
             num_scalar_prefetch=1,
             grid=(width // tile,),
-            in_specs=one + one + [wide] * len(flow),
+            in_specs=[one(spot) for spot in both]
+            + [one(spot) for spot in (ends if outer else both)]
+            + [wide] * len(flow)
+            + [pl.BlockSpec(memory_space=pl.ANY)] * len(after),
             out_specs=[wide, wide],
         ),
         out_shape=[jax.ShapeDtypeStruct((modules, block, width), jnp.bfloat16)] * 2,
         compiler_params=params(12),
-        cost_estimate=pl.CostEstimate(
-            flops=12 * modules * block * width, bytes_accessed=20 * block * width, transcendentals=0
-        ),
-    )(at, own, own, got, got, *flow)
+        cost_estimate=BRIEF,
+    )(at, own, own, got, got, *flow, *after)
 
 
 def update_kernel(count, at_ref, share_ref, own_ref, got_ref, up_ref, low_ref, stored_ref, old_ref, *refs):
@@ -213,54 +226,51 @@
         ],
         input_output_aliases={} if whole is None else {8: 1},
         compiler_params=params(16),
-        cost_estimate=pl.CostEstimate(
-            flops=12 * modules * block * tiles * tile,
-            bytes_accessed=16 * modules * block * tiles * tile,
-            transcendentals=0,
-        ),
+        cost_estimate=BRIEF,
     )(at, share, own, got, *flow, outer_weights, momentum, *extra)
 
 
-def deliver_kernel(line, at_ref, fresh_ref, *refs):
-    ups, lows = refs[: line - 1], refs[line - 1 : 2 * line - 2]
+def deliver_kernel(line, rings, at_ref, fresh_ref, *refs):
+    ups, lows = refs[: len(rings)], refs[len(rings) : 2 * len(rings)]
     near_ref, far_ref, sems = refs[-3:]
     z = at_ref[2]
     for side, out_ref in enumerate((near_ref, far_ref)):
         module = at_ref[side]
 
-        def copy(source, r, side=side, out_ref=out_ref, module=module):
-            return pltpu.make_async_copy(source.at[module], out_ref.at[r], sems.at[side, r])
-
-        copy(fresh_ref, 0).start()
-        for r in range(1, line):
+        def copy(source, i, side=side, out_ref=out_ref, module=module):
+            return pltpu.make_async_copy(source.at[module], out_ref.at[i], sems.at[side, i])
+
+        for i, r in enumerate(rings):
+            if r == 0:
+                copy(fresh_ref, i).start()
+                continue
 
             @pl.when(z >= r)
             def _():
-                copy(ups[r - 1], r).start()
+                copy(ups[i], i).start()
 
             @pl.when(z < r)
             def _():
-                copy(lows[line - 1 - r], r).start()
+                copy(lows[i], i).start()
 
     for side, out_ref in enumerate((near_ref, far_ref)):
-        for r in range(line):
-            pltpu.make_async_copy(fresh_ref.at[0], out_ref.at[r], sems.at[side, r]).wait()
-
-
-def deliver(at, fresh, ups, lows, after):
-    line = len(ups) + 1
-    shape = jax.ShapeDtypeStruct((line,) + fresh.shape[1:], fresh.dtype)
+        for i in range(len(rings)):
+            pltpu.make_async_copy(fresh_ref.at[0], out_ref.at[i], sems.at[side, i]).wait()
+
+
+def deliver(at, fresh, ups, lows, line, rings, after):
+    shape = jax.ShapeDtypeStruct((len(rings),) + fresh.shape[1:], fresh.dtype)
     anywhere = pl.BlockSpec(memory_space=pl.ANY)
-    return pl.pallas_call(
-        functools.partial(deliver_kernel, line),
-        in_specs=[pl.BlockSpec(memory_space=pltpu.SMEM)] + [anywhere] * (2 * line - 1 + len(after)),
+    ups = [ups[r - 1] if r else fresh for r in rings]
+    lows = [lows[line - 1 - r] if r else fresh for r in rings]
+    return pl.pallas_call(
+        functools.partial(deliver_kernel, line, rings),
+        in_specs=[pl.BlockSpec(memory_space=pltpu.SMEM)] + [anywhere] * (2 * len(rings) + 1 + len(after)),
         out_specs=[pl.BlockSpec(memory_space=pltpu.VMEM)] * 2,
         out_shape=[shape, shape],
-        scratch_shapes=[pltpu.SemaphoreType.DMA((2, line))],
+        scratch_shapes=[pltpu.SemaphoreType.DMA((2, len(rings)))],
         compiler_params=params(12),
-        cost_estimate=pl.CostEstimate(
-            flops=0, bytes_accessed=4 * shape.size * 2, transcendentals=0
-        ),
+        cost_estimate=BRIEF,
     )(at, fresh, *ups, *lows, *after)
 
 
@@ -309,40 +319,47 @@
         out_specs=vmem,
         out_shape=jax.ShapeDtypeStruct((pieces, block, rows), dtype),
         compiler_params=params(32),
-        cost_estimate=pl.CostEstimate(
-            flops=2 * rows * chunks * size * pieces * block,
-            bytes_accessed=2 * chunks * size * pieces * block,
-            transcendentals=0,
-        ),
+        cost_estimate=BRIEF,
     )(order, table, inputs, *extra, *parts)
 
 
-def down_kernel(scale, left_ref, near_ref, far_ref, out_ref):
-    line, block, width = near_ref.shape
+def down_kernel(scale, ranks, high_ref, left_ref, *refs):
+    parts, keep_ref, send_ref = refs[:-2], refs[-2], refs[-1]
     rows = left_ref.shape[2]
-    near_left = left_ref[:line].reshape(line * block, rows)
-    far_left = left_ref[line:].reshape(line * block, rows)
-    total = contract(near_left, near_ref[...].reshape(-1, width), 0, 0)
-    total = total + contract(far_left, far_ref[...].reshape(-1, width), 0, 0)
-    out_ref[...] = total * scale
-
-
-def down(left, near, far, scale):
+    total = None
+    at = 0
+    for part in parts:
+        count, block, width = part.shape
+        left = left_ref[at : at + count].reshape(count * block, rows)
+        value = contract(left, part[...].reshape(count * block, width), 0, 0)
+        total = value if total is None else total + value
+        at += count
+    total = total * scale
+    size = width // ranks
+    high = high_ref[0] != 0
+    for i in range(ranks // 2):
+        low_part = total[:, 2 * i * size : (2 * i + 1) * size]
+        high_part = total[:, (2 * i + 1) * size : (2 * i + 2) * size]
+        spot = slice(i * size, (i + 1) * size)
+        keep_ref[:, spot] = jnp.where(high, high_part, low_part)
+        send_ref[:, spot] = jnp.where(high, low_part, high_part).astype(jnp.bfloat16)
+
+
+def down(high, left, parts, ranks, scale):
     pieces, block, rows = left.shape
-    width = near.shape[2]
+    width = parts[0].shape[2]
     vmem = pl.BlockSpec(memory_space=pltpu.VMEM)
     return pl.pallas_call(
-        functools.partial(down_kernel, scale),
-        in_specs=[vmem] * 3,
-        out_specs=vmem,
-        out_shape=jax.ShapeDtypeStruct((rows, width), jnp.float32),
+        functools.partial(down_kernel, scale, ranks),
+        in_specs=[pl.BlockSpec(memory_space=pltpu.SMEM)] + [vmem] * (1 + len(parts)),
+        out_specs=[vmem] * 2,
+        out_shape=[
+            jax.ShapeDtypeStruct((rows, width // 2), jnp.float32),
+            jax.ShapeDtypeStruct((rows, width // 2), jnp.bfloat16),
+        ],
         compiler_params=params(24),
-        cost_estimate=pl.CostEstimate(
-            flops=2 * rows * width * pieces * block,
-            bytes_accessed=2 * pieces * block * width + 4 * rows * width,
-            transcendentals=0,
-        ),
-    )(left, near, far)
+        cost_estimate=BRIEF,
+    )(high, left, *parts)
 
 
 def pairs_of(size, bit):
@@ -350,28 +367,29 @@
 
 
 def gather_mp(values, size):
-    held = [value[None] for value in values]
+    held = [[value[None]] for value in values]
     offsets = [0]
     bit = size // 2
     while bit:
-        held = [jnp.concatenate([part, lax.ppermute(part, "mp", pairs_of(size, bit))], axis=0) for part in held]
+        held = [parts + [lax.ppermute(part, "mp", pairs_of(size, bit)) for part in parts] for parts in held]
         offsets = offsets + [offset ^ bit for offset in offsets]
         bit //= 2
-    return held, offsets
-
-
-def scatter_mp(value, size, index):
-    width = value.shape[1] // size
-    parts = [value[:, i * width : (i + 1) * width] for i in range(size)]
-    bit = 1
+    return [jnp.concatenate(parts, axis=0) for parts in held], offsets
+
+
+def scatter_mp(keep, send, size, index):
+    width = 2 * keep.shape[1] // size
+    value = keep + lax.ppermute(send, "mp", pairs_of(size, 1)).astype(jnp.float32)
+    bit = 2
     while bit < size:
+        parts = [value[:, at : at + width] for at in range(0, value.shape[1], width)]
         high = (index & bit) != 0
         keep = [jnp.where(high, parts[i + 1], parts[i]) for i in range(0, len(parts), 2)]
-        sent = [jnp.where(high, parts[i], parts[i + 1]) for i in range(0, len(parts), 2)]
-        got = lax.ppermute(jnp.concatenate(sent, axis=1), "mp", pairs_of(size, bit))
-        parts = [part + got[:, i * width : (i + 1) * width] for i, part in enumerate(keep)]
+        send = [jnp.where(high, parts[i], parts[i + 1]) for i in range(0, len(parts), 2)]
+        got = lax.ppermute(jnp.concatenate(send, axis=1).astype(jnp.bfloat16), "mp", pairs_of(size, bit))
+        value = jnp.concatenate(keep, axis=1) + got.astype(jnp.float32)
         bit *= 2
-    return parts[0]
+    return value
 
 
 def shards(tokens, cotangent, path_weights, outer_weights, momentum, assignment, owners):
@@ -408,9 +426,6 @@
     down_at = jnp.sum(
         jnp.where(piece_at[1][:, None] == path_ids[None, :], slot[2][None, :], 0), axis=1
     )
-    gate_table = piece_at[0][None]
-    hidden_table = jnp.stack([piece_at[1], down_at])
-
     across = pairs_of(paths, 1)
 
     def permute(value, pairs):
@@ -439,32 +454,57 @@
     )
     sources = ((pre_gate, inputs, scale_d), (pre_up, inputs, scale_d), (hidden, upstream, scale_f))
 
+    late = [r for r in range(line) if max(r - 1, line - 1 - r) == line - 2 and r]
+    soon = [r for r in range(line) if r not in late]
+    parts_of = [(side, r) for rings in (soon, late) for side in range(FOLD) for r in rings]
+    turn = jnp.asarray([parts_of.index((e // line, e % line)) for e in range(paths)], jnp.int32)
+    down_at = jnp.sum(jnp.where(down_at[:, None] == path_ids[None, :], turn[None, :], 0), axis=1)
+    gate_table = piece_at[0][None]
+    hidden_table = jnp.stack([piece_at[1], down_at])
+    high = (rank & 1)[None]
+
     flow = [[] for _ in range(STREAMS)]
     first = [[] for _ in range(STREAMS)]
     waiting = [None] * STREAMS
-    near = [[None] * STREAMS for _ in range(levels)]
-    far = [[None] * STREAMS for _ in range(levels)]
+    near = [[[] for _ in range(STREAMS)] for _ in range(levels)]
+    far = [[[] for _ in range(STREAMS)] for _ in range(levels)]
     whole = None
     hidden_new = gate_new = None
 
-    def give(level, s):
-        near[level][s], leaving = deliver(at_all[level], *waiting[s], [hidden_new] if level == 2 else [])
-        far[level][s] = permute(leaving, across)
+    def give(level, s, rings, after):
+        fresh, ups, lows = waiting[s]
+        held, leaving = deliver(at_all[level], fresh, ups, lows, line, rings, after)
+        near[level][s].append(held)
+        far[level][s].append(permute(leaving, across))
+
+    def ring_parts(level):
+        return [part for half in (near, far) for s in range(STREAMS) for part in half[level][s]]
 
     outs = []
     for level in range(levels + 1):
-        own, got = [None] * STREAMS, [None] * STREAMS
+        own, got, ends = [None] * STREAMS, [None] * STREAMS, [None] * STREAMS
+        split = level == 0 and line > 2
         if level < levels:
             left, right, scale = sources[level]
             for s in range(STREAMS):
-                own[s], send = finals(
-                    leaves[level], order, left, right, path_weights, level, columns(level, s), scale, line, block, first[s]
+                own[s], *sent = finals(
+                    leaves[level], order, left, right, path_weights, level, columns(level, s), scale, line, block,
+                    split, first[s],
                 )
-                got[s] = permute(send, across)
+                if split:
+                    ends[s] = permute(sent[0], across)
+                    middle = permute(sent[1], across)
+                    got[s] = jnp.concatenate([ends[s][:1], middle, ends[s][1:]], axis=0)
+                else:
+                    got[s] = permute(sent[0], across)
         for step in range(1, line):
             for s in range(STREAMS):
                 if level < levels:
-                    value = running(at_all[level], own[s], got[s], flow[s], modules, step)
+                    outer = split and step == 1
+                    after = near[level - 1][s] if level and step == line - 1 else []
+                    value = running(
+                        at_all[level], own[s], ends[s] if outer else got[s], flow[s], modules, step, outer, after
+                    )
                     flow[s] = along(value, 0, step - 1 if level == 0 else line)
                 elif step < line - 1:
                     flow[s] = along(flow[s], step, line)
@@ -474,13 +514,16 @@
                     if step < line - 1:
                         waiting[s][1].append(flow[s][0])
                         waiting[s][2].append(flow[s][1])
-                    if step == max(line - 2, 1):
-                        give(level - 1, s)
+                    if level < levels and step == max(line - 2, 1):
+                        give(level - 1, s, tuple(range(line)), [])
+                    if level == levels:
+                        if step == max(line - 3, 1):
+                            give(level - 1, s, tuple(soon), [hidden_new])
+                        if step == max(line - 2, 1):
+                            give(level - 1, s, tuple(late), [])
         if level < levels:
             for s in range(STREAMS):
-                after = [near[level - 1][s]] if level else []
-                if level == 2:
-                    after.append(gate_new)
+                after = [gate_new] if level == 2 else []
                 fresh, whole = update(
                     at_all[level], shares[level], own[s], got[s], flow[s], outer_weights, momentum, whole, level,
                     columns(level, s), after,
@@ -489,16 +532,18 @@
                 waiting[s] = (fresh, [flow[s][0]], [flow[s][1]])
         if level == 1:
             gate_new = forward(
-                gate_kernel, order, gate_table, inputs, (), near[0] + far[0], jnp.float32, scale_d, line, block
+                gate_kernel, order, gate_table, inputs, (), ring_parts(0), jnp.float32, scale_d, line, block
             )
         if level == 2:
             hidden_new = forward(
-                hidden_kernel, order, hidden_table, inputs, (gate_new,), near[1] + far[1], jnp.bfloat16, scale_d,
+                hidden_kernel, order, hidden_table, inputs, (gate_new,), ring_parts(1), jnp.bfloat16, scale_d,
                 line, block,
             )
         if level == 3:
             for s in range(STREAMS):
-                outs.append(scatter_mp(down(hidden_new, near[2][s], far[2][s], scale_f), ranks, rank))
+                parts = [part for pair in zip(near[2][s], far[2][s]) for part in pair]
+                keep, send = down(high, hidden_new, parts, ranks, scale_f)
+                outs.append(scatter_mp(keep, send, ranks, rank))
 
     outputs = jnp.concatenate(outs, axis=1).astype(jnp.bfloat16)
     return outputs, whole

time: 469 us -> 439 us (0.936)
  waiting for transfers between devices: 188 us -> 150 us
  starting transfers between devices: 154 us -> 170 us
    ppermute x68 -> x72, waiting for transfers between devices: 157 us -> 125 us  [permute(): return lax.ppermute(value, 'path', pairs)]
    ppermute x68 -> x72, starting transfers between devices: 148 us -> 163 us  [permute(): return lax.ppermute(value, 'path', pairs)]
    ppermute x4, waiting for transfers between devices: 16.1 us -> 9 us  [the longest x2 8.99 us: scatter_mp(): lax.ppermute(jnp.concatenate(send, axis=1).astype(jnp.bfloat16), 'mp', pa...]
    pallas_call x26 -> x28, Pallas kernels: 38.6 us -> 37.1 us  [the longest x18 23.8 us: running(): pl.pallas_call(functools.partial(running_kernel, line, step, len(flow)),...]
    unnamed x140 -> x68, local copies, waits for them, and re-layouts: 19.3 us -> 18.3 us
    ppermute x4 -> x6, waiting for transfers between devices: 15.4 us -> 16.1 us  [gather_mp(): lax.ppermute(part, 'mp', pairs_of(size, bit))]
  transfers between devices with their start and end apart: 76 -> 82, of which waited for: 37 -> 40; matrix products, arithmetic and copies ran while one was open for 1% -> 1% of each run, Pallas kernels for 18% -> 19%
where the time goes in v3:
time: 439 us; the launch traced here: 437 us
  starting transfers between devices  170 us (39%)
  waiting for transfers between devices  150 us (34%)
  Pallas kernels  89.4 us (20%)
  local copies, waits for them, and re-layouts  19.4 us (4%)
  other arithmetic  6.26 us (1%)
    ppermute x72, starting transfers between devices, permute(): return lax.ppermute(value, 'path', pairs)  163 us
    ppermute x72, waiting for transfers between devices, permute(): return lax.ppermute(value, 'path', pairs)  125 us
    pallas_call x18, Pallas kernels, running(): pl.pallas_call(functools.partial(running_kernel, line, step, len(flow)),...  23.8 us
    pallas_call x6, Pallas kernels, finals(): pl.pallas_call(kernel, grid_spec=pltpu.PrefetchScalarGridSpec(num_scalar_...  20.3 us
    unnamed x68, local copies, waits for them, and re-layouts  18.3 us
    pallas_call x6, Pallas kernels, update(): pl.pallas_call(functools.partial(update_kernel, modules), grid_spec=pltpu...  16.8 us
    ppermute x6, waiting for transfers between devices, gather_mp(): lax.ppermute(part, 'mp', pairs_of(size, bit))  16.1 us
    pallas_call x2, Pallas kernels, front(): pl.pallas_call(functools.partial(kernel, scale, chunks), grid_spec=pltpu....  9.33 us
  transfers between devices with their start and end apart: 82, of which 40 were waited for; matrix products, arithmetic and copies ran while one was open for 1% of the time, Pallas kernels for 19%

profile of v3, /device:TPU:0, one launch (start us, length us, event | category | flops | bytes accessed | tf_op | source)
XLA Modules:
  0.0 436.7 jit_solution(1755776642508576442)
XLA Ops:
  6.0 8.0 %collective-permute-done = bf16[1,384,512]{2,1,0:T(8,128)(2,1)S(1)} collective-permute-done((bf16[1,384,512]{2,1,0:T(8,128)(2,1)}, bf16[1,384,512]{2,1,0:T(8,128)(2,1)S(1)}, u32[]{:S(2)}, u32[]{:S(2)}) %collective-permute-start) | collective-permute-done | bytes 393248 | tf_op jit(solution)/shard_map/ppermute | solution.py:374
  13.9 8.1 %collective-permute-done.3 = bf16[1,384,512]{2,1,0:T(8,128)(2,1)S(1)} collective-permute-done((bf16[1,384,512]{2,1,0:T(8,128)(2,1)}, bf16[1,384,512]{2,1,0:T(8,128)(2,1)S(1)}, u32[]{:S(2)}, u32[]{:S(2)}) %collective-permute-start.3) | collective-permute-done | bytes 393248 | tf_op jit(solution)/shard_map/ppermute | solution.py:374
  28.7 5.6 %shard_map.104 = (f32[1024,384]{1,0:T(8,128)S(1)}, f32[1024,384]{1,0:T(8,128)S(1)}, bf16[1024,384]{1,0:T(8,128)(2,1)S(1)}) custom-call(s32[4]{0:T(128)S(1)} %select_reduce_fusion.4.order_ref, bf16[4,384,512]{2,1,0:T(8,128)(2,1)S(1)} %pad_maximum_fusion.x_ref.right_ref, bf16[1,3,1024,2048]{3,2,1,0:T(8,128)(2,1)S(1)} %copy-done, ...), custom_call_target="tpu_custom_call" | custom-call | flops 1 | bytes 1 | tf_op jit(solution)/shard_map/pallas_call | solution.py:61
  66.0 4.8 %collective-permute-done.21.refs_2_.refs_3_ = bf16[2,128,1024]{2,1,0:T(8,128)(2,1)S(1)} collective-permute-done((bf16[2,128,1024]{2,1,0:T(8,128)(2,1)S(1)}, bf16[2,128,1024]{2,1,0:T(8,128)(2,1)S(1)}, u32[]{:S(2)}, u32[]{:S(2)}) %collective-permute-start.21) | collective-permute-done | bytes 524320 | tf_op jit(solution)/shard_map/ppermute | solution.py:432
  75.5 6.5 %collective-permute-done.7 = bf16[2,128,1024]{2,1,0:T(8,128)(2,1)S(1)} collective-permute-done((bf16[2,128,1024]{2,1,0:T(8,128)(2,1)S(1)}, bf16[2,128,1024]{2,1,0:T(8,128)(2,1)S(1)}, u32[]{:S(2)}, u32[]{:S(2)}) %collective-permute-start.7) | collective-permute-done | bytes 524320 | tf_op jit(solution)/shard_map/ppermute | solution.py:432
  99.9 10.1 %collective-permute-start.12 = (bf16[2,128,1024]{2,1,0:T(8,128)(2,1)S(1)}, bf16[2,128,1024]{2,1,0:T(8,128)(2,1)S(1)}, u32[]{:S(2)}, u32[]{:S(2)}) collective-permute-start(bf16[2,128,1024]{2,1,0:T(8,128)(2,1)S(1)} %get-tuple-element.99), channel_id=1, source_target_pairs={{0,8},{4,12},{8,16},{12,20},{16,24},{20,28},{1,9},{5,13},{9,17},{1... | collective-permute-start | bytes 1572872 | tf_op jit(solution)/shard_map/ppermute | solution.py:432
  116.7 9.0 %collective-permute-start.27 = (bf16[2,128,1024]{2,1,0:T(8,128)(2,1)S(1)}, bf16[2,128,1024]{2,1,0:T(8,128)(2,1)S(1)}, u32[]{:S(2)}, u32[]{:S(2)}) collective-permute-start(bf16[2,128,1024]{2,1,0:T(8,128)(2,1)S(1)} %get-tuple-element.117), channel_id=1, source_target_pairs={{0,8},{4,12},{8,16},{12,20},{16,24},{20,28},{1,9},{5,13},{9,17},{1... | collective-permute-start | bytes 1572872 | tf_op jit(solution)/shard_map/ppermute | solution.py:432
  138.6 4.6 %collective-permute-start.14 = (bf16[2,128,1024]{2,1,0:T(8,128)(2,1)S(1)}, bf16[2,128,1024]{2,1,0:T(8,128)(2,1)S(1)}, u32[]{:S(2)}, u32[]{:S(2)}) collective-permute-start(bf16[2,128,1024]{2,1,0:T(8,128)(2,1)S(1)} %get-tuple-element.101.fresh_ref.refs_0_.refs_4_), channel_id=1, source_target_pairs={{0,8},{4,12},{8,16},{12,20},{16,24},{20,28},{1,9},{5,13},{9,17},{1... | collective-permute-start | bytes 1572872 | tf_op jit(solution)/shard_map/ppermute | solution.py:432
  149.9 4.6 %collective-permute-start.29 = (bf16[2,128,1024]{2,1,0:T(8,128)(2,1)S(1)}, bf16[2,128,1024]{2,1,0:T(8,128)(2,1)S(1)}, u32[]{:S(2)}, u32[]{:S(2)}) collective-permute-start(bf16[2,128,1024]{2,1,0:T(8,128)(2,1)S(1)} %get-tuple-element.120.fresh_ref.refs_0_.refs_4_), channel_id=1, source_target_pairs={{0,8},{4,12},{8,16},{12,20},{16,24},{20,28},{1,9},{5,13},{9,17},{1... | collective-permute-start | bytes 1572872 | tf_op jit(solution)/shard_map/ppermute | solution.py:432
  163.7 4.7 %collective-permute-done.31.refs_5_.refs_7_ = bf16[2,128,1024]{2,1,0:T(8,128)(2,1)S(1)} collective-permute-done((bf16[2,128,1024]{2,1,0:T(8,128)(2,1)S(1)}, bf16[2,128,1024]{2,1,0:T(8,128)(2,1)S(1)}, u32[]{:S(2)}, u32[]{:S(2)}) %collective-permute-start.31) | collective-permute-done | bytes 524320 | tf_op jit(solution)/shard_map/ppermute | solution.py:432
  233.7 6.2 %collective-permute-done.48.low_ref = bf16[2,128,1024]{2,1,0:T(8,128)(2,1)S(1)} collective-permute-done((bf16[2,128,1024]{2,1,0:T(8,128)(2,1)S(1)}, bf16[2,128,1024]{2,1,0:T(8,128)(2,1)S(1)}, u32[]{:S(2)}, u32[]{:S(2)}) %collective-permute-start.48) | collective-permute-done | bytes 524320 | tf_op jit(solution)/shard_map/ppermute | solution.py:432
  243.8 4.6 %collective-permute-start.49 = (bf16[2,128,1024]{2,1,0:T(8,128)(2,1)S(1)}, bf16[2,128,1024]{2,1,0:T(8,128)(2,1)S(1)}, u32[]{:S(2)}, u32[]{:S(2)}) collective-permute-start(bf16[2,128,1024]{2,1,0:T(8,128)(2,1)S(1)} %get-tuple-element.145.fresh_ref.refs_0_.refs_4_), channel_id=1, source_target_pairs={{0,8},{4,12},{8,16},{12,20},{16,24},{20,28},{1,9},{5,13},{9,17},{1... | collective-permute-start | bytes 1572872 | tf_op jit(solution)/shard_map/ppermute | solution.py:432
  256.4 6.0 %collective-permute-done.51.refs_5_.refs_7_ = bf16[2,128,1024]{2,1,0:T(8,128)(2,1)S(1)} collective-permute-done((bf16[2,128,1024]{2,1,0:T(8,128)(2,1)S(1)}, bf16[2,128,1024]{2,1,0:T(8,128)(2,1)S(1)}, u32[]{:S(2)}, u32[]{:S(2)}) %collective-permute-start.51) | collective-permute-done | bytes 524320 | tf_op jit(solution)/shard_map/ppermute | solution.py:432
  285.8 5.0 %collective-permute-start.54 = (bf16[2,128,1024]{2,1,0:T(8,128)(2,1)S(1)}, bf16[2,128,1024]{2,1,0:T(8,128)(2,1)S(1)}, u32[]{:S(2)}, u32[]{:S(2)}) collective-permute-start(bf16[2,128,1024]{2,1,0:T(8,128)(2,1)S(1)} %get-tuple-element.150), channel_id=1, source_target_pairs={{0,8},{4,12},{8,16},{12,20},{16,24},{20,28},{1,9},{5,13},{9,17},{1... | collective-permute-start | bytes 1572872 | tf_op jit(solution)/shard_map/ppermute | solution.py:432
  317.5 4.7 %collective-permute-done.37.refs_3_ = bf16[4,128,1024]{2,1,0:T(8,128)(2,1)S(1)} collective-permute-done((bf16[4,128,1024]{2,1,0:T(8,128)(2,1)S(1)}, bf16[4,128,1024]{2,1,0:T(8,128)(2,1)S(1)}, u32[]{:S(2)}, u32[]{:S(2)}) %collective-permute-start.37) | collective-permute-done | bytes 1048608 | tf_op jit(solution)/shard_map/ppermute | solution.py:432
  329.8 9.1 %collective-permute-done.71.low_ref = bf16[2,128,1024]{2,1,0:T(8,128)(2,1)S(1)} collective-permute-done((bf16[2,128,1024]{2,1,0:T(8,128)(2,1)S(1)}, bf16[2,128,1024]{2,1,0:T(8,128)(2,1)S(1)}, u32[]{:S(2)}, u32[]{:S(2)}) %collective-permute-start.71) | collective-permute-done | bytes 524320 | tf_op jit(solution)/shard_map/ppermute | solution.py:432
  343.4 4.6 %collective-permute-start.72 = (bf16[2,128,1024]{2,1,0:T(8,128)(2,1)S(1)}, bf16[2,128,1024]{2,1,0:T(8,128)(2,1)S(1)}, u32[]{:S(2)}, u32[]{:S(2)}) collective-permute-start(bf16[2,128,1024]{2,1,0:T(8,128)(2,1)S(1)} %get-tuple-element.168.fresh_ref.refs_0_.refs_2_), channel_id=1, source_target_pairs={{0,8},{4,12},{8,16},{12,20},{16,24},{20,28},{1,9},{5,13},{9,17},{1... | collective-permute-start | bytes 1572872 | tf_op jit(solution)/shard_map/ppermute | solution.py:432
  349.3 4.6 %collective-permute-start.60 = (bf16[2,128,1024]{2,1,0:T(8,128)(2,1)S(1)}, bf16[2,128,1024]{2,1,0:T(8,128)(2,1)S(1)}, u32[]{:S(2)}, u32[]{:S(2)}) collective-permute-start(bf16[2,128,1024]{2,1,0:T(8,128)(2,1)S(1)} %get-tuple-element.158.fresh_ref.refs_0_.refs_2_), channel_id=1, source_target_pairs={{0,8},{4,12},{8,16},{12,20},{16,24},{20,28},{1,9},{5,13},{9,17},{1... | collective-permute-start | bytes 1572872 | tf_op jit(solution)/shard_map/ppermute | solution.py:432
  353.9 5.0 %collective-permute-done.74.refs_3_ = bf16[2,128,1024]{2,1,0:T(8,128)(2,1)S(1)} collective-permute-done((bf16[2,128,1024]{2,1,0:T(8,128)(2,1)S(1)}, bf16[2,128,1024]{2,1,0:T(8,128)(2,1)S(1)}, u32[]{:S(2)}, u32[]{:S(2)}) %collective-permute-start.74) | collective-permute-done | bytes 524320 | tf_op jit(solution)/shard_map/ppermute | solution.py:432
  362.1 8.0 %collective-permute-done.62.refs_3_ = bf16[2,128,1024]{2,1,0:T(8,128)(2,1)S(1)} collective-permute-done((bf16[2,128,1024]{2,1,0:T(8,128)(2,1)S(1)}, bf16[2,128,1024]{2,1,0:T(8,128)(2,1)S(1)}, u32[]{:S(2)}, u32[]{:S(2)}) %collective-permute-start.62) | collective-permute-done | bytes 524320 | tf_op jit(solution)/shard_map/ppermute | solution.py:432
  372.1 5.0 %collective-permute-done.75.refs_3_ = bf16[2,128,1024]{2,1,0:T(8,128)(2,1)S(1)} collective-permute-done((bf16[2,128,1024]{2,1,0:T(8,128)(2,1)S(1)}, bf16[2,128,1024]{2,1,0:T(8,128)(2,1)S(1)}, u32[]{:S(2)}, u32[]{:S(2)}) %collective-permute-start.75) | collective-permute-done | bytes 524320 | tf_op jit(solution)/shard_map/ppermute | solution.py:432
  403.5 4.9 %collective-permute-done.79.refs_3_ = bf16[2,128,1024]{2,1,0:T(8,128)(2,1)} collective-permute-done((bf16[2,128,1024]{2,1,0:T(8,128)(2,1)}, bf16[2,128,1024]{2,1,0:T(8,128)(2,1)}, u32[]{:S(2)}, u32[]{:S(2)}) %collective-permute-start.79) | collective-permute-done | bytes 524320 | tf_op jit(solution)/shard_map/ppermute | solution.py:432
  413.9 5.7 %collective-permute-done.67.refs_3_ = bf16[2,128,1024]{2,1,0:T(8,128)(2,1)} collective-permute-done((bf16[2,128,1024]{2,1,0:T(8,128)(2,1)}, bf16[2,128,1024]{2,1,0:T(8,128)(2,1)}, u32[]{:S(2)}, u32[]{:S(2)}) %collective-permute-start.67) | collective-permute-done | bytes 524320 | tf_op jit(solution)/shard_map/ppermute | solution.py:432
  426.8 5.0 %collective-permute-done.81 = bf16[384,256]{1,0:T(8,128)(2,1)S(1)} collective-permute-done((bf16[384,256]{1,0:T(8,128)(2,1)S(1)}, bf16[384,256]{1,0:T(8,128)(2,1)S(1)}, u32[]{:S(2)}, u32[]{:S(2)}) %collective-permute-start.81) | collective-permute-done | bytes 196640 | tf_op jit(solution)/shard_map/ppermute | solution.py:389
  (286 shorter events, 290.1 us)
Async XLA Ops:
  0.6 22.3 %collective-permute-start.1 = (bf16[1,384,512]{2,1,0:T(8,128)(2,1)}, bf16[1,384,512]{2,1,0:T(8,128)(2,1)S(1)}, u32[]{:S(2)}, u32[]{:S(2)}) collective-permute-start(bf16[1,384,512]{2,1,0:T(8,128)(2,1)} %bitcast.56), channel_id=1, source_target_pairs={{0,1},{1,0},{2,3},{3,2},{4,5},{5,4},{6,7},{7,6},{8,9},{9,8},{10,11... | collective-permute-start | bytes 1179656 | tf_op jit(solution)/shard_map/ppermute | solution.py:374
  3.7 31.5 %collective-permute-start.4 = (bf16[1,384,512]{2,1,0:T(8,128)(2,1)}, bf16[1,384,512]{2,1,0:T(8,128)(2,1)S(1)}, u32[]{:S(2)}, u32[]{:S(2)}) collective-permute-start(bf16[1,384,512]{2,1,0:T(8,128)(2,1)} %bitcast.59), channel_id=1, source_target_pairs={{0,1},{1,0},{2,3},{3,2},{4,5},{5,4},{6,7},{7,6},{8,9},{9,8},{10,11... | collective-permute-start | bytes 1179656 | tf_op jit(solution)/shard_map/ppermute | solution.py:374
  56.4 25.6 %collective-permute-start.7 = (bf16[2,128,1024]{2,1,0:T(8,128)(2,1)S(1)}, bf16[2,128,1024]{2,1,0:T(8,128)(2,1)S(1)}, u32[]{:S(2)}, u32[]{:S(2)}) collective-permute-start(bf16[2,128,1024]{2,1,0:T(8,128)(2,1)S(1)} %get-tuple-element.94), channel_id=1, source_target_pairs={{0,4},{4,0},{8,12},{12,8},{16,20},{20,16},{24,28},{28,24},{1,5},{5... | collective-permute-start | bytes 1572872 | tf_op jit(solution)/shard_map/ppermute | solution.py:432
  59.6 23.2 %collective-permute-start.8 = (bf16[2,128,1024]{2,1,0:T(8,128)(2,1)S(1)}, bf16[2,128,1024]{2,1,0:T(8,128)(2,1)S(1)}, u32[]{:S(2)}, u32[]{:S(2)}) collective-permute-start(bf16[2,128,1024]{2,1,0:T(8,128)(2,1)S(1)} %get-tuple-element.95), channel_id=1, source_target_pairs={{0,8},{4,12},{1,9},{5,13},{2,10},{6,14},{3,11},{7,15}} | collective-permute-start | bytes 1572872 | tf_op jit(solution)/shard_map/ppermute | solution.py:432
  64.1 28.5 %collective-permute-start.22 = (bf16[2,128,1024]{2,1,0:T(8,128)(2,1)S(1)}, bf16[2,128,1024]{2,1,0:T(8,128)(2,1)S(1)}, u32[]{:S(2)}, u32[]{:S(2)}) collective-permute-start(bf16[2,128,1024]{2,1,0:T(8,128)(2,1)S(1)} %get-tuple-element.112), channel_id=1, source_target_pairs={{0,4},{4,0},{8,12},{12,8},{16,20},{20,16},{24,28},{28,24},{1,5},{5... | collective-permute-start | bytes 1572872 | tf_op jit(solution)/shard_map/ppermute | solution.py:432
  71.9 20.8 %collective-permute-start.23 = (bf16[2,128,1024]{2,1,0:T(8,128)(2,1)S(1)}, bf16[2,128,1024]{2,1,0:T(8,128)(2,1)S(1)}, u32[]{:S(2)}, u32[]{:S(2)}) collective-permute-start(bf16[2,128,1024]{2,1,0:T(8,128)(2,1)S(1)} %get-tuple-element.113), channel_id=1, source_target_pairs={{0,8},{4,12},{1,9},{5,13},{2,10},{6,14},{3,11},{7,15}} | collective-permute-start | bytes 1572872 | tf_op jit(solution)/shard_map/ppermute | solution.py:432
  94.1 21.3 %collective-permute-start.25 = (bf16[2,128,1024]{2,1,0:T(8,128)(2,1)S(1)}, bf16[2,128,1024]{2,1,0:T(8,128)(2,1)S(1)}, u32[]{:S(2)}, u32[]{:S(2)}) collective-permute-start(bf16[2,128,1024]{2,1,0:T(8,128)(2,1)S(1)} %get-tuple-element.115), channel_id=1, source_target_pairs={{0,8},{4,12},{8,16},{12,20},{1,9},{5,13},{9,17},{13,21},{2,10},{6,... | collective-permute-start | bytes 1572872 | tf_op jit(solution)/shard_map/ppermute | solution.py:432
  99.9 30.7 %collective-permute-start.12 = (bf16[2,128,1024]{2,1,0:T(8,128)(2,1)S(1)}, bf16[2,128,1024]{2,1,0:T(8,128)(2,1)S(1)}, u32[]{:S(2)}, u32[]{:S(2)}) collective-permute-start(bf16[2,128,1024]{2,1,0:T(8,128)(2,1)S(1)} %get-tuple-element.99), channel_id=1, source_target_pairs={{0,8},{4,12},{8,16},{12,20},{16,24},{20,28},{1,9},{5,13},{9,17},{1... | collective-permute-start | bytes 1572872 | tf_op jit(solution)/shard_map/ppermute | solution.py:432
  113.0 36.9 %collective-permute-start.15 = (bf16[4,128,1024]{2,1,0:T(8,128)(2,1)S(1)}, bf16[4,128,1024]{2,1,0:T(8,128)(2,1)S(1)}, u32[]{:S(2)}, u32[]{:S(2)}) collective-permute-start(bf16[4,128,1024]{2,1,0:T(8,128)(2,1)S(1)} %get-tuple-element.104), channel_id=1, source_target_pairs={{0,4},{4,0},{8,12},{12,8},{16,20},{20,16},{24,28},{28,24},{1,5},{5... | collective-permute-start | bytes 3145736 | tf_op jit(solution)/shard_map/ppermute | solution.py:432
  114.1 20.7 %collective-permute-start.13 = (bf16[2,128,1024]{2,1,0:T(8,128)(2,1)S(1)}, bf16[2,128,1024]{2,1,0:T(8,128)(2,1)S(1)}, u32[]{:S(2)}, u32[]{:S(2)}) collective-permute-start(bf16[2,128,1024]{2,1,0:T(8,128)(2,1)S(1)} %get-tuple-element.100), channel_id=1, source_target_pairs={{28,20},{24,16},{20,12},{16,8},{12,4},{8,0},{29,21},{25,17},{21,13... | collective-permute-start | bytes 1572872 | tf_op jit(solution)/shard_map/ppermute | solution.py:432
  116.7 21.9 %collective-permute-start.27 = (bf16[2,128,1024]{2,1,0:T(8,128)(2,1)S(1)}, bf16[2,128,1024]{2,1,0:T(8,128)(2,1)S(1)}, u32[]{:S(2)}, u32[]{:S(2)}) collective-permute-start(bf16[2,128,1024]{2,1,0:T(8,128)(2,1)S(1)} %get-tuple-element.117), channel_id=1, source_target_pairs={{0,8},{4,12},{8,16},{12,20},{16,24},{20,28},{1,9},{5,13},{9,17},{1... | collective-permute-start | bytes 1572872 | tf_op jit(solution)/shard_map/ppermute | solution.py:432
  130.6 33.1 %collective-permute-start.30 = (bf16[4,128,1024]{2,1,0:T(8,128)(2,1)S(1)}, bf16[4,128,1024]{2,1,0:T(8,128)(2,1)S(1)}, u32[]{:S(2)}, u32[]{:S(2)}) collective-permute-start(bf16[4,128,1024]{2,1,0:T(8,128)(2,1)S(1)} %get-tuple-element.122), channel_id=1, source_target_pairs={{0,4},{4,0},{8,12},{12,8},{16,20},{20,16},{24,28},{28,24},{1,5},{5... | collective-permute-start | bytes 3145736 | tf_op jit(solution)/shard_map/ppermute | solution.py:432
  201.1 42.6 %collective-permute-start.41 = (bf16[4,128,1024]{2,1,0:T(8,128)(2,1)S(1)}, bf16[4,128,1024]{2,1,0:T(8,128)(2,1)S(1)}, u32[]{:S(2)}, u32[]{:S(2)}) collective-permute-start(bf16[4,128,1024]{2,1,0:T(8,128)(2,1)S(1)} %get-tuple-element.136), channel_id=1, source_target_pairs={{0,4},{4,0},{8,12},{12,8},{16,20},{20,16},{24,28},{28,24},{1,5},{5... | collective-permute-start | bytes 3145736 | tf_op jit(solution)/shard_map/ppermute | solution.py:432
  224.4 32.0 %collective-permute-start.50 = (bf16[4,128,1024]{2,1,0:T(8,128)(2,1)S(1)}, bf16[4,128,1024]{2,1,0:T(8,128)(2,1)S(1)}, u32[]{:S(2)}, u32[]{:S(2)}) collective-permute-start(bf16[4,128,1024]{2,1,0:T(8,128)(2,1)S(1)} %get-tuple-element.147), channel_id=1, source_target_pairs={{0,4},{4,0},{8,12},{12,8},{16,20},{20,16},{24,28},{28,24},{1,5},{5... | collective-permute-start | bytes 3145736 | tf_op jit(solution)/shard_map/ppermute | solution.py:432
  227.1 24.0 %collective-permute-start.42 = (bf16[2,128,1024]{2,1,0:T(8,128)(2,1)S(1)}, bf16[2,128,1024]{2,1,0:T(8,128)(2,1)S(1)}, u32[]{:S(2)}, u32[]{:S(2)}) collective-permute-start(bf16[2,128,1024]{2,1,0:T(8,128)(2,1)S(1)} %get-tuple-element.133.fresh_ref.refs_0_.refs_4_), channel_id=1, source_target_pairs={{28,20},{24,16},{20,12},{16,8},{12,4},{8,0},{29,21},{25,17},{21,13... | collective-permute-start | bytes 1572872 | tf_op jit(solution)/shard_map/ppermute | solution.py:432
  229.2 21.9 %collective-permute-start.40 = (bf16[2,128,1024]{2,1,0:T(8,128)(2,1)S(1)}, bf16[2,128,1024]{2,1,0:T(8,128)(2,1)S(1)}, u32[]{:S(2)}, u32[]{:S(2)}) collective-permute-start(bf16[2,128,1024]{2,1,0:T(8,128)(2,1)S(1)} %get-tuple-element.133.fresh_ref.refs_0_.refs_4_), channel_id=1, source_target_pairs={{0,8},{4,12},{8,16},{12,20},{16,24},{20,28},{1,9},{5,13},{9,17},{1... | collective-permute-start | bytes 1572872 | tf_op jit(solution)/shard_map/ppermute | solution.py:432
  277.7 35.8 %collective-permute-start.36 = (bf16[4,128,1024]{2,1,0:T(8,128)(2,1)S(1)}, bf16[4,128,1024]{2,1,0:T(8,128)(2,1)S(1)}, u32[]{:S(2)}, u32[]{:S(2)}) collective-permute-start(bf16[4,128,1024]{2,1,0:T(8,128)(2,1)S(1)} %get-tuple-element.128), channel_id=1, source_target_pairs={{0,4},{4,0},{8,12},{12,8},{16,20},{20,16},{24,28},{28,24},{1,5},{5... | collective-permute-start | bytes 3145736 | tf_op jit(solution)/shard_map/ppermute | solution.py:432
  277.8 44.4 %collective-permute-start.37 = (bf16[4,128,1024]{2,1,0:T(8,128)(2,1)S(1)}, bf16[4,128,1024]{2,1,0:T(8,128)(2,1)S(1)}, u32[]{:S(2)}, u32[]{:S(2)}) collective-permute-start(bf16[4,128,1024]{2,1,0:T(8,128)(2,1)S(1)} %get-tuple-element.129), channel_id=1, source_target_pairs={{0,4},{4,0},{8,12},{12,8},{16,20},{20,16},{24,28},{28,24},{1,5},{5... | collective-permute-start | bytes 3145736 | tf_op jit(solution)/shard_map/ppermute | solution.py:432
  297.9 28.7 %collective-permute-start.58 = (bf16[2,128,1024]{2,1,0:T(8,128)(2,1)S(1)}, bf16[2,128,1024]{2,1,0:T(8,128)(2,1)S(1)}, u32[]{:S(2)}, u32[]{:S(2)}) collective-permute-start(bf16[2,128,1024]{2,1,0:T(8,128)(2,1)S(1)} %get-tuple-element.155), channel_id=1, source_target_pairs={{0,8},{4,12},{8,16},{12,20},{16,24},{20,28},{1,9},{5,13},{9,17},{1... | collective-permute-start | bytes 1572872 | tf_op jit(solution)/shard_map/ppermute | solution.py:432
  304.0 22.6 %collective-permute-start.59 = (bf16[2,128,1024]{2,1,0:T(8,128)(2,1)S(1)}, bf16[2,128,1024]{2,1,0:T(8,128)(2,1)S(1)}, u32[]{:S(2)}, u32[]{:S(2)}) collective-permute-start(bf16[2,128,1024]{2,1,0:T(8,128)(2,1)S(1)} %get-tuple-element.156), channel_id=1, source_target_pairs={{28,20},{24,16},{20,12},{16,8},{12,4},{8,0},{29,21},{25,17},{21,13... | collective-permute-start | bytes 1572872 | tf_op jit(solution)/shard_map/ppermute | solution.py:432
  307.5 53.4 %collective-permute-start.56 = (bf16[4,128,1024]{2,1,0:T(8,128)(2,1)S(1)}, bf16[4,128,1024]{2,1,0:T(8,128)(2,1)S(1)}, u32[]{:S(2)}, u32[]{:S(2)}) collective-permute-start(bf16[4,128,1024]{2,1,0:T(8,128)(2,1)S(1)} %get-tuple-element.153), channel_id=1, source_target_pairs={{0,4},{4,0},{8,12},{12,8},{16,20},{20,16},{24,28},{28,24},{1,5},{5... | collective-permute-start | bytes 3145736 | tf_op jit(solution)/shard_map/ppermute | solution.py:432
  348.0 22.1 %collective-permute-start.62 = (bf16[2,128,1024]{2,1,0:T(8,128)(2,1)S(1)}, bf16[2,128,1024]{2,1,0:T(8,128)(2,1)S(1)}, u32[]{:S(2)}, u32[]{:S(2)}) collective-permute-start(bf16[2,128,1024]{2,1,0:T(8,128)(2,1)S(1)} %get-tuple-element.158.fresh_ref.refs_0_.refs_2_), channel_id=1, source_target_pairs={{28,20},{24,16},{20,12},{16,8},{12,4},{8,0},{29,21},{25,17},{21,13... | collective-permute-start | bytes 1572872 | tf_op jit(solution)/shard_map/ppermute | solution.py:432
  349.3 22.1 %collective-permute-start.60 = (bf16[2,128,1024]{2,1,0:T(8,128)(2,1)S(1)}, bf16[2,128,1024]{2,1,0:T(8,128)(2,1)S(1)}, u32[]{:S(2)}, u32[]{:S(2)}) collective-permute-start(bf16[2,128,1024]{2,1,0:T(8,128)(2,1)S(1)} %get-tuple-element.158.fresh_ref.refs_0_.refs_2_), channel_id=1, source_target_pairs={{0,8},{4,12},{8,16},{12,20},{16,24},{20,28},{1,9},{5,13},{9,17},{1... | collective-permute-start | bytes 1572872 | tf_op jit(solution)/shard_map/ppermute | solution.py:432
  360.9 26.1 %collective-permute-start.57 = (bf16[4,128,1024]{2,1,0:T(8,128)(2,1)S(1)}, bf16[4,128,1024]{2,1,0:T(8,128)(2,1)S(1)}, u32[]{:S(2)}, u32[]{:S(2)}) collective-permute-start(bf16[4,128,1024]{2,1,0:T(8,128)(2,1)S(1)} %get-tuple-element.154), channel_id=1, source_target_pairs={{0,4},{4,0},{8,12},{12,8},{16,20},{20,16},{24,28},{28,24},{1,5},{5... | collective-permute-start | bytes 3145736 | tf_op jit(solution)/shard_map/ppermute | solution.py:432
  (92 other events, 1233.7 us)

commit v4 on v3

--- a/solution.py
+++ b/solution.py
@@ -75,6 +75,19 @@
         compiler_params=params(16),
         cost_estimate=BRIEF,
     )(order, right, *[weights] * len(picked), *extra)
+
+
+def tie(value, after):
+    anywhere = pl.BlockSpec(memory_space=pl.ANY)
+    return pl.pallas_call(
+        lambda *refs: None,
+        in_specs=[anywhere] * (1 + len(after)),
+        out_specs=anywhere,
+        out_shape=jax.ShapeDtypeStruct(value.shape, value.dtype),
+        input_output_aliases={0: 0},
+        compiler_params=params(1),
+        cost_estimate=BRIEF,
+    )(value, *after)
 
 
 def finals_kernel(scale, block, pieces, split, table_ref, left_ref, right_ref, weight_ref, *refs):
@@ -150,31 +163,41 @@
     return ups, downs
 
 
-def running_kernel(line, step, flows, at_ref, *refs):
-    own_refs, got_refs, flow_refs, out_refs = refs[:2], refs[2:4], refs[4 : 4 + flows], refs[-2:]
+def running_kernel(line, step, flows, outs, at_ref, *refs):
+    own_refs, got_refs, flow_refs, out_refs = refs[:2], refs[2:4], refs[4 : 4 + flows], refs[-outs:]
     modules = out_refs[0].shape[0]
     z = at_ref[2]
     lives = (z < step, z >= line - step)
-    for way in range(2):
-        for m in range(modules):
+    lower = 2 * z < line
+    for m in range(modules):
+        totals = []
+        for way in range(2):
             total = jnp.where(lives[way] & (at_ref[0] == m), own_refs[way][0], 0.0)
             total = total + jnp.where(
                 lives[way] & (at_ref[1] == m), got_refs[way][0].astype(jnp.float32), 0.0
             )
-            if flow_refs:
+            if flows == 2:
                 total = total + flow_refs[way][m].astype(jnp.float32)
-            out_refs[way][m] = total.astype(jnp.bfloat16)
+            if flows == 1:
+                mine = lower if way == 0 else jnp.logical_not(lower)
+                total = total + jnp.where(mine, flow_refs[0][m].astype(jnp.float32), 0.0)
+            totals.append(total)
+        if outs == 1:
+            totals = [jnp.where(lower, totals[0], totals[1])]
+        for total, out_ref in zip(totals, out_refs):
+            out_ref[m] = total.astype(jnp.bfloat16)
 
 
 def running(at, own, got, flow, modules, step, outer, after):
     line, block, width = own.shape
+    outs = 1 if not flow and line > 3 else 2
     tile = min(512, width)
     both = places(line, step)
     one = lambda spot: pl.BlockSpec((1, block, tile), lambda t, at: (spot(at), 0, t))
     ends = (lambda at: 1, lambda at: 0)
     wide = pl.BlockSpec((modules, block, tile), lambda t, at: (0, 0, t))
     return pl.pallas_call(
-        functools.partial(running_kernel, line, step, len(flow)),
+        functools.partial(running_kernel, line, step, len(flow), outs),
         grid_spec=pltpu.PrefetchScalarGridSpec(
             num_scalar_prefetch=1,
             grid=(width // tile,),
@@ -182,9 +205,9 @@
             + [one(spot) for spot in (ends if outer else both)]
             + [wide] * len(flow)
             + [pl.BlockSpec(memory_space=pl.ANY)] * len(after),
-            out_specs=[wide, wide],
+            out_specs=[wide] * outs,
         ),
-        out_shape=[jax.ShapeDtypeStruct((modules, block, width), jnp.bfloat16)] * 2,
+        out_shape=[jax.ShapeDtypeStruct((modules, block, width), jnp.bfloat16)] * outs,
         compiler_params=params(12),
         cost_estimate=BRIEF,
     )(at, own, own, got, got, *flow, *after)
@@ -374,7 +397,7 @@
         held = [parts + [lax.ppermute(part, "mp", pairs_of(size, bit)) for part in parts] for parts in held]
         offsets = offsets + [offset ^ bit for offset in offsets]
         bit //= 2
-    return [jnp.concatenate(parts, axis=0) for parts in held], offsets
+    return held, offsets
 
 
 def scatter_mp(keep, send, size, index):
@@ -404,7 +427,8 @@
     scale_d = width ** (-0.5)
     scale_f = (units * ranks) ** (-0.5)
 
-    (inputs, upstream), offsets = gather_mp([tokens, cotangent], ranks)
+    held, offsets = gather_mp([tokens, cotangent], ranks)
+    inputs, upstream = (jnp.concatenate(parts, axis=0) for parts in held)
     spots = jnp.asarray([offsets.index(i) for i in range(ranks)], jnp.int32)
     rank_ids = jnp.arange(ranks, dtype=jnp.int32)
     order = jnp.sum(jnp.where((rank_ids ^ rank)[:, None] == rank_ids[None, :], spots[None, :], 0), axis=1)
@@ -434,6 +458,8 @@
     def along(values, first, last):
         up = [(i, i + FOLD) for i in range(paths - FOLD) if first <= i // FOLD <= last]
         low = [(paths - 1 - i, paths - 1 - j) for i, j in up]
+        if len(values) == 1:
+            return [permute(values[0], up + low)]
         return [permute(values[0], up), permute(values[1], low)]
 
     half = width // STREAMS
@@ -455,8 +481,8 @@
     sources = ((pre_gate, inputs, scale_d), (pre_up, inputs, scale_d), (hidden, upstream, scale_f))
 
     late = [r for r in range(line) if max(r - 1, line - 1 - r) == line - 2 and r]
-    soon = [r for r in range(line) if r not in late]
-    parts_of = [(side, r) for rings in (soon, late) for side in range(FOLD) for r in rings]
+    soon = [r for r in range(1, line) if r not in late]
+    parts_of = [(side, r) for rings in ([0], soon, late) for side in range(FOLD) for r in rings]
     turn = jnp.asarray([parts_of.index((e // line, e % line)) for e in range(paths)], jnp.int32)
     down_at = jnp.sum(jnp.where(down_at[:, None] == path_ids[None, :], turn[None, :], 0), axis=1)
     gate_table = piece_at[0][None]
@@ -464,7 +490,7 @@
     high = (rank & 1)[None]
 
     flow = [[] for _ in range(STREAMS)]
-    first = [[] for _ in range(STREAMS)]
+    first = [[[] for _ in range(STREAMS)] for _ in range(levels)]
     waiting = [None] * STREAMS
     near = [[[] for _ in range(STREAMS)] for _ in range(levels)]
     far = [[[] for _ in range(STREAMS)] for _ in range(levels)]
@@ -480,36 +506,55 @@
     def ring_parts(level):
         return [part for half in (near, far) for s in range(STREAMS) for part in half[level][s]]
 
+    own = [[None] * STREAMS for _ in range(levels)]
+    got = [[None] * STREAMS for _ in range(levels)]
+    ends = [None] * STREAMS
+
+    def prepare(level):
+        left, right, scale = sources[level]
+        for s in range(STREAMS):
+            own[level][s], *sent = finals(
+                leaves[level], order, left, right, path_weights, level, columns(level, s), scale, line, block,
+                level == 0 and line > 2, first[level][s],
+            )
+            if len(sent) > 1:
+                ends[s] = permute(sent[0], across)
+                middle = permute(sent[1], across)
+                got[level][s] = jnp.concatenate([ends[s][:1], middle, ends[s][1:]], axis=0)
+            else:
+                got[level][s] = permute(sent[0], across)
+
     outs = []
     for level in range(levels + 1):
-        own, got, ends = [None] * STREAMS, [None] * STREAMS, [None] * STREAMS
-        split = level == 0 and line > 2
-        if level < levels:
-            left, right, scale = sources[level]
-            for s in range(STREAMS):
-                own[s], *sent = finals(
-                    leaves[level], order, left, right, path_weights, level, columns(level, s), scale, line, block,
-                    split, first[s],
-                )
-                if split:
-                    ends[s] = permute(sent[0], across)
-                    middle = permute(sent[1], across)
-                    got[s] = jnp.concatenate([ends[s][:1], middle, ends[s][1:]], axis=0)
-                else:
-                    got[s] = permute(sent[0], across)
+        if level == 0:
+            prepare(0)
+        if level == 1:
+            prepare(1)
+            prepare(2)
+        if level == 2:
+            gate_new = forward(
+                gate_kernel, order, gate_table, inputs, (), ring_parts(0), jnp.float32, scale_d, line, block
+            )
         for step in range(1, line):
             for s in range(STREAMS):
                 if level < levels:
-                    outer = split and step == 1
+                    outer = level == 0 and line > 2 and step == 1
                     after = near[level - 1][s] if level and step == line - 1 else []
+                    if level == 1 and step == line - 1:
+                        after = after + [got[2][s]]
+                    if level == 2 and step == line - 2 and s == 0:
+                        after = after + [gate_new]
                     value = running(
-                        at_all[level], own[s], ends[s] if outer else got[s], flow[s], modules, step, outer, after
+                        at_all[level], own[level][s], ends[s] if outer else got[level][s], flow[s], modules, step,
+                        outer, after,
                     )
                     flow[s] = along(value, 0, step - 1 if level == 0 else line)
                 elif step < line - 1:
+                    if s == STREAMS - 1:
+                        flow[s][0] = waiting[s][1][-1] = tie(flow[s][0], [hidden_new] + near[2][0] + far[2][0][:1] if step == 1 else near[2][0] + far[2][0][:1] + far[2][-1][:1])
                     flow[s] = along(flow[s], step, line)
-                if step == 1:
-                    first[s] = flow[s][:1]
+                if step == 1 and level == 0:
+                    first[1][s] = flow[s][:1]
                 if waiting[s] is not None:
                     if step < line - 1:
                         waiting[s][1].append(flow[s][0])
@@ -517,23 +562,22 @@
                     if level < levels and step == max(line - 2, 1):
                         give(level - 1, s, tuple(range(line)), [])
                     if level == levels:
-                        if step == max(line - 3, 1):
+                        if step == max(line - 3, 1) and soon:
                             give(level - 1, s, tuple(soon), [hidden_new])
                         if step == max(line - 2, 1):
                             give(level - 1, s, tuple(late), [])
         if level < levels:
             for s in range(STREAMS):
-                after = [gate_new] if level == 2 else []
                 fresh, whole = update(
-                    at_all[level], shares[level], own[s], got[s], flow[s], outer_weights, momentum, whole, level,
-                    columns(level, s), after,
+                    at_all[level], shares[level], own[level][s], got[level][s], flow[s], outer_weights, momentum, whole, level,
+                    columns(level, s), [],
                 )
                 flow[s] = along((fresh, fresh), 0, line)
                 waiting[s] = (fresh, [flow[s][0]], [flow[s][1]])
-        if level == 1:
-            gate_new = forward(
-                gate_kernel, order, gate_table, inputs, (), ring_parts(0), jnp.float32, scale_d, line, block
-            )
+                if level == 0:
+                    first[2][s] = flow[s][:1]
+                if level == 2:
+                    give(level, s, (0,), [])
         if level == 2:
             hidden_new = forward(
                 hidden_kernel, order, hidden_table, inputs, (gate_new,), ring_parts(1), jnp.bfloat16, scale_d,

time: 439 us -> 430 us (0.979)
  starting transfers between devices: 170 us -> 152 us
  waiting for transfers between devices: 150 us -> 157 us
    ppermute x72, starting transfers between devices: 163 us -> 145 us  [permute(): return lax.ppermute(value, 'path', pairs)]
    ppermute x72, waiting for transfers between devices: 125 us -> 133 us  [permute(): return lax.ppermute(value, 'path', pairs)]
    pallas_call x8 -> x10, Pallas kernels: 9.19 us -> 10.3 us  [deliver(): pl.pallas_call(functools.partial(deliver_kernel, line, rings), in_specs=[...]
    pallas_call x18 -> x20, Pallas kernels: 23.8 us -> 23.7 us  [the longest x18 23.7 us: running(): pl.pallas_call(functools.partial(running_kernel, line, step, len(flow), o...]
  transfers between devices with their start and end apart: 82 -> 82, of which waited for: 40 -> 36; matrix products, arithmetic and copies ran while one was open for 1% -> 1% of each run, Pallas kernels for 19% -> 19%
where the time goes in v4:
time: 430 us; the launch traced here: 428 us
  waiting for transfers between devices  157 us (37%)
  starting transfers between devices  152 us (35%)
  Pallas kernels  90.9 us (21%)
  local copies, waits for them, and re-layouts  20.9 us (5%)
  other arithmetic  5.26 us (1%)
    ppermute x72, starting transfers between devices, permute(): return lax.ppermute(value, 'path', pairs)  145 us
    ppermute x72, waiting for transfers between devices, permute(): return lax.ppermute(value, 'path', pairs)  133 us
    pallas_call x18, Pallas kernels, running(): pl.pallas_call(functools.partial(running_kernel, line, step, len(flow), o...  23.7 us
    pallas_call x6, Pallas kernels, finals(): pl.pallas_call(kernel, grid_spec=pltpu.PrefetchScalarGridSpec(num_scalar_...  20.3 us
    unnamed x68, local copies, waits for them, and re-layouts  19.8 us
    pallas_call x6, Pallas kernels, update(): pl.pallas_call(functools.partial(update_kernel, modules), grid_spec=pltpu...  16.8 us
    ppermute x6, waiting for transfers between devices, gather_mp(): lax.ppermute(part, 'mp', pairs_of(size, bit))  15.4 us
    pallas_call x10, Pallas kernels, deliver(): pl.pallas_call(functools.partial(deliver_kernel, line, rings), in_specs=[...  10.3 us
  transfers between devices with their start and end apart: 82, of which 36 were waited for; matrix products, arithmetic and copies ran while one was open for 1% of the time, Pallas kernels for 19%

profile of v4, /device:TPU:0, one launch (start us, length us, event | category | flops | bytes accessed | tf_op | source)
XLA Modules:
  0.0 427.8 jit_solution(5859962304642595360)
XLA Ops:
  6.0 7.9 %collective-permute-done = bf16[1,384,512]{2,1,0:T(8,128)(2,1)S(1)} collective-permute-done((bf16[1,384,512]{2,1,0:T(8,128)(2,1)}, bf16[1,384,512]{2,1,0:T(8,128)(2,1)S(1)}, u32[]{:S(2)}, u32[]{:S(2)}) %collective-permute-start) | collective-permute-done | bytes 393248 | tf_op jit(solution)/shard_map/ppermute | solution.py:397
  13.8 7.6 %collective-permute-done.3 = bf16[1,384,512]{2,1,0:T(8,128)(2,1)S(1)} collective-permute-done((bf16[1,384,512]{2,1,0:T(8,128)(2,1)}, bf16[1,384,512]{2,1,0:T(8,128)(2,1)S(1)}, u32[]{:S(2)}, u32[]{:S(2)}) %collective-permute-start.3) | collective-permute-done | bytes 393248 | tf_op jit(solution)/shard_map/ppermute | solution.py:397
  28.1 5.6 %shard_map.104 = (f32[1024,384]{1,0:T(8,128)S(1)}, f32[1024,384]{1,0:T(8,128)S(1)}, bf16[1024,384]{1,0:T(8,128)(2,1)S(1)}) custom-call(s32[4]{0:T(128)S(1)} %select_reduce_fusion.4.order_ref, bf16[4,384,512]{2,1,0:T(8,128)(2,1)S(1)} %pad_maximum_fusion.x_ref.right_ref, bf16[1,3,1024,2048]{3,2,1,0:T(8,128)(2,1)S(1)} %copy-done, ...), custom_call_target="tpu_custom_call" | custom-call | flops 1 | bytes 1 | tf_op jit(solution)/shard_map/pallas_call | solution.py:61
  45.0 4.6 %copy-done.2 = bf16[1,3,1024,2048]{3,2,1,0:T(8,128)(2,1)S(1)} copy-done((bf16[1,3,1024,2048]{3,2,1,0:T(8,128)(2,1)S(1)}, bf16[1,3,1024,2048]{3,2,1,0:T(8,128)(2,1)}, u32[]{:S(2)}) %copy-start.2) | copy-done | bytes 12582936
  64.5 5.6 %collective-permute-done.20.refs_2_.refs_3_ = bf16[2,128,1024]{2,1,0:T(8,128)(2,1)S(1)} collective-permute-done((bf16[2,128,1024]{2,1,0:T(8,128)(2,1)S(1)}, bf16[2,128,1024]{2,1,0:T(8,128)(2,1)S(1)}, u32[]{:S(2)}, u32[]{:S(2)}) %collective-permute-start.20) | collective-permute-done | bytes 524320 | tf_op jit(solution)/shard_map/ppermute | solution.py:456
  74.7 6.6 %collective-permute-done.7 = bf16[2,128,1024]{2,1,0:T(8,128)(2,1)S(1)} collective-permute-done((bf16[2,128,1024]{2,1,0:T(8,128)(2,1)S(1)}, bf16[2,128,1024]{2,1,0:T(8,128)(2,1)S(1)}, u32[]{:S(2)}, u32[]{:S(2)}) %collective-permute-start.7) | collective-permute-done | bytes 524320 | tf_op jit(solution)/shard_map/ppermute | solution.py:456
  87.1 4.8 %collective-permute-done.21 = bf16[2,128,1024]{2,1,0:T(8,128)(2,1)S(1)} collective-permute-done((bf16[2,128,1024]{2,1,0:T(8,128)(2,1)S(1)}, bf16[2,128,1024]{2,1,0:T(8,128)(2,1)S(1)}, u32[]{:S(2)}, u32[]{:S(2)}) %collective-permute-start.21) | collective-permute-done | bytes 524320 | tf_op jit(solution)/shard_map/ppermute | solution.py:456
  99.2 6.2 %collective-permute-start.11 = (bf16[2,128,1024]{2,1,0:T(8,128)(2,1)S(1)}, bf16[2,128,1024]{2,1,0:T(8,128)(2,1)S(1)}, u32[]{:S(2)}, u32[]{:S(2)}) collective-permute-start(bf16[2,128,1024]{2,1,0:T(8,128)(2,1)S(1)} %get-tuple-element.97), channel_id=1, source_target_pairs={{0,8},{4,12},{8,16},{12,20},{16,24},{20,28},{1,9},{5,13},{9,17},{1... | collective-permute-start | bytes 1572872 | tf_op jit(solution)/shard_map/ppermute | solution.py:456
  112.8 4.6 %collective-permute-start.25 = (bf16[2,128,1024]{2,1,0:T(8,128)(2,1)S(1)}, bf16[2,128,1024]{2,1,0:T(8,128)(2,1)S(1)}, u32[]{:S(2)}, u32[]{:S(2)}) collective-permute-start(bf16[2,128,1024]{2,1,0:T(8,128)(2,1)S(1)} %get-tuple-element.113), channel_id=1, source_target_pairs={{0,8},{4,12},{8,16},{12,20},{16,24},{20,28},{1,9},{5,13},{9,17},{1... | collective-permute-start | bytes 1572872 | tf_op jit(solution)/shard_map/ppermute | solution.py:456
  144.1 4.9 %collective-permute-done.15.refs_5_.refs_7_ = bf16[2,128,1024]{2,1,0:T(8,128)(2,1)S(1)} collective-permute-done((bf16[2,128,1024]{2,1,0:T(8,128)(2,1)S(1)}, bf16[2,128,1024]{2,1,0:T(8,128)(2,1)S(1)}, u32[]{:S(2)}, u32[]{:S(2)}) %collective-permute-start.15) | collective-permute-done | bytes 524320 | tf_op jit(solution)/shard_map/ppermute | solution.py:456
  155.3 4.9 %collective-permute-done.29.refs_5_.refs_7_ = bf16[2,128,1024]{2,1,0:T(8,128)(2,1)S(1)} collective-permute-done((bf16[2,128,1024]{2,1,0:T(8,128)(2,1)S(1)}, bf16[2,128,1024]{2,1,0:T(8,128)(2,1)S(1)}, u32[]{:S(2)}, u32[]{:S(2)}) %collective-permute-start.29) | collective-permute-done | bytes 524320 | tf_op jit(solution)/shard_map/ppermute | solution.py:456
  172.9 4.6 %collective-permute-start.18 = (bf16[2,128,1024]{2,1,0:T(8,128)(2,1)S(1)}, bf16[2,128,1024]{2,1,0:T(8,128)(2,1)S(1)}, u32[]{:S(2)}, u32[]{:S(2)}) collective-permute-start(bf16[2,128,1024]{2,1,0:T(8,128)(2,1)S(1)} %get-tuple-element.105), channel_id=1, source_target_pairs={{0,8},{4,12},{8,16},{12,20},{16,24},{20,28},{1,9},{5,13},{9,17},{1... | collective-permute-start | bytes 1572872 | tf_op jit(solution)/shard_map/ppermute | solution.py:456
  184.7 4.6 %collective-permute-start.32 = (bf16[2,128,1024]{2,1,0:T(8,128)(2,1)S(1)}, bf16[2,128,1024]{2,1,0:T(8,128)(2,1)S(1)}, u32[]{:S(2)}, u32[]{:S(2)}) collective-permute-start(bf16[2,128,1024]{2,1,0:T(8,128)(2,1)S(1)} %get-tuple-element.121), channel_id=1, source_target_pairs={{0,8},{4,12},{8,16},{12,20},{16,24},{20,28},{1,9},{5,13},{9,17},{1... | collective-permute-start | bytes 1572872 | tf_op jit(solution)/shard_map/ppermute | solution.py:456
  191.1 7.0 %collective-permute-done.19.refs_5_ = bf16[2,128,1024]{2,1,0:T(8,128)(2,1)S(1)} collective-permute-done((bf16[2,128,1024]{2,1,0:T(8,128)(2,1)S(1)}, bf16[2,128,1024]{2,1,0:T(8,128)(2,1)S(1)}, u32[]{:S(2)}, u32[]{:S(2)}) %collective-permute-start.19) | collective-permute-done | bytes 524320 | tf_op jit(solution)/shard_map/ppermute | solution.py:456
  203.5 5.8 %collective-permute-done.33.refs_5_ = bf16[2,128,1024]{2,1,0:T(8,128)(2,1)S(1)} collective-permute-done((bf16[2,128,1024]{2,1,0:T(8,128)(2,1)S(1)}, bf16[2,128,1024]{2,1,0:T(8,128)(2,1)S(1)}, u32[]{:S(2)}, u32[]{:S(2)}) %collective-permute-start.33) | collective-permute-done | bytes 524320 | tf_op jit(solution)/shard_map/ppermute | solution.py:456
  226.2 5.2 %collective-permute-done.47.low_ref = bf16[2,128,1024]{2,1,0:T(8,128)(2,1)S(1)} collective-permute-done((bf16[2,128,1024]{2,1,0:T(8,128)(2,1)S(1)}, bf16[2,128,1024]{2,1,0:T(8,128)(2,1)S(1)}, u32[]{:S(2)}, u32[]{:S(2)}) %collective-permute-start.47) | collective-permute-done | bytes 524320 | tf_op jit(solution)/shard_map/ppermute | solution.py:456
  272.4 4.6 %collective-permute-done.51.refs_5_.refs_6_ = bf16[2,128,1024]{2,1,0:T(8,128)(2,1)S(1)} collective-permute-done((bf16[2,128,1024]{2,1,0:T(8,128)(2,1)S(1)}, bf16[2,128,1024]{2,1,0:T(8,128)(2,1)S(1)}, u32[]{:S(2)}, u32[]{:S(2)}) %collective-permute-start.51) | collective-permute-done | bytes 524320 | tf_op jit(solution)/shard_map/ppermute | solution.py:456
  283.6 4.6 %collective-permute-done.44.refs_5_ = bf16[2,128,1024]{2,1,0:T(8,128)(2,1)S(1)} collective-permute-done((bf16[2,128,1024]{2,1,0:T(8,128)(2,1)S(1)}, bf16[2,128,1024]{2,1,0:T(8,128)(2,1)S(1)}, u32[]{:S(2)}, u32[]{:S(2)}) %collective-permute-start.44) | collective-permute-done | bytes 524320 | tf_op jit(solution)/shard_map/ppermute | solution.py:456
  341.0 5.7 %collective-permute-done.74.refs_3_ = bf16[2,128,1024]{2,1,0:T(8,128)(2,1)S(1)} collective-permute-done((bf16[2,128,1024]{2,1,0:T(8,128)(2,1)S(1)}, bf16[2,128,1024]{2,1,0:T(8,128)(2,1)S(1)}, u32[]{:S(2)}, u32[]{:S(2)}) %collective-permute-start.74) | collective-permute-done | bytes 524320 | tf_op jit(solution)/shard_map/ppermute | solution.py:456
  347.9 9.9 %collective-permute-done.62.refs_1_ = bf16[2,128,1024]{2,1,0:T(8,128)(2,1)S(1)} collective-permute-done((bf16[2,128,1024]{2,1,0:T(8,128)(2,1)S(1)}, bf16[2,128,1024]{2,1,0:T(8,128)(2,1)S(1)}, u32[]{:S(2)}, u32[]{:S(2)}) %collective-permute-start.62) | collective-permute-done | bytes 524320 | tf_op jit(solution)/shard_map/ppermute | solution.py:456
  364.3 4.8 %collective-permute-done.75.refs_1_ = bf16[2,128,1024]{2,1,0:T(8,128)(2,1)S(1)} collective-permute-done((bf16[2,128,1024]{2,1,0:T(8,128)(2,1)S(1)}, bf16[2,128,1024]{2,1,0:T(8,128)(2,1)S(1)}, u32[]{:S(2)}, u32[]{:S(2)}) %collective-permute-start.75) | collective-permute-done | bytes 524320 | tf_op jit(solution)/shard_map/ppermute | solution.py:456
  371.8 6.7 %collective-permute-done.65.refs_2_ = bf16[2,128,1024]{2,1,0:T(8,128)(2,1)S(1)} collective-permute-done((bf16[2,128,1024]{2,1,0:T(8,128)(2,1)S(1)}, bf16[2,128,1024]{2,1,0:T(8,128)(2,1)S(1)}, u32[]{:S(2)}, u32[]{:S(2)}) %collective-permute-start.65) | collective-permute-done | bytes 524320 | tf_op jit(solution)/shard_map/ppermute | solution.py:456
  387.9 8.2 %collective-permute-done.63.refs_3_ = bf16[1,128,1024]{2,1,0:T(8,128)(2,1)S(1)} collective-permute-done((bf16[1,128,1024]{2,1,0:T(8,128)(2,1)}, bf16[1,128,1024]{2,1,0:T(8,128)(2,1)S(1)}, u32[]{:S(2)}, u32[]{:S(2)}) %collective-permute-start.63) | collective-permute-done | bytes 262176 | tf_op jit(solution)/shard_map/ppermute | solution.py:456
  402.6 8.1 %collective-permute-done.76.refs_3_ = bf16[1,128,1024]{2,1,0:T(8,128)(2,1)S(1)} collective-permute-done((bf16[1,128,1024]{2,1,0:T(8,128)(2,1)}, bf16[1,128,1024]{2,1,0:T(8,128)(2,1)S(1)}, u32[]{:S(2)}, u32[]{:S(2)}) %collective-permute-start.76) | collective-permute-done | bytes 262176 | tf_op jit(solution)/shard_map/ppermute | solution.py:456
  (290 shorter events, 282.9 us)
Async XLA Ops:
  3.8 30.8 %collective-permute-start.4 = (bf16[1,384,512]{2,1,0:T(8,128)(2,1)}, bf16[1,384,512]{2,1,0:T(8,128)(2,1)S(1)}, u32[]{:S(2)}, u32[]{:S(2)}) collective-permute-start(bf16[1,384,512]{2,1,0:T(8,128)(2,1)} %bitcast.60), channel_id=1, source_target_pairs={{0,1},{1,0},{2,3},{3,2},{4,5},{5,4},{6,7},{7,6},{8,9},{9,8},{10,11... | collective-permute-start | bytes 1179656 | tf_op jit(solution)/shard_map/ppermute | solution.py:397
  55.7 25.6 %collective-permute-start.7 = (bf16[2,128,1024]{2,1,0:T(8,128)(2,1)S(1)}, bf16[2,128,1024]{2,1,0:T(8,128)(2,1)S(1)}, u32[]{:S(2)}, u32[]{:S(2)}) collective-permute-start(bf16[2,128,1024]{2,1,0:T(8,128)(2,1)S(1)} %get-tuple-element.94), channel_id=1, source_target_pairs={{0,4},{4,0},{8,12},{12,8},{16,20},{20,16},{24,28},{28,24},{1,5},{5... | collective-permute-start | bytes 1572872 | tf_op jit(solution)/shard_map/ppermute | solution.py:456
  58.9 22.6 %collective-permute-start.8 = (bf16[2,128,1024]{2,1,0:T(8,128)(2,1)S(1)}, bf16[2,128,1024]{2,1,0:T(8,128)(2,1)S(1)}, u32[]{:S(2)}, u32[]{:S(2)}) collective-permute-start(bf16[2,128,1024]{2,1,0:T(8,128)(2,1)S(1)} %shard_map.107), channel_id=1, source_target_pairs={{0,8},{4,12},{28,20},{24,16},{1,9},{5,13},{29,21},{25,17},{2,10},{... | collective-permute-start | bytes 1572872 | tf_op jit(solution)/shard_map/ppermute | solution.py:456
  62.6 29.3 %collective-permute-start.21 = (bf16[2,128,1024]{2,1,0:T(8,128)(2,1)S(1)}, bf16[2,128,1024]{2,1,0:T(8,128)(2,1)S(1)}, u32[]{:S(2)}, u32[]{:S(2)}) collective-permute-start(bf16[2,128,1024]{2,1,0:T(8,128)(2,1)S(1)} %get-tuple-element.110), channel_id=1, source_target_pairs={{0,4},{4,0},{8,12},{12,8},{16,20},{20,16},{24,28},{28,24},{1,5},{5... | collective-permute-start | bytes 1572872 | tf_op jit(solution)/shard_map/ppermute | solution.py:456
  71.2 20.8 %collective-permute-start.22 = (bf16[2,128,1024]{2,1,0:T(8,128)(2,1)S(1)}, bf16[2,128,1024]{2,1,0:T(8,128)(2,1)S(1)}, u32[]{:S(2)}, u32[]{:S(2)}) collective-permute-start(bf16[2,128,1024]{2,1,0:T(8,128)(2,1)S(1)} %shard_map.116), channel_id=1, source_target_pairs={{0,8},{4,12},{28,20},{24,16},{1,9},{5,13},{29,21},{25,17},{2,10},{... | collective-permute-start | bytes 1572872 | tf_op jit(solution)/shard_map/ppermute | solution.py:456
  99.2 22.8 %collective-permute-start.11 = (bf16[2,128,1024]{2,1,0:T(8,128)(2,1)S(1)}, bf16[2,128,1024]{2,1,0:T(8,128)(2,1)S(1)}, u32[]{:S(2)}, u32[]{:S(2)}) collective-permute-start(bf16[2,128,1024]{2,1,0:T(8,128)(2,1)S(1)} %get-tuple-element.97), channel_id=1, source_target_pairs={{0,8},{4,12},{8,16},{12,20},{16,24},{20,28},{1,9},{5,13},{9,17},{1... | collective-permute-start | bytes 1572872 | tf_op jit(solution)/shard_map/ppermute | solution.py:456
  108.4 32.5 %collective-permute-start.14 = (bf16[4,128,1024]{2,1,0:T(8,128)(2,1)S(1)}, bf16[4,128,1024]{2,1,0:T(8,128)(2,1)S(1)}, u32[]{:S(2)}, u32[]{:S(2)}) collective-permute-start(bf16[4,128,1024]{2,1,0:T(8,128)(2,1)S(1)} %get-tuple-element.102), channel_id=1, source_target_pairs={{0,4},{4,0},{8,12},{12,8},{16,20},{20,16},{24,28},{28,24},{1,5},{5... | collective-permute-start | bytes 3145736 | tf_op jit(solution)/shard_map/ppermute | solution.py:456
  122.0 33.2 %collective-permute-start.28 = (bf16[4,128,1024]{2,1,0:T(8,128)(2,1)S(1)}, bf16[4,128,1024]{2,1,0:T(8,128)(2,1)S(1)}, u32[]{:S(2)}, u32[]{:S(2)}) collective-permute-start(bf16[4,128,1024]{2,1,0:T(8,128)(2,1)S(1)} %get-tuple-element.118), channel_id=1, source_target_pairs={{0,4},{4,0},{8,12},{12,8},{16,20},{20,16},{24,28},{28,24},{1,5},{5... | collective-permute-start | bytes 3145736 | tf_op jit(solution)/shard_map/ppermute | solution.py:456
  140.9 19.3 %collective-permute-start.29 = (bf16[2,128,1024]{2,1,0:T(8,128)(2,1)S(1)}, bf16[2,128,1024]{2,1,0:T(8,128)(2,1)S(1)}, u32[]{:S(2)}, u32[]{:S(2)}) collective-permute-start(bf16[2,128,1024]{2,1,0:T(8,128)(2,1)S(1)} %get-tuple-element.116.fresh_ref.refs_0_.refs_4_), channel_id=1, source_target_pairs={{28,20},{24,16},{20,12},{16,8},{12,4},{8,0},{29,21},{25,17},{21,13... | collective-permute-start | bytes 1572872 | tf_op jit(solution)/shard_map/ppermute | solution.py:456
  150.3 21.2 %collective-permute-start.16 = (bf16[2,128,1024]{2,1,0:T(8,128)(2,1)S(1)}, bf16[2,128,1024]{2,1,0:T(8,128)(2,1)S(1)}, u32[]{:S(2)}, u32[]{:S(2)}) collective-permute-start(bf16[2,128,1024]{2,1,0:T(8,128)(2,1)S(1)} %get-tuple-element.103), channel_id=1, source_target_pairs={{0,8},{4,12},{8,16},{12,20},{16,24},{20,28},{1,9},{5,13},{9,17},{1... | collective-permute-start | bytes 1572872 | tf_op jit(solution)/shard_map/ppermute | solution.py:456
  161.5 20.5 %collective-permute-start.30 = (bf16[2,128,1024]{2,1,0:T(8,128)(2,1)S(1)}, bf16[2,128,1024]{2,1,0:T(8,128)(2,1)S(1)}, u32[]{:S(2)}, u32[]{:S(2)}) collective-permute-start(bf16[2,128,1024]{2,1,0:T(8,128)(2,1)S(1)} %get-tuple-element.119), channel_id=1, source_target_pairs={{0,8},{4,12},{8,16},{12,20},{16,24},{20,28},{1,9},{5,13},{9,17},{1... | collective-permute-start | bytes 1572872 | tf_op jit(solution)/shard_map/ppermute | solution.py:456
  168.9 30.0 %collective-permute-start.36 = (bf16[4,128,1024]{2,1,0:T(8,128)(2,1)S(1)}, bf16[4,128,1024]{2,1,0:T(8,128)(2,1)S(1)}, u32[]{:S(2)}, u32[]{:S(2)}) collective-permute-start(bf16[4,128,1024]{2,1,0:T(8,128)(2,1)S(1)} %get-tuple-element.127), channel_id=1, source_target_pairs={{0,4},{4,0},{8,12},{12,8},{16,20},{20,16},{24,28},{28,24},{1,5},{5... | collective-permute-start | bytes 3145736 | tf_op jit(solution)/shard_map/ppermute | solution.py:456
  181.2 29.0 %collective-permute-start.45 = (bf16[4,128,1024]{2,1,0:T(8,128)(2,1)S(1)}, bf16[4,128,1024]{2,1,0:T(8,128)(2,1)S(1)}, u32[]{:S(2)}, u32[]{:S(2)}) collective-permute-start(bf16[4,128,1024]{2,1,0:T(8,128)(2,1)S(1)} %get-tuple-element.138), channel_id=1, source_target_pairs={{0,4},{4,0},{8,12},{12,8},{16,20},{20,16},{24,28},{28,24},{1,5},{5... | collective-permute-start | bytes 3145736 | tf_op jit(solution)/shard_map/ppermute | solution.py:456
  189.8 19.5 %collective-permute-start.33 = (bf16[2,128,1024]{2,1,0:T(8,128)(2,1)S(1)}, bf16[2,128,1024]{2,1,0:T(8,128)(2,1)S(1)}, u32[]{:S(2)}, u32[]{:S(2)}) collective-permute-start(bf16[2,128,1024]{2,1,0:T(8,128)(2,1)S(1)} %get-tuple-element.122), channel_id=1, source_target_pairs={{28,20},{24,16},{20,12},{16,8},{12,4},{8,0},{29,21},{25,17},{21,13... | collective-permute-start | bytes 1572872 | tf_op jit(solution)/shard_map/ppermute | solution.py:456
  215.9 41.5 %collective-permute-start.34 = (bf16[4,128,1024]{2,1,0:T(8,128)(2,1)S(1)}, bf16[4,128,1024]{2,1,0:T(8,128)(2,1)S(1)}, u32[]{:S(2)}, u32[]{:S(2)}) collective-permute-start(bf16[4,128,1024]{2,1,0:T(8,128)(2,1)S(1)} %get-tuple-element.124), channel_id=1, source_target_pairs={{0,4},{4,0},{8,12},{12,8},{16,20},{20,16},{24,28},{28,24},{1,5},{5... | collective-permute-start | bytes 3145736 | tf_op jit(solution)/shard_map/ppermute | solution.py:456
  237.5 21.6 %collective-permute-start.35 = (bf16[4,128,1024]{2,1,0:T(8,128)(2,1)S(1)}, bf16[4,128,1024]{2,1,0:T(8,128)(2,1)S(1)}, u32[]{:S(2)}, u32[]{:S(2)}) collective-permute-start(bf16[4,128,1024]{2,1,0:T(8,128)(2,1)S(1)} %get-tuple-element.125), channel_id=1, source_target_pairs={{0,4},{4,0},{8,12},{12,8},{16,20},{20,16},{24,28},{28,24},{1,5},{5... | collective-permute-start | bytes 3145736 | tf_op jit(solution)/shard_map/ppermute | solution.py:456
  257.5 19.5 %collective-permute-start.51 = (bf16[2,128,1024]{2,1,0:T(8,128)(2,1)S(1)}, bf16[2,128,1024]{2,1,0:T(8,128)(2,1)S(1)}, u32[]{:S(2)}, u32[]{:S(2)}) collective-permute-start(bf16[2,128,1024]{2,1,0:T(8,128)(2,1)S(1)} %get-tuple-element.145), channel_id=1, source_target_pairs={{28,20},{24,16},{20,12},{16,8},{12,4},{8,0},{29,21},{25,17},{21,13... | collective-permute-start | bytes 1572872 | tf_op jit(solution)/shard_map/ppermute | solution.py:456
  294.4 35.5 %collective-permute-start.54 = (bf16[4,128,1024]{2,1,0:T(8,128)(2,1)S(1)}, bf16[4,128,1024]{2,1,0:T(8,128)(2,1)S(1)}, u32[]{:S(2)}, u32[]{:S(2)}) collective-permute-start(bf16[4,128,1024]{2,1,0:T(8,128)(2,1)S(1)} %get-tuple-element.149), channel_id=1, source_target_pairs={{0,4},{4,0},{8,12},{12,8},{16,20},{20,16},{24,28},{28,24},{1,5},{5... | collective-permute-start | bytes 3145736 | tf_op jit(solution)/shard_map/ppermute | solution.py:456
  304.9 31.7 %collective-permute-start.55 = (bf16[4,128,1024]{2,1,0:T(8,128)(2,1)S(1)}, bf16[4,128,1024]{2,1,0:T(8,128)(2,1)S(1)}, u32[]{:S(2)}, u32[]{:S(2)}) collective-permute-start(bf16[4,128,1024]{2,1,0:T(8,128)(2,1)S(1)} %get-tuple-element.150), channel_id=1, source_target_pairs={{0,4},{4,0},{8,12},{12,8},{16,20},{20,16},{24,28},{28,24},{1,5},{5... | collective-permute-start | bytes 3145736 | tf_op jit(solution)/shard_map/ppermute | solution.py:456
  326.3 32.9 %collective-permute-start.72 = (bf16[2,128,1024]{2,1,0:T(8,128)(2,1)S(1)}, bf16[2,128,1024]{2,1,0:T(8,128)(2,1)S(1)}, u32[]{:S(2)}, u32[]{:S(2)}) collective-permute-start(bf16[2,128,1024]{2,1,0:T(8,128)(2,1)S(1)} %get-tuple-element.166.fresh_ref.refs_0_.refs_1_), channel_id=1, source_target_pairs={{0,8},{4,12},{8,16},{12,20},{16,24},{20,28},{1,9},{5,13},{9,17},{1... | collective-permute-start | bytes 1572872 | tf_op jit(solution)/shard_map/ppermute | solution.py:456
  334.7 23.2 %collective-permute-start.62 = (bf16[2,128,1024]{2,1,0:T(8,128)(2,1)S(1)}, bf16[2,128,1024]{2,1,0:T(8,128)(2,1)S(1)}, u32[]{:S(2)}, u32[]{:S(2)}) collective-permute-start(bf16[2,128,1024]{2,1,0:T(8,128)(2,1)S(1)} %collective-permute-done.61.refs_3_), channel_id=1, source_target_pairs={{20,12},{16,8},{12,4},{8,0},{21,13},{17,9},{13,5},{9,1},{22,14},{1... | collective-permute-start | bytes 1572872 | tf_op jit(solution)/shard_map/ppermute | solution.py:456
  336.6 22.6 %collective-permute-start.58 = (bf16[1,128,1024]{2,1,0:T(8,128)(2,1)S(1)}, bf16[1,128,1024]{2,1,0:T(8,128)(2,1)S(1)}, u32[]{:S(2)}, u32[]{:S(2)}) collective-permute-start(bf16[1,128,1024]{2,1,0:T(8,128)(2,1)S(1)} %get-tuple-element.156), channel_id=1, source_target_pairs={{0,4},{4,0},{8,12},{12,8},{16,20},{20,16},{24,28},{28,24},{1,5},{5... | collective-permute-start | bytes 786440 | tf_op jit(solution)/shard_map/ppermute | solution.py:456
  346.6 22.5 %collective-permute-start.75 = (bf16[2,128,1024]{2,1,0:T(8,128)(2,1)S(1)}, bf16[2,128,1024]{2,1,0:T(8,128)(2,1)S(1)}, u32[]{:S(2)}, u32[]{:S(2)}) collective-permute-start(bf16[2,128,1024]{2,1,0:T(8,128)(2,1)S(1)} %collective-permute-done.74.refs_3_), channel_id=1, source_target_pairs={{20,12},{16,8},{12,4},{8,0},{21,13},{17,9},{13,5},{9,1},{22,14},{1... | collective-permute-start | bytes 1572872 | tf_op jit(solution)/shard_map/ppermute | solution.py:456
  386.6 24.1 %collective-permute-start.79 = (bf16[2,128,1024]{2,1,0:T(8,128)(2,1)}, bf16[2,128,1024]{2,1,0:T(8,128)(2,1)}, u32[]{:S(2)}, u32[]{:S(2)}) collective-permute-start(bf16[2,128,1024]{2,1,0:T(8,128)(2,1)} %get-tuple-element.172), channel_id=1, source_target_pairs={{0,4},{4,0},{8,12},{12,8},{16,20},{20,16},{24,28},{28,24},{1,5},{5... | collective-permute-start | bytes 1572872 | tf_op jit(solution)/shard_map/ppermute | solution.py:456
  (92 other events, 1108.2 us)

commit v5 on v4

--- a/solution.py
+++ b/solution.py
@@ -35,28 +35,28 @@
     return total
 
 
-def open_kernel(scale, chunks, order_ref, x_ref, gate_w_ref, up_w_ref, gate_ref, up_ref, hidden_ref):
+def open_kernel(scale, chunks, order_ref, x_ref, gate_w_ref, up_w_ref, gate_ref, up_ref):
     position = lambda j: order_ref[j]
     gate = spread(position, gate_w_ref[0, 0], x_ref, chunks) * scale
     upper = spread(position, up_w_ref[0, 0], x_ref, chunks) * scale
     gate_ref[...] = gate
     up_ref[...] = upper
-    hidden_ref[...] = (gate * jax.nn.sigmoid(gate) * upper).astype(jnp.bfloat16)
-
-
-def close_kernel(scale, chunks, order_ref, c_ref, weight_ref, gate_ref, up_ref, pre_gate_ref, pre_up_ref):
+
+
+def close_kernel(scale, chunks, order_ref, c_ref, weight_ref, gate_ref, up_ref, pre_gate_ref, pre_up_ref, hidden_ref):
     grad = spread(lambda j: order_ref[j], weight_ref[0, 0], c_ref, chunks) * scale
     gate, upper = gate_ref[...], up_ref[...]
     sig = jax.nn.sigmoid(gate)
     act = gate * sig
     pre_gate_ref[...] = (grad * upper * sig * (1.0 + gate * (1.0 - sig))).astype(jnp.bfloat16)
     pre_up_ref[...] = (grad * act).astype(jnp.bfloat16)
+    hidden_ref[...] = (act * upper).astype(jnp.bfloat16)
 
 
 def front(kernel, scale, order, right, weights, picked, extra, dtypes):
     chunks, rows, size = right.shape
     units, width = weights.shape[2:]
-    tile = min(256, units)
+    tile = min(512, units)
     thin = pl.BlockSpec((tile, rows), lambda i, order: (i, 0))
     return pl.pallas_call(
         functools.partial(kernel, scale, chunks),
@@ -472,11 +472,11 @@
         tile = min(chunk, half)
         return (lambda t: s * (half // tile) + t), half // tile, tile
 
-    gate, upper, hidden = front(
-        open_kernel, scale_d, order, inputs, path_weights, (0, 1), (), (jnp.float32, jnp.float32, jnp.bfloat16)
+    gate, upper = front(
+        open_kernel, scale_d, order, inputs, path_weights, (0, 1), (), (jnp.float32, jnp.float32)
     )
-    pre_gate, pre_up = front(
-        close_kernel, scale_f, order, upstream, path_weights, (2,), (gate, upper), (jnp.bfloat16, jnp.bfloat16)
+    pre_gate, pre_up, hidden = front(
+        close_kernel, scale_f, order, upstream, path_weights, (2,), (gate, upper), (jnp.bfloat16,) * 3
     )
     sources = ((pre_gate, inputs, scale_d), (pre_up, inputs, scale_d), (hidden, upstream, scale_f))
 

time: 430 us -> 429 us (level)
  no operation moved by 1% of the time
where the time goes in v5:
time: 429 us; the launch traced here: 427 us
  waiting for transfers between devices  158 us (37%)
  starting transfers between devices  151 us (35%)
  Pallas kernels  90.4 us (21%)
  local copies, waits for them, and re-layouts  20 us (5%)
  other arithmetic  5.26 us (1%)
    ppermute x72, starting transfers between devices, permute(): return lax.ppermute(value, 'path', pairs)  144 us
    ppermute x72, waiting for transfers between devices, permute(): return lax.ppermute(value, 'path', pairs)  135 us
    pallas_call x18, Pallas kernels, running(): pl.pallas_call(functools.partial(running_kernel, line, step, len(flow), o...  23.7 us
    pallas_call x6, Pallas kernels, finals(): pl.pallas_call(kernel, grid_spec=pltpu.PrefetchScalarGridSpec(num_scalar_...  20.3 us
    unnamed x68, local copies, waits for them, and re-layouts  18.9 us
    pallas_call x6, Pallas kernels, update(): pl.pallas_call(functools.partial(update_kernel, modules), grid_spec=pltpu...  16.8 us
    ppermute x6, waiting for transfers between devices, gather_mp(): lax.ppermute(part, 'mp', pairs_of(size, bit))  15.4 us
    pallas_call x10, Pallas kernels, deliver(): pl.pallas_call(functools.partial(deliver_kernel, line, rings), in_specs=[...  10.3 us
  transfers between devices with their start and end apart: 82, of which 36 were waited for; matrix products, arithmetic and copies ran while one was open for 1% of the time, Pallas kernels for 19%

profile of v5, /device:TPU:0, one launch (start us, length us, event | category | flops | bytes accessed | tf_op | source)
XLA Modules:
  0.0 426.8 jit_solution(4321671070867066392)
XLA Ops:
  6.0 7.9 %collective-permute-done = bf16[1,384,512]{2,1,0:T(8,128)(2,1)S(1)} collective-permute-done((bf16[1,384,512]{2,1,0:T(8,128)(2,1)}, bf16[1,384,512]{2,1,0:T(8,128)(2,1)S(1)}, u32[]{:S(2)}, u32[]{:S(2)}) %collective-permute-start) | collective-permute-done | bytes 393248 | tf_op jit(solution)/shard_map/ppermute | solution.py:397
  13.8 7.6 %collective-permute-done.3 = bf16[1,384,512]{2,1,0:T(8,128)(2,1)S(1)} collective-permute-done((bf16[1,384,512]{2,1,0:T(8,128)(2,1)}, bf16[1,384,512]{2,1,0:T(8,128)(2,1)S(1)}, u32[]{:S(2)}, u32[]{:S(2)}) %collective-permute-start.3) | collective-permute-done | bytes 393248 | tf_op jit(solution)/shard_map/ppermute | solution.py:397
  23.5 4.6 %copy-done = bf16[1,3,1024,2048]{3,2,1,0:T(8,128)(2,1)S(1)} copy-done((bf16[1,3,1024,2048]{3,2,1,0:T(8,128)(2,1)S(1)}, bf16[1,3,1024,2048]{3,2,1,0:T(8,128)(2,1)}, u32[]{:S(2)}) %copy-start) | copy-done | bytes 12582936
  28.1 5.2 %shard_map.104 = (f32[1024,384]{1,0:T(8,128)S(1)}, f32[1024,384]{1,0:T(8,128)S(1)}) custom-call(s32[4]{0:T(128)S(1)} %select_reduce_fusion.4.order_ref, bf16[4,384,512]{2,1,0:T(8,128)(2,1)S(1)} %pad_maximum_fusion.x_ref.right_ref, bf16[1,3,1024,2048]{3,2,1,0:T(8,128)(2,1)S(1)} %copy-done, bf16[1,3,1024,2048]{3,2,1,0:T(8,128)(2,1)S(1)} %copy-done), custom_call_target="tpu_custom_call" | custom-call | flops 1 | bytes 1 | tf_op jit(solution)/shard_map/pallas_call | solution.py:61
  43.6 4.6 %copy-done.2 = bf16[1,3,1024,2048]{3,2,1,0:T(8,128)(2,1)S(1)} copy-done((bf16[1,3,1024,2048]{3,2,1,0:T(8,128)(2,1)S(1)}, bf16[1,3,1024,2048]{3,2,1,0:T(8,128)(2,1)}, u32[]{:S(2)}) %copy-start.2) | copy-done | bytes 12582936
  63.1 5.6 %collective-permute-done.20.refs_2_.refs_3_ = bf16[2,128,1024]{2,1,0:T(8,128)(2,1)S(1)} collective-permute-done((bf16[2,128,1024]{2,1,0:T(8,128)(2,1)S(1)}, bf16[2,128,1024]{2,1,0:T(8,128)(2,1)S(1)}, u32[]{:S(2)}, u32[]{:S(2)}) %collective-permute-start.20) | collective-permute-done | bytes 524320 | tf_op jit(solution)/shard_map/ppermute | solution.py:456
  73.4 6.6 %collective-permute-done.7 = bf16[2,128,1024]{2,1,0:T(8,128)(2,1)S(1)} collective-permute-done((bf16[2,128,1024]{2,1,0:T(8,128)(2,1)S(1)}, bf16[2,128,1024]{2,1,0:T(8,128)(2,1)S(1)}, u32[]{:S(2)}, u32[]{:S(2)}) %collective-permute-start.7) | collective-permute-done | bytes 524320 | tf_op jit(solution)/shard_map/ppermute | solution.py:456
  85.7 4.8 %collective-permute-done.21 = bf16[2,128,1024]{2,1,0:T(8,128)(2,1)S(1)} collective-permute-done((bf16[2,128,1024]{2,1,0:T(8,128)(2,1)S(1)}, bf16[2,128,1024]{2,1,0:T(8,128)(2,1)S(1)}, u32[]{:S(2)}, u32[]{:S(2)}) %collective-permute-start.21) | collective-permute-done | bytes 524320 | tf_op jit(solution)/shard_map/ppermute | solution.py:456
  97.8 6.2 %collective-permute-start.11 = (bf16[2,128,1024]{2,1,0:T(8,128)(2,1)S(1)}, bf16[2,128,1024]{2,1,0:T(8,128)(2,1)S(1)}, u32[]{:S(2)}, u32[]{:S(2)}) collective-permute-start(bf16[2,128,1024]{2,1,0:T(8,128)(2,1)S(1)} %get-tuple-element.97), channel_id=1, source_target_pairs={{0,8},{4,12},{8,16},{12,20},{16,24},{20,28},{1,9},{5,13},{9,17},{1... | collective-permute-start | bytes 1572872 | tf_op jit(solution)/shard_map/ppermute | solution.py:456
  111.4 4.6 %collective-permute-start.25 = (bf16[2,128,1024]{2,1,0:T(8,128)(2,1)S(1)}, bf16[2,128,1024]{2,1,0:T(8,128)(2,1)S(1)}, u32[]{:S(2)}, u32[]{:S(2)}) collective-permute-start(bf16[2,128,1024]{2,1,0:T(8,128)(2,1)S(1)} %get-tuple-element.113), channel_id=1, source_target_pairs={{0,8},{4,12},{8,16},{12,20},{16,24},{20,28},{1,9},{5,13},{9,17},{1... | collective-permute-start | bytes 1572872 | tf_op jit(solution)/shard_map/ppermute | solution.py:456
  142.7 4.8 %collective-permute-done.15.refs_5_.refs_7_ = bf16[2,128,1024]{2,1,0:T(8,128)(2,1)S(1)} collective-permute-done((bf16[2,128,1024]{2,1,0:T(8,128)(2,1)S(1)}, bf16[2,128,1024]{2,1,0:T(8,128)(2,1)S(1)}, u32[]{:S(2)}, u32[]{:S(2)}) %collective-permute-start.15) | collective-permute-done | bytes 524320 | tf_op jit(solution)/shard_map/ppermute | solution.py:456
  154.0 4.8 %collective-permute-done.29.refs_5_.refs_7_ = bf16[2,128,1024]{2,1,0:T(8,128)(2,1)S(1)} collective-permute-done((bf16[2,128,1024]{2,1,0:T(8,128)(2,1)S(1)}, bf16[2,128,1024]{2,1,0:T(8,128)(2,1)S(1)}, u32[]{:S(2)}, u32[]{:S(2)}) %collective-permute-start.29) | collective-permute-done | bytes 524320 | tf_op jit(solution)/shard_map/ppermute | solution.py:456
  171.7 4.6 %collective-permute-start.18 = (bf16[2,128,1024]{2,1,0:T(8,128)(2,1)S(1)}, bf16[2,128,1024]{2,1,0:T(8,128)(2,1)S(1)}, u32[]{:S(2)}, u32[]{:S(2)}) collective-permute-start(bf16[2,128,1024]{2,1,0:T(8,128)(2,1)S(1)} %get-tuple-element.105), channel_id=1, source_target_pairs={{0,8},{4,12},{8,16},{12,20},{16,24},{20,28},{1,9},{5,13},{9,17},{1... | collective-permute-start | bytes 1572872 | tf_op jit(solution)/shard_map/ppermute | solution.py:456
  183.6 4.5 %collective-permute-start.32 = (bf16[2,128,1024]{2,1,0:T(8,128)(2,1)S(1)}, bf16[2,128,1024]{2,1,0:T(8,128)(2,1)S(1)}, u32[]{:S(2)}, u32[]{:S(2)}) collective-permute-start(bf16[2,128,1024]{2,1,0:T(8,128)(2,1)S(1)} %get-tuple-element.121), channel_id=1, source_target_pairs={{0,8},{4,12},{8,16},{12,20},{16,24},{20,28},{1,9},{5,13},{9,17},{1... | collective-permute-start | bytes 1572872 | tf_op jit(solution)/shard_map/ppermute | solution.py:456
  189.9 7.3 %collective-permute-done.19.refs_5_ = bf16[2,128,1024]{2,1,0:T(8,128)(2,1)S(1)} collective-permute-done((bf16[2,128,1024]{2,1,0:T(8,128)(2,1)S(1)}, bf16[2,128,1024]{2,1,0:T(8,128)(2,1)S(1)}, u32[]{:S(2)}, u32[]{:S(2)}) %collective-permute-start.19) | collective-permute-done | bytes 524320 | tf_op jit(solution)/shard_map/ppermute | solution.py:456
  202.7 5.7 %collective-permute-done.33.refs_5_ = bf16[2,128,1024]{2,1,0:T(8,128)(2,1)S(1)} collective-permute-done((bf16[2,128,1024]{2,1,0:T(8,128)(2,1)S(1)}, bf16[2,128,1024]{2,1,0:T(8,128)(2,1)S(1)}, u32[]{:S(2)}, u32[]{:S(2)}) %collective-permute-start.33) | collective-permute-done | bytes 524320 | tf_op jit(solution)/shard_map/ppermute | solution.py:456
  271.5 4.6 %collective-permute-done.51.refs_5_.refs_6_ = bf16[2,128,1024]{2,1,0:T(8,128)(2,1)S(1)} collective-permute-done((bf16[2,128,1024]{2,1,0:T(8,128)(2,1)S(1)}, bf16[2,128,1024]{2,1,0:T(8,128)(2,1)S(1)}, u32[]{:S(2)}, u32[]{:S(2)}) %collective-permute-start.51) | collective-permute-done | bytes 524320 | tf_op jit(solution)/shard_map/ppermute | solution.py:456
  282.7 4.6 %collective-permute-done.44.refs_5_ = bf16[2,128,1024]{2,1,0:T(8,128)(2,1)S(1)} collective-permute-done((bf16[2,128,1024]{2,1,0:T(8,128)(2,1)S(1)}, bf16[2,128,1024]{2,1,0:T(8,128)(2,1)S(1)}, u32[]{:S(2)}, u32[]{:S(2)}) %collective-permute-start.44) | collective-permute-done | bytes 524320 | tf_op jit(solution)/shard_map/ppermute | solution.py:456
  339.7 5.5 %collective-permute-done.74.refs_3_ = bf16[2,128,1024]{2,1,0:T(8,128)(2,1)S(1)} collective-permute-done((bf16[2,128,1024]{2,1,0:T(8,128)(2,1)S(1)}, bf16[2,128,1024]{2,1,0:T(8,128)(2,1)S(1)}, u32[]{:S(2)}, u32[]{:S(2)}) %collective-permute-start.74) | collective-permute-done | bytes 524320 | tf_op jit(solution)/shard_map/ppermute | solution.py:456
  346.5 9.9 %collective-permute-done.62.refs_1_ = bf16[2,128,1024]{2,1,0:T(8,128)(2,1)S(1)} collective-permute-done((bf16[2,128,1024]{2,1,0:T(8,128)(2,1)S(1)}, bf16[2,128,1024]{2,1,0:T(8,128)(2,1)S(1)}, u32[]{:S(2)}, u32[]{:S(2)}) %collective-permute-start.62) | collective-permute-done | bytes 524320 | tf_op jit(solution)/shard_map/ppermute | solution.py:456
  363.0 4.7 %collective-permute-done.75.refs_1_ = bf16[2,128,1024]{2,1,0:T(8,128)(2,1)S(1)} collective-permute-done((bf16[2,128,1024]{2,1,0:T(8,128)(2,1)S(1)}, bf16[2,128,1024]{2,1,0:T(8,128)(2,1)S(1)}, u32[]{:S(2)}, u32[]{:S(2)}) %collective-permute-start.75) | collective-permute-done | bytes 524320 | tf_op jit(solution)/shard_map/ppermute | solution.py:456
  370.3 6.9 %collective-permute-done.65.refs_2_ = bf16[2,128,1024]{2,1,0:T(8,128)(2,1)S(1)} collective-permute-done((bf16[2,128,1024]{2,1,0:T(8,128)(2,1)S(1)}, bf16[2,128,1024]{2,1,0:T(8,128)(2,1)S(1)}, u32[]{:S(2)}, u32[]{:S(2)}) %collective-permute-start.65) | collective-permute-done | bytes 524320 | tf_op jit(solution)/shard_map/ppermute | solution.py:456
  386.6 8.4 %collective-permute-done.63.refs_3_ = bf16[1,128,1024]{2,1,0:T(8,128)(2,1)S(1)} collective-permute-done((bf16[1,128,1024]{2,1,0:T(8,128)(2,1)}, bf16[1,128,1024]{2,1,0:T(8,128)(2,1)S(1)}, u32[]{:S(2)}, u32[]{:S(2)}) %collective-permute-start.63) | collective-permute-done | bytes 262176 | tf_op jit(solution)/shard_map/ppermute | solution.py:456
  401.4 8.2 %collective-permute-done.76.refs_3_ = bf16[1,128,1024]{2,1,0:T(8,128)(2,1)S(1)} collective-permute-done((bf16[1,128,1024]{2,1,0:T(8,128)(2,1)}, bf16[1,128,1024]{2,1,0:T(8,128)(2,1)S(1)}, u32[]{:S(2)}, u32[]{:S(2)}) %collective-permute-start.76) | collective-permute-done | bytes 262176 | tf_op jit(solution)/shard_map/ppermute | solution.py:456
  (290 shorter events, 282.5 us)
Async XLA Ops:
  3.8 29.5 %collective-permute-start.4 = (bf16[1,384,512]{2,1,0:T(8,128)(2,1)}, bf16[1,384,512]{2,1,0:T(8,128)(2,1)S(1)}, u32[]{:S(2)}, u32[]{:S(2)}) collective-permute-start(bf16[1,384,512]{2,1,0:T(8,128)(2,1)} %bitcast.60), channel_id=1, source_target_pairs={{0,1},{1,0},{2,3},{3,2},{4,5},{5,4},{6,7},{7,6},{8,9},{9,8},{10,11... | collective-permute-start | bytes 1179656 | tf_op jit(solution)/shard_map/ppermute | solution.py:397
  54.4 25.6 %collective-permute-start.7 = (bf16[2,128,1024]{2,1,0:T(8,128)(2,1)S(1)}, bf16[2,128,1024]{2,1,0:T(8,128)(2,1)S(1)}, u32[]{:S(2)}, u32[]{:S(2)}) collective-permute-start(bf16[2,128,1024]{2,1,0:T(8,128)(2,1)S(1)} %get-tuple-element.94), channel_id=1, source_target_pairs={{0,4},{4,0},{8,12},{12,8},{16,20},{20,16},{24,28},{28,24},{1,5},{5... | collective-permute-start | bytes 1572872 | tf_op jit(solution)/shard_map/ppermute | solution.py:456
  57.5 22.6 %collective-permute-start.8 = (bf16[2,128,1024]{2,1,0:T(8,128)(2,1)S(1)}, bf16[2,128,1024]{2,1,0:T(8,128)(2,1)S(1)}, u32[]{:S(2)}, u32[]{:S(2)}) collective-permute-start(bf16[2,128,1024]{2,1,0:T(8,128)(2,1)S(1)} %shard_map.107), channel_id=1, source_target_pairs={{0,8},{4,12},{28,20},{24,16},{1,9},{5,13},{29,21},{25,17},{2,10},{... | collective-permute-start | bytes 1572872 | tf_op jit(solution)/shard_map/ppermute | solution.py:456
  61.2 29.3 %collective-permute-start.21 = (bf16[2,128,1024]{2,1,0:T(8,128)(2,1)S(1)}, bf16[2,128,1024]{2,1,0:T(8,128)(2,1)S(1)}, u32[]{:S(2)}, u32[]{:S(2)}) collective-permute-start(bf16[2,128,1024]{2,1,0:T(8,128)(2,1)S(1)} %get-tuple-element.110), channel_id=1, source_target_pairs={{0,4},{4,0},{8,12},{12,8},{16,20},{20,16},{24,28},{28,24},{1,5},{5... | collective-permute-start | bytes 1572872 | tf_op jit(solution)/shard_map/ppermute | solution.py:456
  69.8 20.8 %collective-permute-start.22 = (bf16[2,128,1024]{2,1,0:T(8,128)(2,1)S(1)}, bf16[2,128,1024]{2,1,0:T(8,128)(2,1)S(1)}, u32[]{:S(2)}, u32[]{:S(2)}) collective-permute-start(bf16[2,128,1024]{2,1,0:T(8,128)(2,1)S(1)} %shard_map.116), channel_id=1, source_target_pairs={{0,8},{4,12},{28,20},{24,16},{1,9},{5,13},{29,21},{25,17},{2,10},{... | collective-permute-start | bytes 1572872 | tf_op jit(solution)/shard_map/ppermute | solution.py:456
  97.8 23.0 %collective-permute-start.11 = (bf16[2,128,1024]{2,1,0:T(8,128)(2,1)S(1)}, bf16[2,128,1024]{2,1,0:T(8,128)(2,1)S(1)}, u32[]{:S(2)}, u32[]{:S(2)}) collective-permute-start(bf16[2,128,1024]{2,1,0:T(8,128)(2,1)S(1)} %get-tuple-element.97), channel_id=1, source_target_pairs={{0,8},{4,12},{8,16},{12,20},{16,24},{20,28},{1,9},{5,13},{9,17},{1... | collective-permute-start | bytes 1572872 | tf_op jit(solution)/shard_map/ppermute | solution.py:456
  107.0 32.6 %collective-permute-start.14 = (bf16[4,128,1024]{2,1,0:T(8,128)(2,1)S(1)}, bf16[4,128,1024]{2,1,0:T(8,128)(2,1)S(1)}, u32[]{:S(2)}, u32[]{:S(2)}) collective-permute-start(bf16[4,128,1024]{2,1,0:T(8,128)(2,1)S(1)} %get-tuple-element.102), channel_id=1, source_target_pairs={{0,4},{4,0},{8,12},{12,8},{16,20},{20,16},{24,28},{28,24},{1,5},{5... | collective-permute-start | bytes 3145736 | tf_op jit(solution)/shard_map/ppermute | solution.py:456
  120.7 33.2 %collective-permute-start.28 = (bf16[4,128,1024]{2,1,0:T(8,128)(2,1)S(1)}, bf16[4,128,1024]{2,1,0:T(8,128)(2,1)S(1)}, u32[]{:S(2)}, u32[]{:S(2)}) collective-permute-start(bf16[4,128,1024]{2,1,0:T(8,128)(2,1)S(1)} %get-tuple-element.118), channel_id=1, source_target_pairs={{0,4},{4,0},{8,12},{12,8},{16,20},{20,16},{24,28},{28,24},{1,5},{5... | collective-permute-start | bytes 3145736 | tf_op jit(solution)/shard_map/ppermute | solution.py:456
  139.6 19.2 %collective-permute-start.29 = (bf16[2,128,1024]{2,1,0:T(8,128)(2,1)S(1)}, bf16[2,128,1024]{2,1,0:T(8,128)(2,1)S(1)}, u32[]{:S(2)}, u32[]{:S(2)}) collective-permute-start(bf16[2,128,1024]{2,1,0:T(8,128)(2,1)S(1)} %get-tuple-element.116.fresh_ref.refs_0_.refs_4_), channel_id=1, source_target_pairs={{28,20},{24,16},{20,12},{16,8},{12,4},{8,0},{29,21},{25,17},{21,13... | collective-permute-start | bytes 1572872 | tf_op jit(solution)/shard_map/ppermute | solution.py:456
  148.9 21.4 %collective-permute-start.16 = (bf16[2,128,1024]{2,1,0:T(8,128)(2,1)S(1)}, bf16[2,128,1024]{2,1,0:T(8,128)(2,1)S(1)}, u32[]{:S(2)}, u32[]{:S(2)}) collective-permute-start(bf16[2,128,1024]{2,1,0:T(8,128)(2,1)S(1)} %get-tuple-element.103), channel_id=1, source_target_pairs={{0,8},{4,12},{8,16},{12,20},{16,24},{20,28},{1,9},{5,13},{9,17},{1... | collective-permute-start | bytes 1572872 | tf_op jit(solution)/shard_map/ppermute | solution.py:456
  160.1 20.7 %collective-permute-start.30 = (bf16[2,128,1024]{2,1,0:T(8,128)(2,1)S(1)}, bf16[2,128,1024]{2,1,0:T(8,128)(2,1)S(1)}, u32[]{:S(2)}, u32[]{:S(2)}) collective-permute-start(bf16[2,128,1024]{2,1,0:T(8,128)(2,1)S(1)} %get-tuple-element.119), channel_id=1, source_target_pairs={{0,8},{4,12},{8,16},{12,20},{16,24},{20,28},{1,9},{5,13},{9,17},{1... | collective-permute-start | bytes 1572872 | tf_op jit(solution)/shard_map/ppermute | solution.py:456
  167.7 30.3 %collective-permute-start.36 = (bf16[4,128,1024]{2,1,0:T(8,128)(2,1)S(1)}, bf16[4,128,1024]{2,1,0:T(8,128)(2,1)S(1)}, u32[]{:S(2)}, u32[]{:S(2)}) collective-permute-start(bf16[4,128,1024]{2,1,0:T(8,128)(2,1)S(1)} %get-tuple-element.127), channel_id=1, source_target_pairs={{0,4},{4,0},{8,12},{12,8},{16,20},{20,16},{24,28},{28,24},{1,5},{5... | collective-permute-start | bytes 3145736 | tf_op jit(solution)/shard_map/ppermute | solution.py:456
  180.0 29.3 %collective-permute-start.45 = (bf16[4,128,1024]{2,1,0:T(8,128)(2,1)S(1)}, bf16[4,128,1024]{2,1,0:T(8,128)(2,1)S(1)}, u32[]{:S(2)}, u32[]{:S(2)}) collective-permute-start(bf16[4,128,1024]{2,1,0:T(8,128)(2,1)S(1)} %get-tuple-element.138), channel_id=1, source_target_pairs={{0,4},{4,0},{8,12},{12,8},{16,20},{20,16},{24,28},{28,24},{1,5},{5... | collective-permute-start | bytes 3145736 | tf_op jit(solution)/shard_map/ppermute | solution.py:456
  188.6 19.8 %collective-permute-start.33 = (bf16[2,128,1024]{2,1,0:T(8,128)(2,1)S(1)}, bf16[2,128,1024]{2,1,0:T(8,128)(2,1)S(1)}, u32[]{:S(2)}, u32[]{:S(2)}) collective-permute-start(bf16[2,128,1024]{2,1,0:T(8,128)(2,1)S(1)} %get-tuple-element.122), channel_id=1, source_target_pairs={{28,20},{24,16},{20,12},{16,8},{12,4},{8,0},{29,21},{25,17},{21,13... | collective-permute-start | bytes 1572872 | tf_op jit(solution)/shard_map/ppermute | solution.py:456
  214.4 42.4 %collective-permute-start.34 = (bf16[4,128,1024]{2,1,0:T(8,128)(2,1)S(1)}, bf16[4,128,1024]{2,1,0:T(8,128)(2,1)S(1)}, u32[]{:S(2)}, u32[]{:S(2)}) collective-permute-start(bf16[4,128,1024]{2,1,0:T(8,128)(2,1)S(1)} %get-tuple-element.124), channel_id=1, source_target_pairs={{0,4},{4,0},{8,12},{12,8},{16,20},{20,16},{24,28},{28,24},{1,5},{5... | collective-permute-start | bytes 3145736 | tf_op jit(solution)/shard_map/ppermute | solution.py:456
  236.8 21.6 %collective-permute-start.35 = (bf16[4,128,1024]{2,1,0:T(8,128)(2,1)S(1)}, bf16[4,128,1024]{2,1,0:T(8,128)(2,1)S(1)}, u32[]{:S(2)}, u32[]{:S(2)}) collective-permute-start(bf16[4,128,1024]{2,1,0:T(8,128)(2,1)S(1)} %get-tuple-element.125), channel_id=1, source_target_pairs={{0,4},{4,0},{8,12},{12,8},{16,20},{20,16},{24,28},{28,24},{1,5},{5... | collective-permute-start | bytes 3145736 | tf_op jit(solution)/shard_map/ppermute | solution.py:456
  256.7 19.3 %collective-permute-start.51 = (bf16[2,128,1024]{2,1,0:T(8,128)(2,1)S(1)}, bf16[2,128,1024]{2,1,0:T(8,128)(2,1)S(1)}, u32[]{:S(2)}, u32[]{:S(2)}) collective-permute-start(bf16[2,128,1024]{2,1,0:T(8,128)(2,1)S(1)} %get-tuple-element.145), channel_id=1, source_target_pairs={{28,20},{24,16},{20,12},{16,8},{12,4},{8,0},{29,21},{25,17},{21,13... | collective-permute-start | bytes 1572872 | tf_op jit(solution)/shard_map/ppermute | solution.py:456
  293.1 35.3 %collective-permute-start.54 = (bf16[4,128,1024]{2,1,0:T(8,128)(2,1)S(1)}, bf16[4,128,1024]{2,1,0:T(8,128)(2,1)S(1)}, u32[]{:S(2)}, u32[]{:S(2)}) collective-permute-start(bf16[4,128,1024]{2,1,0:T(8,128)(2,1)S(1)} %get-tuple-element.149), channel_id=1, source_target_pairs={{0,4},{4,0},{8,12},{12,8},{16,20},{20,16},{24,28},{28,24},{1,5},{5... | collective-permute-start | bytes 3145736 | tf_op jit(solution)/shard_map/ppermute | solution.py:456
  304.3 31.1 %collective-permute-start.55 = (bf16[4,128,1024]{2,1,0:T(8,128)(2,1)S(1)}, bf16[4,128,1024]{2,1,0:T(8,128)(2,1)S(1)}, u32[]{:S(2)}, u32[]{:S(2)}) collective-permute-start(bf16[4,128,1024]{2,1,0:T(8,128)(2,1)S(1)} %get-tuple-element.150), channel_id=1, source_target_pairs={{0,4},{4,0},{8,12},{12,8},{16,20},{20,16},{24,28},{28,24},{1,5},{5... | collective-permute-start | bytes 3145736 | tf_op jit(solution)/shard_map/ppermute | solution.py:456
  325.3 32.4 %collective-permute-start.72 = (bf16[2,128,1024]{2,1,0:T(8,128)(2,1)S(1)}, bf16[2,128,1024]{2,1,0:T(8,128)(2,1)S(1)}, u32[]{:S(2)}, u32[]{:S(2)}) collective-permute-start(bf16[2,128,1024]{2,1,0:T(8,128)(2,1)S(1)} %get-tuple-element.166.fresh_ref.refs_0_.refs_1_), channel_id=1, source_target_pairs={{0,8},{4,12},{8,16},{12,20},{16,24},{20,28},{1,9},{5,13},{9,17},{1... | collective-permute-start | bytes 1572872 | tf_op jit(solution)/shard_map/ppermute | solution.py:456
  333.4 23.1 %collective-permute-start.62 = (bf16[2,128,1024]{2,1,0:T(8,128)(2,1)S(1)}, bf16[2,128,1024]{2,1,0:T(8,128)(2,1)S(1)}, u32[]{:S(2)}, u32[]{:S(2)}) collective-permute-start(bf16[2,128,1024]{2,1,0:T(8,128)(2,1)S(1)} %collective-permute-done.61.refs_3_), channel_id=1, source_target_pairs={{20,12},{16,8},{12,4},{8,0},{21,13},{17,9},{13,5},{9,1},{22,14},{1... | collective-permute-start | bytes 1572872 | tf_op jit(solution)/shard_map/ppermute | solution.py:456
  335.3 22.5 %collective-permute-start.58 = (bf16[1,128,1024]{2,1,0:T(8,128)(2,1)S(1)}, bf16[1,128,1024]{2,1,0:T(8,128)(2,1)S(1)}, u32[]{:S(2)}, u32[]{:S(2)}) collective-permute-start(bf16[1,128,1024]{2,1,0:T(8,128)(2,1)S(1)} %get-tuple-element.156), channel_id=1, source_target_pairs={{0,4},{4,0},{8,12},{12,8},{16,20},{20,16},{24,28},{28,24},{1,5},{5... | collective-permute-start | bytes 786440 | tf_op jit(solution)/shard_map/ppermute | solution.py:456
  345.2 22.5 %collective-permute-start.75 = (bf16[2,128,1024]{2,1,0:T(8,128)(2,1)S(1)}, bf16[2,128,1024]{2,1,0:T(8,128)(2,1)S(1)}, u32[]{:S(2)}, u32[]{:S(2)}) collective-permute-start(bf16[2,128,1024]{2,1,0:T(8,128)(2,1)S(1)} %collective-permute-done.74.refs_3_), channel_id=1, source_target_pairs={{20,12},{16,8},{12,4},{8,0},{21,13},{17,9},{13,5},{9,1},{22,14},{1... | collective-permute-start | bytes 1572872 | tf_op jit(solution)/shard_map/ppermute | solution.py:456
  385.4 24.3 %collective-permute-start.79 = (bf16[2,128,1024]{2,1,0:T(8,128)(2,1)}, bf16[2,128,1024]{2,1,0:T(8,128)(2,1)}, u32[]{:S(2)}, u32[]{:S(2)}) collective-permute-start(bf16[2,128,1024]{2,1,0:T(8,128)(2,1)} %get-tuple-element.172), channel_id=1, source_target_pairs={{0,4},{4,0},{8,12},{12,8},{16,20},{20,16},{24,28},{28,24},{1,5},{5... | collective-permute-start | bytes 1572872 | tf_op jit(solution)/shard_map/ppermute | solution.py:456
  (92 other events, 1108.3 us)
